TPU v7x, 32 devices: a whole 2x2x4 slice. The times are simulated.
32 devices in a mesh: seq: 2 (over y), fsdp: 16 (over z, x, core).
Axes of the slice: x: 2, y: 2, z: 4, core: 2. Of those that a mesh axis runs over, the one named last changes fastest.
Arguments:
- token_ids: int32 [16, 2048], P('fsdp', 'seq'), may hold values from 0 to 151935
- seq_lengths: int32 [16, 4], P('fsdp'), may hold values from 1 to 1024, 2048 in all within a row
- pairing: int32 [48], replicated, may hold values from 0 to 47, each once
- step_count: float32 [1], replicated, may hold values from 1 to 20
- embedding: float32 [151936, 1024], P('fsdp', 'seq'), may hold values from -0.6 to 0.6
- embedding_one: float32 [151936, 1024], P('fsdp', 'seq'), may hold values from -5e-05 to 5e-05
- embedding_two: float32 [151936, 1024], P('fsdp', 'seq'), may hold values from 3e-10 to 1.2e-09
- qkv_weight: float32 [1024, 4096], P(('seq', 'fsdp')), may hold values from -0.1875 to 0.1875
- qkv_one: float32 [1024, 4096], P(('seq', 'fsdp')), may hold values from -0.00015 to 0.00015
- qkv_two: float32 [1024, 4096], P(('seq', 'fsdp')), may hold values from 2.8e-09 to 1.1e-08
- out_weight: float32 [2048, 1024], P(('seq', 'fsdp')), may hold values from -1 to 1
- out_one: float32 [2048, 1024], P(('seq', 'fsdp')), may hold values from -0.00015 to 0.00015
- out_two: float32 [2048, 1024], P(('seq', 'fsdp')), may hold values from 2.8e-09 to 1.1e-08
- gate_up_weight: float32 [1024, 6144], P(('seq', 'fsdp')), may hold values from -0.1875 to 0.1875
- gate_up_one: float32 [1024, 6144], P(('seq', 'fsdp')), may hold values from -0.00015 to 0.00015
- gate_up_two: float32 [1024, 6144], P(('seq', 'fsdp')), may hold values from 2.8e-09 to 1.1e-08
- down_weight: float32 [3072, 1024], P(('seq', 'fsdp')), may hold values from -0.109375 to 0.109375
- down_one: float32 [3072, 1024], P(('seq', 'fsdp')), may hold values from -0.00015 to 0.00015
- down_two: float32 [3072, 1024], P(('seq', 'fsdp')), may hold values from 2.8e-09 to 1.1e-08
- norm_gains: float32 [3328], replicated, may hold values from 0.5 to 1.5
- gains_one: float32 [3328], replicated, may hold values from -0.00033 to 0.00033
- gains_two: float32 [3328], replicated, may hold values from 1e-08 to 4e-08
- score_weight: float32 [1024], replicated, may hold values from -0.1875 to 0.1875
- score_one: float32 [1024], replicated, may hold values from -0.0066 to 0.0066
- score_two: float32 [1024], replicated, may hold values from 5.3e-06 to 2.1e-05
Outputs:
- ranking_loss: float32 [], replicated
- grad_norm: float32 [], replicated
- new_embedding: float32 [151936, 1024], P('fsdp', 'seq')
- new_embedding_one: float32 [151936, 1024], P('fsdp', 'seq')
- new_embedding_two: float32 [151936, 1024], P('fsdp', 'seq')
- new_qkv: float32 [1024, 4096], P(('seq', 'fsdp'))
- new_qkv_one: float32 [1024, 4096], P(('seq', 'fsdp'))
- new_qkv_two: float32 [1024, 4096], P(('seq', 'fsdp'))
- new_out: float32 [2048, 1024], P(('seq', 'fsdp'))
- new_out_one: float32 [2048, 1024], P(('seq', 'fsdp'))
- new_out_two: float32 [2048, 1024], P(('seq', 'fsdp'))
- new_gate_up: float32 [1024, 6144], P(('seq', 'fsdp'))
- new_gate_up_one: float32 [1024, 6144], P(('seq', 'fsdp'))
- new_gate_up_two: float32 [1024, 6144], P(('seq', 'fsdp'))
- new_down: float32 [3072, 1024], P(('seq', 'fsdp'))
- new_down_one: float32 [3072, 1024], P(('seq', 'fsdp'))
- new_down_two: float32 [3072, 1024], P(('seq', 'fsdp'))
- clipped_gains: float32 [3328], replicated
- new_gains_one: float32 [3328], replicated
- new_gains_two: float32 [3328], replicated
- new_score: float32 [1024], replicated
- new_score_one: float32 [1024], replicated
- new_score_two: float32 [1024], replicated
Inputs may be any that keep to these rules, and one draw needn't show every extreme that they name: `token_ids`: the ids of padding tokens are drawn like the others. `seq_lengths`: each row holds the lengths of its group's 4 - 1 sequences in token order, then the padding's length; a row sums to 2048 and its largest entry is 1024. A permutation of the 48 sequence numbers; pair p prefers sequence pairing[2p] to pairing[2p + 1].
All inputs are finite; a program needn't handle non-finite values.
Results may differ from a plain program's by a relative error of at most 0.012.
Values may be sent and summed in bfloat16 or wider, within the bound.
A program may use at most 352 MiB of HBM per device.

v0:
```python
import jax
import jax.numpy as jnp
from jax import lax
from jax.sharding import PartitionSpec as P

D = 1024
QUERY_HEADS = 16
KEY_VALUE_HEADS = 8
HEAD_SIZE = 128
FF = 3072


NORM_EPS = 1e-06
ROPE_THETA = 1000000.0
LEARN_RATE = 0.04
BETA_ONE = 0.9
BETA_TWO = 0.95
ADAM_EPS = 1e-08
WEIGHT_DECAY = 0.1
CLIP_NORM = 1.0
PRECISE = lax.Precision.HIGHEST
MASKED = -1e30


def rms_norm(values, gain_vec):
    return (
        values * lax.rsqrt(jnp.mean(values * values, axis=-1, keepdims=True) + NORM_EPS) * gain_vec
    )


def rotary(values, position):
    half_width = values.shape[-1] // 2
    frequency = ROPE_THETA ** (-2.0 * jnp.arange(half_width, dtype=jnp.float32) / values.shape[-1])
    angles = position.astype(jnp.float32)[:, None] * frequency[None, :]
    cosine = jnp.cos(angles)[:, None, :]
    sine_part = jnp.sin(angles)[:, None, :]
    lower = values[..., :half_width]
    upper = values[..., half_width:]
    return jnp.concatenate(
        [lower * cosine - upper * sine_part, upper * cosine + lower * sine_part], axis=-1
    )


def layout(seg_ends, length):
    token_pos = jnp.arange(length, dtype=jnp.int32)
    bounds = seg_ends[:-1]
    segment = jnp.sum((token_pos[:, None] >= bounds[None, :]).astype(jnp.int32), axis=1)
    starts_all = jnp.concatenate([jnp.zeros((1,), jnp.int32), bounds])
    slot_ids = jnp.arange(seg_ends.shape[0], dtype=jnp.int32)
    begin = jnp.sum(
        jnp.where(segment[:, None] == slot_ids[None, :], starts_all[None, :], 0), axis=1
    )
    return (segment, token_pos - begin)


def masked(scores, row_start, block_size, segment):
    key_pos = jnp.arange(segment.shape[0], dtype=jnp.int32)
    row_pos = row_start + jnp.arange(block_size, dtype=jnp.int32)
    row_seg = lax.dynamic_slice_in_dim(segment, row_start, block_size)
    allowed = (key_pos[None, :] <= row_pos[:, None]) & (segment[None, :] == row_seg[:, None])
    return jnp.where(allowed[None], scores, MASKED)


def shape_heads(raw_heads, gain_vec, position):
    return rotary(rms_norm(raw_heads, gain_vec), position)


def attention_forward(query_low, key_low, value_low, segment):
    seq_len, head_count, head_width = query_low.shape
    group_length = head_count // key_low.shape[1]
    block_size = min(512, seq_len)
    score_scale = head_width ** (-0.5)
    key_all = jnp.repeat(key_low, group_length, axis=1)
    value_all = jnp.repeat(value_low, group_length, axis=1)

    def one_block(row_start):
        row_block = lax.dynamic_slice_in_dim(query_low, row_start, block_size)
        scores = (
            jnp.einsum("qhd,khd->hqk", row_block, key_all, preferred_element_type=jnp.float32)
            * score_scale
        )
        scores = masked(scores, row_start, block_size, segment)
        row_max = jnp.max(scores, axis=-1, keepdims=True)
        exponent = jnp.exp(scores - row_max)
        row_total = jnp.sum(exponent, axis=-1, keepdims=True)
        probs = (exponent / row_total).astype(jnp.bfloat16)
        output = jnp.einsum("hqk,khd->qhd", probs, value_all, preferred_element_type=jnp.float32)
        return (output, (row_max + jnp.log(row_total))[..., 0])

    starts = jnp.arange(seq_len // block_size, dtype=jnp.int32) * block_size
    output, logsum = lax.map(one_block, starts)
    return (output.reshape(seq_len, head_count, head_width), logsum)


def attention_backward(query_low, key_low, value_low, logsum, grad_out, segment):
    seq_len, head_count, head_width = query_low.shape
    kv_count = key_low.shape[1]
    group_length = head_count // kv_count
    block_size = min(512, seq_len)
    score_scale = head_width ** (-0.5)
    key_all = jnp.repeat(key_low, group_length, axis=1)
    value_all = jnp.repeat(value_low, group_length, axis=1)

    def one_block(accum, packed):
        key_grad, value_grad = accum
        row_start, block_lse = packed
        row_block = lax.dynamic_slice_in_dim(query_low, row_start, block_size)
        grad_block = lax.dynamic_slice_in_dim(grad_out, row_start, block_size)
        scores = (
            jnp.einsum("qhd,khd->hqk", row_block, key_all, preferred_element_type=jnp.float32)
            * score_scale
        )
        scores = masked(scores, row_start, block_size, segment)
        probs = jnp.exp(scores - block_lse[..., None])
        value_grad = value_grad + jnp.einsum(
            "hqk,qhd->khd",
            probs.astype(jnp.bfloat16),
            grad_block,
            preferred_element_type=jnp.float32,
        )
        prob_grad = jnp.einsum(
            "qhd,khd->hqk", grad_block, value_all, preferred_element_type=jnp.float32
        )
        score_grad = (
            probs * (prob_grad - jnp.sum(probs * prob_grad, axis=-1, keepdims=True))
        ).astype(jnp.bfloat16)
        query_grad = (
            jnp.einsum("hqk,khd->qhd", score_grad, key_all, preferred_element_type=jnp.float32)
            * score_scale
        )
        key_grad = (
            key_grad
            + jnp.einsum("hqk,qhd->khd", score_grad, row_block, preferred_element_type=jnp.float32)
            * score_scale
        )
        return ((key_grad, value_grad), query_grad)

    starts = jnp.arange(seq_len // block_size, dtype=jnp.int32) * block_size
    empty = jnp.zeros((seq_len, head_count, head_width), jnp.float32)
    (key_grad, value_grad), query_grad = lax.scan(one_block, (empty, empty), (starts, logsum))
    key_grad = key_grad.reshape(seq_len, kv_count, group_length, head_width).sum(axis=2)
    value_grad = value_grad.reshape(seq_len, kv_count, group_length, head_width).sum(axis=2)
    return (query_grad.reshape(seq_len, head_count, head_width), key_grad, value_grad)


def fetch_attention(qkv_weight, out_weight):
    return (
        lax.all_gather(qkv_weight.astype(jnp.bfloat16), ("seq", "fsdp"), axis=0, tiled=True),
        lax.all_gather(out_weight.astype(jnp.bfloat16), ("seq", "fsdp"), axis=0, tiled=True),
    )


def fetch_mlp(gate_up_weight, down_weight):
    return (
        lax.all_gather(gate_up_weight.astype(jnp.bfloat16), ("seq", "fsdp"), axis=0, tiled=True),
        lax.all_gather(down_weight.astype(jnp.bfloat16), ("seq", "fsdp"), axis=0, tiled=True),
    )


def reduce_grads(pieces):
    return tuple(
        (
            lax.psum_scatter(pieces[0], ("seq", "fsdp"), scatter_dimension=0, tiled=True),
            lax.psum_scatter(pieces[1], ("seq", "fsdp"), scatter_dimension=0, tiled=True),
            lax.psum_scatter(pieces[2], ("seq", "fsdp"), scatter_dimension=0, tiled=True),
            lax.psum_scatter(pieces[3], ("seq", "fsdp"), scatter_dimension=0, tiled=True),
        )
    )


def embed_forward(token_ids, table):
    token_rows = token_ids.shape[1]
    all_ids = lax.all_gather(token_ids.reshape(token_rows), ("seq", "fsdp"), axis=0, tiled=True)
    all_ids = all_ids.reshape(lax.axis_size("seq"), lax.axis_size("fsdp"), token_rows)
    height = table.shape[0]
    local_row = all_ids - lax.axis_index("fsdp") * height
    owned_mask = (local_row >= 0) & (local_row < height)
    picked = jnp.take(table.astype(jnp.bfloat16), jnp.clip(local_row, 0, height - 1), axis=0)
    picked = jnp.where(owned_mask[..., None], picked.astype(jnp.float32), 0.0)
    summed = lax.psum_scatter(picked.astype(jnp.bfloat16), "fsdp", scatter_dimension=1, tiled=True)
    arrived = lax.all_to_all(summed, "seq", split_axis=0, concat_axis=3, tiled=True)
    return (arrived.reshape(token_rows, -1), local_row, owned_mask)


def embed_backward(token_grad, local_row, owned_mask, height):
    token_rows, columns = token_grad.shape
    parted = lax.all_to_all(
        token_grad.astype(jnp.bfloat16).reshape(1, 1, token_rows, columns),
        "seq",
        split_axis=3,
        concat_axis=0,
        tiled=True,
    )
    gathered = lax.all_gather(parted, "fsdp", axis=1, tiled=True)
    target = jnp.where(owned_mask, local_row, height).reshape(-1)
    rows_in = gathered.reshape(target.shape[0], -1).astype(jnp.float32)
    return jax.ops.segment_sum(rows_in, target, num_segments=height + 1)[:height]


def adam_update(weight, moment_one, moment_two, grad, factor, step_float):
    grad = grad * factor
    moment_one = BETA_ONE * moment_one + (1.0 - BETA_ONE) * grad
    moment_two = BETA_TWO * moment_two + (1.0 - BETA_TWO) * grad * grad
    fix_one = 1.0 - BETA_ONE**step_float
    fix_two = 1.0 - BETA_TWO**step_float
    weight = weight - LEARN_RATE * (
        moment_one / fix_one / (jnp.sqrt(moment_two / fix_two) + ADAM_EPS) + WEIGHT_DECAY * weight
    )
    return (weight, moment_one, moment_two)


def body(
    token_ids,
    seq_lengths,
    pairing,
    step_count,
    embedding,
    embedding_one,
    embedding_two,
    qkv_weight,
    qkv_one,
    qkv_two,
    out_weight,
    out_one,
    out_two,
    gate_up_weight,
    gate_up_one,
    gate_up_two,
    down_weight,
    down_one,
    down_two,
    norm_gains,
    gains_one,
    gains_two,
    score_weight,
    score_one,
    score_two,
):
    seq_count = lax.axis_size("seq")
    seq_at = lax.axis_index("seq")
    group_at = lax.axis_index("fsdp")
    token_rows = token_ids.shape[1]
    seq_len = token_rows * seq_count
    per_group = seq_lengths.shape[1] - 1
    seg_ends = jnp.cumsum(seq_lengths[0])
    segment, position = layout(seg_ends, seq_len)
    attn_gain = norm_gains[:D]
    mlp_gain = norm_gains[D : 2 * D]
    final_gain = norm_gains[2 * D : 3 * D]
    query_gain = norm_gains[3 * D : 3 * D + HEAD_SIZE]
    key_gain = norm_gains[3 * D + HEAD_SIZE :]
    embedded, local_row, owned_mask = embed_forward(token_ids, embedding)
    resid_in = embedded.astype(jnp.float32)
    qkv_full, out_full = fetch_attention(qkv_weight, out_weight)
    normed_low = rms_norm(resid_in, attn_gain).astype(jnp.bfloat16)
    projected_rows = jnp.dot(normed_low, qkv_full, preferred_element_type=jnp.float32).astype(
        jnp.bfloat16
    )
    queries = projected_rows[:, : QUERY_HEADS * HEAD_SIZE].reshape(
        token_rows, QUERY_HEADS, HEAD_SIZE
    )
    key_head_rows = projected_rows[
        :, QUERY_HEADS * HEAD_SIZE : (QUERY_HEADS + KEY_VALUE_HEADS) * HEAD_SIZE
    ].reshape(token_rows, KEY_VALUE_HEADS, HEAD_SIZE)
    value_head_rows = projected_rows[:, (QUERY_HEADS + KEY_VALUE_HEADS) * HEAD_SIZE :].reshape(
        token_rows, KEY_VALUE_HEADS, HEAD_SIZE
    )
    query_raw, key_raw, value_low = (
        lax.all_to_all(queries, "seq", split_axis=1, concat_axis=0, tiled=True),
        lax.all_to_all(key_head_rows, "seq", split_axis=1, concat_axis=0, tiled=True),
        lax.all_to_all(value_head_rows, "seq", split_axis=1, concat_axis=0, tiled=True),
    )
    query_low = shape_heads(query_raw.astype(jnp.float32), query_gain, position).astype(
        jnp.bfloat16
    )
    key_low = shape_heads(key_raw.astype(jnp.float32), key_gain, position).astype(jnp.bfloat16)
    attended, logsum = attention_forward(query_low, key_low, value_low, segment)
    merged = lax.all_to_all(
        attended.astype(jnp.bfloat16), "seq", split_axis=0, concat_axis=1, tiled=True
    ).reshape(token_rows, QUERY_HEADS * HEAD_SIZE)
    resid_mid = resid_in + jnp.dot(merged, out_full, preferred_element_type=jnp.float32)
    gate_up_full, down_full = fetch_mlp(gate_up_weight, down_weight)
    normed_two = rms_norm(resid_mid, mlp_gain).astype(jnp.bfloat16)
    gate_up = jnp.dot(normed_two, gate_up_full, preferred_element_type=jnp.float32)
    activated = (jax.nn.silu(gate_up[:, :FF]) * gate_up[:, FF:]).astype(jnp.bfloat16)
    resid_out = resid_mid + jnp.dot(activated, down_full, preferred_element_type=jnp.float32)
    final = rms_norm(resid_out, final_gain)
    per_token = jnp.dot(final, score_weight, precision=PRECISE)
    local_seg = lax.dynamic_slice_in_dim(segment, seq_at * token_rows, token_rows)
    slot_list = jnp.arange(per_group, dtype=jnp.int32)
    seq_size = seq_lengths[0, :per_group].astype(jnp.float32)
    picker = (local_seg[None, :] == slot_list[:, None]).astype(jnp.float32) / seq_size[:, None]
    own_scores = jnp.dot(picker, per_token, precision=PRECISE)
    seq_total = pairing.shape[0]
    score_board = lax.dynamic_update_slice(
        jnp.zeros((seq_total,), jnp.float32), own_scores, (group_at * per_group,)
    )
    all_scores = lax.psum(score_board, ("seq", "fsdp"))
    pair_table = pairing.reshape(-1, 2)
    seq_ids = jnp.arange(seq_total, dtype=jnp.int32)
    choose = (pair_table[:, 0:1] == seq_ids[None, :]).astype(jnp.float32)
    reject = (pair_table[:, 1:2] == seq_ids[None, :]).astype(jnp.float32)
    margin = jnp.dot(choose, all_scores, precision=PRECISE) - jnp.dot(
        reject, all_scores, precision=PRECISE
    )
    ranking_loss = jnp.sum(jax.nn.softplus(-margin))
    margin_grad = -jax.nn.sigmoid(-margin)
    score_grads = jnp.dot(margin_grad, choose, precision=PRECISE) - jnp.dot(
        margin_grad, reject, precision=PRECISE
    )
    own_grads = lax.dynamic_slice_in_dim(score_grads, group_at * per_group, per_group)
    token_grad = jnp.dot(own_grads, picker, precision=PRECISE)
    score_part = jnp.dot(token_grad, final, precision=PRECISE)
    final_grad = token_grad[:, None] * score_weight[None, :]
    final_back = jax.vjp(rms_norm, resid_out, final_gain)[1]
    dresid_out, dfinal_gain = final_back(final_grad)
    gate_up_full, down_full = fetch_mlp(gate_up_weight, down_weight)
    mlp_low = dresid_out.astype(jnp.bfloat16)
    down_grad = jnp.dot(activated.T, mlp_low, preferred_element_type=jnp.float32)
    act_grad = jnp.dot(mlp_low, down_full.T, preferred_element_type=jnp.float32)
    act_back = jax.vjp(lambda joined: jax.nn.silu(joined[:, :FF]) * joined[:, FF:], gate_up)[1]
    gate_up_low = act_back(act_grad)[0].astype(jnp.bfloat16)
    gate_up_grad = jnp.dot(normed_two.T, gate_up_low, preferred_element_type=jnp.float32)
    normed_two_grad = jnp.dot(gate_up_low, gate_up_full.T, preferred_element_type=jnp.float32)
    mid_back = jax.vjp(rms_norm, resid_mid, mlp_gain)[1]
    mid_extra, dmlp_gain = mid_back(normed_two_grad)
    dresid_mid = dresid_out + mid_extra
    qkv_full, out_full = fetch_attention(qkv_weight, out_weight)
    attn_low = dresid_mid.astype(jnp.bfloat16)
    out_grad = jnp.dot(merged.T, attn_low, preferred_element_type=jnp.float32)
    merged_grad = jnp.dot(attn_low, out_full.T, preferred_element_type=jnp.float32).astype(
        jnp.bfloat16
    )
    head_grad = lax.all_to_all(
        merged_grad.reshape(token_rows, QUERY_HEADS, HEAD_SIZE),
        "seq",
        split_axis=1,
        concat_axis=0,
        tiled=True,
    )
    query_grad, key_grad, value_grad = attention_backward(
        query_low, key_low, value_low, logsum, head_grad, segment
    )
    query_back = jax.vjp(
        lambda raw_heads, gain_vec: shape_heads(raw_heads, gain_vec, position),
        query_raw.astype(jnp.float32),
        query_gain,
    )[1]
    key_back = jax.vjp(
        lambda raw_heads, gain_vec: shape_heads(raw_heads, gain_vec, position),
        key_raw.astype(jnp.float32),
        key_gain,
    )[1]
    query_raw_grad, dquery_gain = query_back(query_grad)
    key_raw_grad, dkey_gain = key_back(key_grad)
    back_query, back_key, back_value = (
        lax.all_to_all(
            query_raw_grad.astype(jnp.bfloat16), "seq", split_axis=0, concat_axis=1, tiled=True
        ),
        lax.all_to_all(
            key_raw_grad.astype(jnp.bfloat16), "seq", split_axis=0, concat_axis=1, tiled=True
        ),
        lax.all_to_all(
            value_grad.astype(jnp.bfloat16), "seq", split_axis=0, concat_axis=1, tiled=True
        ),
    )
    projected_grad = jnp.concatenate(
        [
            back_query.reshape(token_rows, -1),
            back_key.reshape(token_rows, -1),
            back_value.reshape(token_rows, -1),
        ],
        axis=1,
    )
    qkv_grad = jnp.dot(normed_low.T, projected_grad, preferred_element_type=jnp.float32)
    normed_grad = jnp.dot(projected_grad, qkv_full.T, preferred_element_type=jnp.float32)
    in_back = jax.vjp(rms_norm, resid_in, attn_gain)[1]
    in_extra, dattn_gain = in_back(normed_grad)
    dresid_in = dresid_mid + in_extra
    shards = reduce_grads((qkv_grad, out_grad, gate_up_grad, down_grad))
    embed_grad = embed_backward(dresid_in, local_row, owned_mask, embedding.shape[0])
    square = jnp.sum(embed_grad * embed_grad)
    for shard in shards:
        square = square + jnp.sum(shard * shard)
    gain_part = jnp.concatenate([dattn_gain, dmlp_gain, dfinal_gain, dquery_gain, dkey_gain])
    gain_sum, score_sum, square_sum = lax.psum((gain_part, score_part, square), ("seq", "fsdp"))
    grad_norm = jnp.sqrt(square_sum + jnp.sum(gain_sum * gain_sum) + jnp.sum(score_sum * score_sum))
    factor = CLIP_NORM / jnp.maximum(grad_norm, CLIP_NORM)
    step_float = step_count[0]
    e_new = adam_update(embedding, embedding_one, embedding_two, embed_grad, factor, step_float)
    q_new = adam_update(qkv_weight, qkv_one, qkv_two, shards[0], factor, step_float)
    o_new = adam_update(out_weight, out_one, out_two, shards[1], factor, step_float)
    g_new = adam_update(gate_up_weight, gate_up_one, gate_up_two, shards[2], factor, step_float)
    d_new = adam_update(down_weight, down_one, down_two, shards[3], factor, step_float)
    n_new = adam_update(norm_gains, gains_one, gains_two, gain_sum, factor, step_float)
    s_new = adam_update(score_weight, score_one, score_two, score_sum, factor, step_float)
    clipped_gains = gain_sum * factor
    return (
        ranking_loss,
        grad_norm,
        e_new[0],
        e_new[1],
        e_new[2],
        q_new[0],
        q_new[1],
        q_new[2],
        o_new[0],
        o_new[1],
        o_new[2],
        g_new[0],
        g_new[1],
        g_new[2],
        d_new[0],
        d_new[1],
        d_new[2],
        clipped_gains,
        n_new[1],
        n_new[2],
        s_new[0],
        s_new[1],
        s_new[2],
    )


def solution(mesh):
    return jax.shard_map(
        body,
        mesh=mesh,
        in_specs=(
            P("fsdp", "seq"),
            P("fsdp", None),
            P(),
            P(),
            P("fsdp", "seq"),
            P("fsdp", "seq"),
            P("fsdp", "seq"),
            P(("seq", "fsdp"), None),
            P(("seq", "fsdp"), None),
            P(("seq", "fsdp"), None),
            P(("seq", "fsdp"), None),
            P(("seq", "fsdp"), None),
            P(("seq", "fsdp"), None),
            P(("seq", "fsdp"), None),
            P(("seq", "fsdp"), None),
            P(("seq", "fsdp"), None),
            P(("seq", "fsdp"), None),
            P(("seq", "fsdp"), None),
            P(("seq", "fsdp"), None),
            P(),
            P(),
            P(),
            P(),
            P(),
            P(),
        ),
        out_specs=(
            P(),
            P(),
            P("fsdp", "seq"),
            P("fsdp", "seq"),
            P("fsdp", "seq"),
            P(("seq", "fsdp"), None),
            P(("seq", "fsdp"), None),
            P(("seq", "fsdp"), None),
            P(("seq", "fsdp"), None),
            P(("seq", "fsdp"), None),
            P(("seq", "fsdp"), None),
            P(("seq", "fsdp"), None),
            P(("seq", "fsdp"), None),
            P(("seq", "fsdp"), None),
            P(("seq", "fsdp"), None),
            P(("seq", "fsdp"), None),
            P(("seq", "fsdp"), None),
            P(),
            P(),
            P(),
            P(),
            P(),
            P(),
        ),
        check_vma=False,
    )
```

profile of v0, /device:TPU:0, one launch (start us, length us, event | category | flops | bytes accessed | tf_op | source)
XLA Modules:
  0.0 3057.6 jit_solution(15443162414317213026)
XLA Ops:
  8.1 43.8 %all-gather = s32[1,32768]{1,0:T(1,128)S(1)} all-gather(s32[1,1024]{1,0:T(1,128)} %param.29), channel_id=2, replica_groups=mesh['seq'=2,'fsdp'=16] {'seq','fsdp'}, dimensions={1}, use_global_device_ids=true | all-gather | bytes 135168 | tf_op jit(solution)/shard_map/all_gather | solution.py:173
  64.5 137.5 %gather_fusion = bf16[32768,512]{1,0:T(8,128)(2,1)} fusion(bf16[9496,512]{1,0:T(8,128)(2,1)} %convert_element_type.169, s32[32768]{0:T(1024)S(1)} %broadcast_clamp_fusion), kind=kCustom, calls=%fused_computation | custom fusion | bytes 67239936 | tf_op jit(solution)/shard_map/jit(_take)/gather | solution.py:178
  202.1 42.1 %copy.288 = bf16[2,16,1024,512]{2,3,1,0:T(8,128)(2,1)} copy(bf16[2,16,1024,512]{3,2,1,0:T(8,128)(2,1)} %bitcast.274) | data formatting | bytes 67108864 | tf_op jit(solution)/shard_map/jit(_take)/gather | solution.py:178
  244.2 23.2 select_convert_fusion
  271.4 644.4 %all-reduce.10.cloned.1.call-done = bf16[2,16,1024,512]{2,3,1,0:T(8,128)(2,1)} async-done(((bf16[2,16,1024,512]{2,3,1,0:T(8,128)(2,1)}), bf16[2,16,1024,512]{2,3,1,0:T(8,128)(2,1)}) %all-reduce.10.cloned.1.call-update) | async-done | bytes 33554448
  923.9 24.8 all-to-all-done
  952.4 12.9 convolution_convert_fusion
  979.8 21.0 all-to-all-done.3
  1020.5 16.8 all-to-all-done.2
  1064.5 24.3 all-to-all-done.1
  1118.5 232.8 %while.30 = (s32[]{:T(128)}, bf16[4,512,8,128]{3,2,1,0:T(8,128)(2,1)}, f32[4,8,512]{2,1,0:T(8,128)}, s32[4]{0:T(128)S(1)}, s32[2048]{0:T(1024)S(1)}, /*index=5*/...) while((s32[]{:T(128)}, ...), condition=%wide.region_10.11_spmd.clone.clone, body=%wide.region_7.10_spmd.clone.sunk.clone | while | flops 4398772736 | bytes 155338960 | solution.py:91
  1127.8 15.5 fusion.177
  1143.2 15.4 fusion.178
  1158.7 15.8 fusion.179
  1185.9 15.5 fusion.177
  1201.4 15.4 fusion.178
  1216.8 15.8 fusion.179
  1244.1 15.5 fusion.177
  1259.6 15.4 fusion.178
  1275.0 15.8 fusion.179
  1302.2 15.5 fusion.177
  1317.7 15.4 fusion.178
  1333.1 15.8 fusion.179
  1357.8 44.6 %all-to-all-done.4 = bf16[2048,8,128]{2,1,0:T(8,128)(2,1)} async-done(((bf16[2048,8,128]{2,1,0:T(8,128)(2,1)}), bf16[2048,8,128]{2,1,0:T(8,128)(2,1)}, u32[]{:S(2)}, u32[]{:S(2)}) %all-to-all-start.4) | async-done | bytes 4194336 | tf_op jit(solution)/shard_map/all_to_all | solution.py:278
  1419.5 22.5 fusion.104
  1441.9 13.2 multiply_convert_fusion.1
  1471.6 38.9 %psum.28 = f32[48]{0:T(128)S(1)} all-reduce(f32[48]{0:T(128)S(1)} %dynamic_update_slice.14), channel_id=1, replica_groups=mesh['seq'=2,'fsdp'=16] {'seq','fsdp'}, use_global_device_ids=true, to_apply=%region_13.14 | all-reduce | flops 48 | bytes 384 | tf_op jit(solution)/shard_map/psum | solution.py:298
  1516.2 24.4 fusion.69
  1540.7 22.6 multiply_reduce_fusion.6
  1577.0 14.2 fusion.105
  1608.2 25.7 fusion.67
  1633.9 40.7 %all-to-all-done.5 = bf16[1024,16,128]{2,0,1:T(8,128)(2,1)} async-done(((bf16[1024,16,128]{2,0,1:T(8,128)(2,1)}), bf16[1024,16,128]{2,0,1:T(8,128)(2,1)}, u32[]{:S(2)}, u32[]{:S(2)}) %all-to-all-start.5) | async-done | bytes 4194336 | tf_op jit(solution)/shard_map/all_to_all | solution.py:334
  1679.4 507.2 %while.31 = (s32[]{:T(128)}, f32[2048,8,128]{0,2,1:T(8,128)}, f32[2048,8,128]{0,2,1:T(8,128)}, f32[4,512,8,128]{3,2,1,0:T(8,128)}, s32[4]{0:T(128)S(1)}, /*index...) while((s32[]{:T(128)}, f32[2048,8,128]{0,2,1:T(8,128)}, ...), condition=%wide.region_19.20_spmd.clone.clone, body=%wide.region_17.19_spmd.clone.sunk.clone | while | flops 10827067392 | bytes 331450592 | solution.py:140
  1688.9 14.6 fusion.189
  1703.5 26.5 multiply_reduce_fusion.20
  1730.1 30.2 multiply_convert_fusion.7
  1760.3 18.0 bitcast_add_fusion.8
  1787.7 12.9 bitcast_add_fusion.7
  1812.4 14.9 fusion.189
  1827.4 26.8 multiply_reduce_fusion.20
  1854.2 28.0 multiply_convert_fusion.7
  1882.2 19.4 bitcast_add_fusion.8
  1913.2 18.4 bitcast_add_fusion.7
  1943.5 15.3 fusion.189
  1958.7 26.6 multiply_reduce_fusion.20
  1985.3 28.3 multiply_convert_fusion.7
  2013.7 19.2 bitcast_add_fusion.8
  2043.1 16.2 bitcast_add_fusion.7
  2071.1 14.8 fusion.189
  2085.9 26.7 multiply_reduce_fusion.20
  2112.6 27.8 multiply_convert_fusion.7
  2140.4 18.5 bitcast_add_fusion.8
  2168.3 15.3 bitcast_add_fusion.7
  2214.3 12.9 multiply_add_fusion.2
  2286.2 32.8 %all-to-all-done.6 = bf16[2048,8,128]{2,1,0:T(8,128)(2,1)} async-done(((bf16[2048,8,128]{2,1,0:T(8,128)(2,1)}), bf16[2048,8,128]{2,1,0:T(8,128)(2,1)}, u32[]{:S(2)}, u32[]{:S(2)}) %all-to-all-start.6) | async-done | bytes 4194336 | tf_op jit(solution)/shard_map/all_to_all | solution.py:357
  2325.7 15.1 fusion.60
  2342.4 14.8 fusion.51
  2364.2 12.8 reduce.13
  2379.5 49.8 %all_to_all.141 = bf16[2,2,262144]{2,1,0:T(2,128)(2,1)S(1)} all-to-all(bf16[2,2,262144]{2,1,0:T(2,128)(2,1)} %reshape.608), channel_id=1, replica_groups=mesh['seq'=2,'fsdp'=16] {'seq'}, dimensions={0} | all-to-all | bytes 4194304 | tf_op jit(solution)/shard_map/all_to_all | solution.py:187
  2450.0 231.4 %reduce-scatter.8.cloned.1.call-done = f32[32,4096]{1,0:T(8,128)} async-done(((f32[1024,4096]{1,0:T(8,128)}), f32[32,4096]{1,0:T(8,128)}) %reduce-scatter.8.cloned.1.call-update) | async-done | bytes 524304 | tf_op jit(solution)/shard_map/reduce_scatter | solution.py:163
  2683.2 22.9 copy.324
  2706.1 227.4 %scatter_custom_fusion = f32[9497,512]{1,0:T(8,128)} fusion(s32[32768]{0:T(1024)} %get-tuple-element.434, bf16[32768,512]{1,0:T(8,128)(2,1)} %bitcast.275, f32[]{:T(128)} %constant.60.clone.1), kind=kCustom, calls=%fused_computation.45 | custom fusion | flops 33554432 | bytes 53004800 | tf_op jit(solution)/shard_map/scatter-add | solution.py:197
  2946.8 41.8 %all-reduce.7 = (f32[]{:T(128)}, f32[3328]{0:T(1024)S(1)}, f32[1024]{0:T(1024)S(1)}) all-reduce(f32[]{:T(128)S(6)} %add.341, f32[3328]{0:T(1024)S(1)} %constant_dynamic-update-slice_fusion, f32[1024]{0:T(1024)S(1)} %bitcast.313), channel_id=1, replica_groups=mesh['seq'=2,'fsdp'=16] {'seq','fsdp'}, use_global_device_ids=true, to_apply=%region_35.36 | all-reduce | flops 4353 | bytes 34824 | tf_op jit(solution)/shard_map/psum | solution.py:386
  2993.8 48.1 %multiply_subtract_fusion = (f32[9496,512]{1,0:T(8,128)}, f32[9496,512]{1,0:T(8,128)}, f32[9496,512]{1,0:T(8,128)}) fusion(f32[9496,512]{1,0:T(8,128)} %param.33, f32[]{:T(128)} %bitcast.67, f32[]{:T(128)} %bitcast.66, f32[]{:T(128)S(6)} %div.206, f32[9497,512]{1,0:T(8,128)} %scatter_custom_fusion, f32[9496,512]{1,0:T(8,128)} %param.35, f32[9496,512]{1,0:T(8,128)} %param.34), kind=kLoop, calls=%fused_computation.51 | loop fusion | flops 77791232 | bytes 136134672 | tf_op jit(solution)/shard_map/sub | solution.py:206
  (438 shorter events, 463.7 us)
Async XLA Ops:
  8.0 907.8 %all-reduce.10.cloned.1.call-start = ((), (), s32[]{:S(2)}) async-start(), calls=%async_computation.23 | async-start | bytes 67108864
  267.4 685.0 %all-gather.8.cloned.1.call-start = ((), (), s32[]{:S(2)}) async-start(), calls=%async_computation.14 | async-start | bytes 8650752 | tf_op jit(solution)/shard_map/all_gather | solution.py:148
  269.1 1140.1 %all-gather.10.cloned.1.call-start = ((), (), s32[]{:S(2)}) async-start(), calls=%async_computation.15 | async-start | bytes 4325376 | tf_op jit(solution)/shard_map/all_gather | solution.py:149
  269.9 1149.6 %all-gather.12.cloned.1.call-start = ((), (), s32[]{:S(2)}) async-start(), calls=%async_computation.16 | async-start | bytes 12976128 | tf_op jit(solution)/shard_map/all_gather | solution.py:155
  915.8 7.5 copy-start.73
  919.5 29.2 all-to-all-start
  923.9 41.4 %copy-start.63 = (f32[1024]{0:T(1024)}, f32[1024]{0:T(1024)S(1)}, u32[]{:S(2)}) copy-start(f32[1024]{0:T(1024)S(1)} %get-tuple-element.437) | copy-start | bytes 12292
  948.7 16.6 copy-start.8
  969.4 6.6 copy-start.82
  971.1 29.7 all-to-all-start.3
  974.8 480.3 %all-gather.14.cloned.1.call-start = ((), (), s32[]{:S(2)}) async-start(), calls=%async_computation.17 | async-start | bytes 6488064 | tf_op jit(solution)/shard_map/all_gather | solution.py:156
  1002.2 35.1 %all-to-all-start.2 = ((bf16[1024,8,128]{2,0,1:T(8,128)(2,1)}), bf16[1024,8,128]{2,0,1:T(8,128)(2,1)S(1)}, u32[]{:S(2)}, u32[]{:S(2)}) async-start(bf16[1024,8,128]{2,0,1:T(8,128)(2,1)} %bitcast.289), calls=%async_computation.2 | async-start | bytes 4194304 | tf_op jit(solution)/shard_map/all_to_all | solution.py:270
  1010.1 97.2 %copy-start.15 = (f32[2048,64]{1,0:T(8,128)}, f32[2048,64]{1,0:T(8,128)S(1)}, u32[]{:S(2)}) copy-start(f32[2048,64]{1,0:T(8,128)S(1)} %copy.294) | copy-start | bytes 1572868
  1015.2 42.7 %copy-start.76 = (f32[128]{0:T(128)}, f32[128]{0:T(128)S(1)}, u32[]{:S(2)}) copy-start(f32[128]{0:T(128)S(1)} %get-tuple-element.439) | copy-start | bytes 1540
  1015.2 84.1 %copy-start.74 = (f32[128]{0:T(128)}, f32[128]{0:T(128)S(1)}, u32[]{:S(2)}) copy-start(f32[128]{0:T(128)S(1)} %get-tuple-element.440) | copy-start | bytes 1540
  1037.3 51.5 %all-to-all-start.1 = ((bf16[1024,16,128]{2,0,1:T(8,128)(2,1)}), bf16[1024,16,128]{2,0,1:T(8,128)(2,1)}, u32[]{:S(2)}, u32[]{:S(2)}) async-start(bf16[1024,16,128]{2,0,1:T(8,128)(2,1)} %copy_bitcast_fusion.1), calls=%async_computation.1 | async-start | bytes 8388608 | tf_op jit(solution)/shard_map/all_to_all | solution.py:269
  1047.2 10.7 copy-start.51
  1047.2 10.7 copy-start.45
  1143.2 15.4 copy-start.4
  1201.4 15.4 copy-start.4
  1259.6 15.4 copy-start.4
  1317.7 15.4 copy-start.4
  1351.8 50.6 %all-to-all-start.4 = ((bf16[2048,8,128]{2,1,0:T(8,128)(2,1)}), bf16[2048,8,128]{2,1,0:T(8,128)(2,1)}, u32[]{:S(2)}, u32[]{:S(2)}) async-start(bf16[2048,8,128]{2,1,0:T(8,128)(2,1)} %bitcast.282), calls=%async_computation.4 | async-start | bytes 8388608 | tf_op jit(solution)/shard_map/all_to_all | solution.py:278
  1357.4 1087.4 %reduce-scatter.10.cloned.1.call-start = ((), (), s32[]{:S(2)}) async-start(), calls=%async_computation.19 | async-start | bytes 8650752 | tf_op jit(solution)/shard_map/reduce_scatter | solution.py:164
  1402.3 6.9 copy-start.9
  1409.2 10.3 copy-start.72
  1455.1 13.4 copy-start.56
  1455.1 13.4 copy-start.59
  1466.6 110.4 %copy-start.54 = (f32[1024]{0:T(1024)}, f32[1024]{0:T(1024)S(1)}, u32[]{:S(2)}) copy-start(f32[1024]{0:T(1024)S(1)} %fusion.92) | copy-start | bytes 12292
  1512.2 64.8 %copy-start.67 = (f32[1,1024]{1,0:T(1,128)}, f32[1,1024]{1,0:T(1,128)S(1)}, u32[]{:S(2)}) copy-start(f32[1,1024]{1,0:T(1,128)S(1)} %fusion.83) | copy-start | bytes 12292
  1563.3 6.6 copy-start.25
  1577.0 869.4 %reduce-scatter.14.cloned.1.call-start = ((), (), s32[]{:S(2)}) async-start(), calls=%async_computation.21 | async-start | bytes 12976128 | tf_op jit(solution)/shard_map/reduce_scatter | solution.py:166
  1602.5 72.1 %all-to-all-start.5 = ((bf16[1024,16,128]{2,0,1:T(8,128)(2,1)}), bf16[1024,16,128]{2,0,1:T(8,128)(2,1)}, u32[]{:S(2)}, u32[]{:S(2)}) async-start(bf16[1024,16,128]{2,0,1:T(8,128)(2,1)} %bitcast.283), calls=%async_computation.5 | async-start | bytes 8388608 | tf_op jit(solution)/shard_map/all_to_all | solution.py:334
  1608.1 839.9 %reduce-scatter.12.cloned.1.call-start = ((), (), s32[]{:S(2)}) async-start(), calls=%async_computation.20 | async-start | bytes 25952256 | tf_op jit(solution)/shard_map/reduce_scatter | solution.py:165
  2193.9 46.0 %all-to-all-start.8 = ((bf16[2048,4,128]{2,1,0:T(4,128)(2,1)}), bf16[2048,4,128]{2,1,0:T(4,128)(2,1)}, u32[]{:S(2)}, u32[]{:S(2)}) async-start(bf16[2048,4,128]{2,1,0:T(4,128)(2,1)} %copy.318), calls=%async_computation.8 | async-start | bytes 4194304 | tf_op jit(solution)/shard_map/all_to_all | solution.py:363
  2214.3 12.9 slice-start
  2214.3 12.9 slice-start.1
  2214.3 12.9 copy-start.12
  2214.3 12.9 copy-start.75
  2227.3 11.2 copy-start.44
  2239.9 27.7 all-to-all-start.7
  2267.6 51.4 %all-to-all-start.6 = ((bf16[2048,8,128]{2,1,0:T(8,128)(2,1)}), bf16[2048,8,128]{2,1,0:T(8,128)(2,1)}, u32[]{:S(2)}, u32[]{:S(2)}) async-start(bf16[2048,8,128]{2,1,0:T(8,128)(2,1)} %fusion.39), calls=%async_computation.6 | async-start | bytes 8388608 | tf_op jit(solution)/shard_map/all_to_all | solution.py:357
  2273.4 408.0 %reduce-scatter.8.cloned.1.call-start = ((), (), s32[]{:S(2)}) async-start(), calls=%async_computation.18 | async-start | bytes 17301504 | tf_op jit(solution)/shard_map/reduce_scatter | solution.py:163
  2318.9 6.7 copy-start.29
  2340.8 16.4 copy-start.66
  2340.8 342.4 %all-gather.16.cloned.1.call-start = ((), (), s32[]{:S(2)}) async-start(), calls=%async_computation.22 | async-start | bytes 35651584 | tf_op jit(solution)/shard_map/all_gather | solution.py:194
  2342.4 14.9 copy-start.14
  2438.1 6.6 copy-start.78
  2438.1 6.6 copy-start.71
  2933.4 58.4 %copy-start.70 = (f32[3328]{0:T(1024)S(1)}, f32[3328]{0:T(1024)}, u32[]{:S(2)}) copy-start(f32[3328]{0:T(1024)} %param.50) | copy-start | bytes 39940
  2933.4 59.1 %copy-start.69 = (f32[3328]{0:T(1024)S(1)}, f32[3328]{0:T(1024)}, u32[]{:S(2)}) copy-start(f32[3328]{0:T(1024)} %param.49) | copy-start | bytes 39940
  2933.4 59.7 %copy-start.60 = (f32[1024]{0:T(1024)S(1)}, f32[1024]{0:T(1024)}, u32[]{:S(2)}) copy-start(f32[1024]{0:T(1024)} %param.51) | copy-start | bytes 12292
  2933.4 59.7 %copy-start.79 = (f32[1024]{0:T(1024)S(1)}, f32[1024]{0:T(1024)}, u32[]{:S(2)}) copy-start(f32[1024]{0:T(1024)} %param.53) | copy-start | bytes 12292
  2933.5 59.7 %copy-start.80 = (f32[1024]{0:T(1024)S(1)}, f32[1024]{0:T(1024)}, u32[]{:S(2)}) copy-start(f32[1024]{0:T(1024)} %param.52) | copy-start | bytes 12292
  2992.5 49.4 %copy-start.58 = (f32[3328]{0:T(1024)}, f32[3328]{0:T(1024)S(1)}, u32[]{:S(2)}) copy-start(f32[3328]{0:T(1024)S(1)} %get-tuple-element.402) | copy-start | bytes 39940
  2993.8 48.2 %copy-start.39 = (f32[64,1024]{1,0:T(8,128)S(1)}, f32[64,1024]{1,0:T(8,128)}, u32[]{:S(2)}) copy-start(f32[64,1024]{1,0:T(8,128)} %param.39) | copy-start | bytes 786436
  2993.8 48.2 %copy-start.40 = (f32[64,1024]{1,0:T(8,128)S(1)}, f32[64,1024]{1,0:T(8,128)}, u32[]{:S(2)}) copy-start(f32[64,1024]{1,0:T(8,128)} %reduce-scatter.10.cloned.1.call-done) | copy-start | bytes 786436
  2993.8 48.2 %copy-start.53 = (f32[64,1024]{1,0:T(8,128)S(1)}, f32[64,1024]{1,0:T(8,128)}, u32[]{:S(2)}) copy-start(f32[64,1024]{1,0:T(8,128)} %param.41) | copy-start | bytes 786436
  2993.8 50.3 %copy-start.36 = (f32[96,1024]{1,0:T(8,128)S(1)}, f32[96,1024]{1,0:T(8,128)}, u32[]{:S(2)}) copy-start(f32[96,1024]{1,0:T(8,128)} %param.45) | copy-start | bytes 1179652
  2993.8 50.3 %copy-start.37 = (f32[96,1024]{1,0:T(8,128)S(1)}, f32[96,1024]{1,0:T(8,128)}, u32[]{:S(2)}) copy-start(f32[96,1024]{1,0:T(8,128)} %reduce-scatter.14.cloned.1.call-done) | copy-start | bytes 1179652
  2993.8 50.3 %copy-start.49 = (f32[96,1024]{1,0:T(8,128)S(1)}, f32[96,1024]{1,0:T(8,128)}, u32[]{:S(2)}) copy-start(f32[96,1024]{1,0:T(8,128)} %param.47) | copy-start | bytes 1179652
  2993.8 50.3 %copy-start.50 = (f32[96,1024]{1,0:T(8,128)S(1)}, f32[96,1024]{1,0:T(8,128)}, u32[]{:S(2)}) copy-start(f32[96,1024]{1,0:T(8,128)} %param.46) | copy-start | bytes 1179652
  2993.8 51.5 %copy-start.47 = (f32[32,4096]{1,0:T(8,128)S(1)}, f32[32,4096]{1,0:T(8,128)}, u32[]{:S(2)}) copy-start(f32[32,4096]{1,0:T(8,128)} %param.38) | copy-start | bytes 1572868
  2993.8 51.5 %copy-start.48 = (f32[32,4096]{1,0:T(8,128)S(1)}, f32[32,4096]{1,0:T(8,128)}, u32[]{:S(2)}) copy-start(f32[32,4096]{1,0:T(8,128)} %param.37) | copy-start | bytes 1572868
  (53 other events, 193.1 us)
Sparse Core Ops, SparseCore 0:
  267.5 648.2 all-reduce.9
  2438.2 194.1 all-gather.15
Sparse Core Ops, SparseCore 1:
  271.7 147.3 all-gather.7
  422.7 119.9 all-gather.9
  546.4 163.1 all-gather.11
  979.5 75.9 all-gather.13
  1577.0 148.7 reduce-scatter.9
  1733.5 150.5 reduce-scatter.13
  1890.3 241.2 reduce-scatter.11
  2340.9 340.4 reduce-scatter.7
where the time goes:
time: 3070 us; the launch traced here: 3060 us
  waiting for transfers between devices  1090 us (36%)
  matrix products  669 us (22%)
  other arithmetic  654 us (21%)
  local copies, waits for them, and re-layouts  382 us (12%)
  blocking collectives  174 us (6%)
  starting transfers between devices  43.3 us (1%)
    unnamed x11, waiting for transfers between devices  645 us
    reduce_scatter x1, waiting for transfers between devices, reduce_grads(): lax.psum_scatter(pieces[0], ('seq', 'fsdp'), scatter_dimension=0, tiled=T...  231 us
    scatter-add x1, other arithmetic, embed_backward(): jax.ops.segment_sum(rows_in, target, num_segments=height + 1)[:height]  227 us
    gather x2, local copies, waits for them, and re-layouts, embed_forward(): jnp.take(table.astype(jnp.bfloat16), jnp.clip(local_row, 0, height - 1),...  180 us
    dot_general x8, matrix products, one_block(): jnp.einsum('qhd,khd->hqk', row_block, key_all, preferred_element_type=jnp...  169 us
    convert_element_type x4, other arithmetic, one_block(): score_grad = (probs * (prob_grad - jnp.sum(probs * prob_grad, axis=-1, ke...  114 us
    dot_general x4, matrix products, one_block(): jnp.einsum('hqk,qhd->khd', probs.astype(jnp.bfloat16), grad_block, prefer...  75 us
    dot_general x4, matrix products, one_block(): jnp.einsum('hqk,khd->qhd', probs, value_all, preferred_element_type=jnp.f...  63.3 us
  transfers between devices with their start and end apart: 19, of which 10 were waited for; matrix products, arithmetic and copies ran while one was open for 35% of the time, Pallas kernels for 0%

commit v1 on v0

v1 whole, which is shorter than its diff:
```python
import functools

import jax
import jax.numpy as jnp
from jax import lax
from jax.experimental import pallas as pl
from jax.experimental.pallas import tpu as pltpu
from jax.sharding import PartitionSpec as P

D = 1024
QUERY_HEADS = 16
KEY_VALUE_HEADS = 8
HEAD_SIZE = 128
FF = 3072
QUERY_COLS = QUERY_HEADS * HEAD_SIZE
KEY_COLS = KEY_VALUE_HEADS * HEAD_SIZE

NORM_EPS = 1e-06
ROPE_THETA = 1000000.0
LEARN_RATE = 0.04
BETA_ONE = 0.9
BETA_TWO = 0.95
ADAM_EPS = 1e-08
WEIGHT_DECAY = 0.1
CLIP_NORM = 1.0
PRECISE = lax.Precision.HIGHEST
MASKED = -1e30
LOG2E = 1.4426950408889634
MESH = pl.DeviceIdType.MESH
VMEM_BYTES = 56 * 2**20


def rms_norm(values, gain_vec):
    return (
        values * lax.rsqrt(jnp.mean(values * values, axis=-1, keepdims=True) + NORM_EPS) * gain_vec
    )


def layout(bounds, token_pos):
    segment = jnp.sum((token_pos[:, None] >= bounds[None, :]).astype(jnp.int32), axis=1)
    starts_all = jnp.concatenate([jnp.zeros((1,), jnp.int32), bounds])
    slot_ids = jnp.arange(bounds.shape[0] + 1, dtype=jnp.int32)
    begin = jnp.sum(
        jnp.where(segment[:, None] == slot_ids[None, :], starts_all[None, :], 0), axis=1
    )
    return (segment, begin)


def exchange_kernel(n_seq, n_fsdp, to_all, x_ref, *refs):
    o_ref, send_sem, recv_sem, own_sem = refs[-4:]
    seq_at, fsdp_at = lax.axis_index("seq"), lax.axis_index("fsdp")
    count = n_seq * n_fsdp
    me = seq_at * n_fsdp + fsdp_at

    def place(step):
        other = lax.rem(me + step, count)
        return other, (other // n_fsdp, lax.rem(other, n_fsdp))

    barrier = pltpu.get_barrier_semaphore()

    def greet(step, carry):
        pl.semaphore_signal(barrier, inc=1, device_id=place(step)[1], device_id_type=MESH)
        return carry

    lax.fori_loop(1, count, greet, 0)
    pl.semaphore_wait(barrier, count - 1)
    own = pltpu.make_async_copy(x_ref if to_all else x_ref.at[me], o_ref.at[me], own_sem)
    own.start()

    def copy(step):
        other, where = place(step)
        return pltpu.make_async_remote_copy(
            src_ref=x_ref if to_all else x_ref.at[other],
            dst_ref=o_ref.at[me],
            send_sem=send_sem.at[step],
            recv_sem=recv_sem.at[step],
            device_id=where,
            device_id_type=MESH,
        )

    def begin(step, carry):
        copy(step).start()
        return carry

    def finish(step, carry):
        copy(step).wait()
        return carry

    lax.fori_loop(1, count, begin, 0)
    own.wait()
    lax.fori_loop(1, count, finish, 0)


def exchange(blocks, to_all, collective_id, after=()):
    n_seq, n_fsdp = lax.axis_size("seq"), lax.axis_size("fsdp")
    count = n_seq * n_fsdp
    shape = (count,) + blocks.shape if to_all else blocks.shape
    return pl.pallas_call(
        functools.partial(exchange_kernel, n_seq, n_fsdp, to_all),
        out_shape=jax.ShapeDtypeStruct(shape, blocks.dtype),
        in_specs=[pl.BlockSpec(memory_space=pl.ANY)] * (1 + len(after)),
        out_specs=pl.BlockSpec(memory_space=pl.ANY),
        scratch_shapes=[
            pltpu.SemaphoreType.DMA((count,)),
            pltpu.SemaphoreType.DMA((count,)),
            pltpu.SemaphoreType.DMA,
        ],
        compiler_params=pltpu.CompilerParams(collective_id=collective_id, has_side_effects=True),
    )(blocks, *after)


def sum_small(values, collective_id):
    rows = -(-values.shape[0] // 1024) * 8
    block = jnp.zeros((rows * 128,), jnp.float32).at[: values.shape[0]].set(values)
    parts = exchange(block.reshape(rows, 128), True, collective_id)
    return jnp.sum(parts, axis=0).reshape(-1)[: values.shape[0]]


def capacity(tokens, owners):
    return -(-(5 * tokens) // (4 * owners * 16)) * 16


def rank_ids(ids, height):
    at = jnp.arange(ids.shape[0], dtype=jnp.int32)
    again = jnp.any((ids[:, None] == ids[None, :]) & (at[None, :] < at[:, None]), axis=1)
    owner = ids // height
    floor = owner * height
    below = (
        (ids[None, :] < ids[:, None]) & (ids[None, :] >= floor[:, None]) & jnp.logical_not(again)[None, :]
    )
    return owner, jnp.sum(below.astype(jnp.int32), axis=1)


def slot_lists(ids, owner, rank, start, size, owners, height):
    within = rank - start
    valid = (within >= 0) & (within < size)
    slot = jnp.where(valid, owner * size + within, -1)
    slot_ids = jnp.arange(owners * size, dtype=jnp.int32)
    rows = jnp.max(
        jnp.where(slot[None, :] == slot_ids[:, None], (ids - owner * height)[None, :], -1), axis=1
    )
    return slot, rows.reshape(owners, size)


def pick_rows(table, wanted):
    count, size = wanted.shape
    rows = jnp.take(table, jnp.maximum(wanted, 0).reshape(-1), axis=0)
    return lax.optimization_barrier(rows).astype(jnp.bfloat16).reshape(count, size, table.shape[1])


def one_hot(slot, slots):
    return (slot[:, None] == jnp.arange(slots, dtype=jnp.int32)[None, :]).astype(jnp.bfloat16)


def spread_rows(arrived, slot, n_seq):
    count, size, columns = arrived.shape
    chosen = one_hot(slot, count // n_seq * size)
    parts = arrived.reshape(n_seq, -1, columns)
    return jnp.concatenate(
        [jnp.dot(chosen, parts[s], preferred_element_type=jnp.float32) for s in range(n_seq)], axis=1
    ).astype(jnp.bfloat16)


def collect_rows(token_grad, slot, n_seq, n_fsdp, size):
    chosen = one_hot(slot, n_fsdp * size)
    columns = token_grad.shape[1] // n_seq
    parts = [
        lax.dot_general(
            chosen,
            token_grad[:, s * columns : (s + 1) * columns],
            (((0,), (0,)), ((), ())),
            preferred_element_type=jnp.float32,
        )
        .astype(jnp.bfloat16)
        .reshape(n_fsdp, size, columns)
        for s in range(n_seq)
    ]
    return jnp.concatenate(parts, axis=0)


def embed_forward(token_ids, table):
    n_seq, n_fsdp = lax.axis_size("seq"), lax.axis_size("fsdp")
    ids = token_ids.reshape(-1)
    tokens, height = ids.shape[0], table.shape[0]
    size = capacity(tokens, n_fsdp)
    owner, rank = rank_ids(ids, height)
    slot, rows = slot_lists(ids, owner, rank, 0, size, n_fsdp, height)
    width = -(-(size + 1) // 1024) * 1024
    note = jnp.zeros((n_fsdp, width), jnp.int32)
    note = note.at[:, :size].set(rows).at[:, size].set(jnp.max(rank))
    note = note.reshape(n_fsdp, width // 128, 128)
    note = jnp.concatenate([note] * n_seq, axis=0)
    heard = exchange(note, False, 1).reshape(n_seq * n_fsdp, width)
    wanted = heard[:, :size]
    most = jnp.max(heard[:, size])
    arrived = exchange(pick_rows(table, wanted), False, 2)

    def plain(arrived):
        return spread_rows(arrived, slot, n_seq)

    def rounds(arrived):
        def another(carry):
            start, total = carry
            slot, rows = slot_lists(ids, owner, rank, start, size, n_fsdp, height)
            wanted = lax.all_to_all(
                jnp.concatenate([rows] * n_seq, axis=0), ("seq", "fsdp"), 0, 0, tiled=True
            )
            own_table = lax.optimization_barrier((table, start))[0]
            arrived = lax.all_to_all(pick_rows(own_table, wanted), ("seq", "fsdp"), 0, 0, tiled=True)
            return start + size, total + spread_rows(arrived, slot, n_seq)

        return lax.while_loop(lambda carry: carry[0] <= most, another, (jnp.int32(size), plain(arrived)))[1]

    embedded = lax.cond(most < size, plain, rounds, arrived)
    return embedded, (ids, owner, rank, slot, wanted, most, size)


def add_rows(total, arrived, wanted):
    height = total.shape[0]
    target = jnp.where(wanted >= 0, wanted, height).reshape(-1)
    rows = arrived.reshape(target.shape[0], -1).astype(jnp.float32)
    return total.at[target].add(rows, mode="drop")


def scatter_kernel(size, wanted_ref, count_ref, arrived_ref, *refs):
    total_ref, square_ref, rows_ref = refs[-3:]
    sources = arrived_ref.shape[0]
    height = total_ref.shape[0]

    def clear(i, carry):
        at = pl.ds(pl.multiple_of(i * 8, 8), 8)
        total_ref[at, :] = jnp.zeros((8, total_ref.shape[1]), jnp.float32)
        return carry

    whole = height // 8
    lax.fori_loop(0, whole, clear, 0, unroll=8)
    if height % 8:
        total_ref[whole * 8 :, :] = jnp.zeros((height % 8, total_ref.shape[1]), jnp.float32)

    def one_source(k, carry):
        rows_ref[...] = arrived_ref[k].astype(jnp.float32)
        count = count_ref[k]

        def four(i, inner):
            first = i * 4
            at = [wanted_ref[k * size + first + n] for n in range(4)]
            sums = [total_ref[pl.ds(at[n], 1), :] + rows_ref[pl.ds(first + n, 1), :] for n in range(4)]
            for n in range(4):
                total_ref[pl.ds(at[n], 1), :] = sums[n]
            return inner

        def one(i, inner):
            at = wanted_ref[k * size + i]
            total_ref[pl.ds(at, 1), :] += rows_ref[pl.ds(i, 1), :]
            return inner

        lax.fori_loop(0, count // 4, four, 0)
        lax.fori_loop(count // 4 * 4, count, one, 0)
        return carry

    lax.fori_loop(0, sources, one_source, 0)

    def add_square(i, carry):
        block = total_ref[pl.ds(pl.multiple_of(i * 8, 8), 8), :]
        return carry + block * block

    partial = lax.fori_loop(0, whole, add_square, jnp.zeros((8, total_ref.shape[1]), jnp.float32), unroll=8)
    if height % 8:
        rest = total_ref[whole * 8 :, :]
        partial = partial + jnp.concatenate(
            [rest * rest, jnp.zeros((8 - height % 8, total_ref.shape[1]), jnp.float32)], axis=0
        )
    square_ref[...] = partial


def scatter_rows(arrived, wanted, height, after):
    sources, size, width = arrived.shape
    counts = jnp.sum((wanted >= 0).astype(jnp.int32), axis=1)
    vmem = pl.BlockSpec(memory_space=pltpu.VMEM)
    return pl.pallas_call(
        functools.partial(scatter_kernel, size),
        grid_spec=pltpu.PrefetchScalarGridSpec(
            num_scalar_prefetch=2,
            grid=(),
            in_specs=[vmem] + [pl.BlockSpec(memory_space=pl.ANY)] * len(after),
            out_specs=[vmem, vmem],
            scratch_shapes=[pltpu.VMEM((size, width), jnp.float32)],
        ),
        out_shape=[
            jax.ShapeDtypeStruct((height, width), jnp.float32),
            jax.ShapeDtypeStruct((8, width), jnp.float32),
        ],
        compiler_params=pltpu.CompilerParams(vmem_limit_bytes=VMEM_BYTES),
        cost_estimate=pl.CostEstimate(flops=10**9, bytes_accessed=80 * 2**20, transcendentals=0),
    )(wanted.reshape(-1), counts, arrived, *after)


def embed_send(token_grad, kept, after):
    n_seq, n_fsdp = lax.axis_size("seq"), lax.axis_size("fsdp")
    slot, size = kept[3], kept[6]
    return exchange(collect_rows(token_grad, slot, n_seq, n_fsdp, size), False, 5, after)


def embed_backward(token_grad, arrived, kept, height, after):
    n_seq, n_fsdp = lax.axis_size("seq"), lax.axis_size("fsdp")
    ids, owner, rank, slot, wanted, most, size = kept

    def plain(arrived, *after):
        total, squares = scatter_rows(arrived, wanted, height, after)
        return total, jnp.sum(squares)

    def rounds(arrived, *after):
        def another(carry):
            start, total = carry
            slot, rows = slot_lists(ids, owner, rank, start, size, n_fsdp, height)
            wanted = lax.all_to_all(
                jnp.concatenate([rows] * n_seq, axis=0), ("seq", "fsdp"), 0, 0, tiled=True
            )
            arrived = lax.all_to_all(
                collect_rows(token_grad, slot, n_seq, n_fsdp, size), ("seq", "fsdp"), 0, 0, tiled=True
            )
            return start + size, add_rows(total, arrived, wanted)

        total = plain(arrived, *after)[0]
        total = lax.while_loop(lambda carry: carry[0] <= most, another, (jnp.int32(size), total))[1]
        return total, jnp.sum(total * total)

    return lax.cond(most < size, plain, rounds, arrived, *after)


ANY = pl.BlockSpec(memory_space=pl.ANY)
HALF = KEY_VALUE_HEADS // 2


def turn(values):
    return pltpu.roll(values, HEAD_SIZE // 2, axis=1)


def columns(head):
    return slice(head * HEAD_SIZE, (head + 1) * HEAD_SIZE)


def shape_head(raw, cosine, sine, gain):
    raw = raw.astype(jnp.float32)
    scale = lax.rsqrt(jnp.mean(raw * raw, axis=-1, keepdims=True) + NORM_EPS)
    normed = raw * scale * gain
    return (normed * cosine + turn(normed) * sine).astype(jnp.bfloat16)


def shape_head_back(raw, cosine, sine, gain, grad):
    raw = raw.astype(jnp.float32)
    scale = lax.rsqrt(jnp.mean(raw * raw, axis=-1, keepdims=True) + NORM_EPS)
    grad = grad * cosine + turn(grad * sine)
    unit = raw * scale
    gain_grad = jnp.sum(grad * unit, axis=0, keepdims=True)
    grad = grad * gain
    inner = jnp.mean(grad * unit, axis=-1, keepdims=True)
    return (scale * (grad - unit * inner)).astype(jnp.bfloat16), gain_grad


def queries_kernel(raw_ref, cos_ref, sin_ref, gain_ref, out_ref):
    for head in range(QUERY_HEADS):
        at = columns(head)
        out_ref[:, at] = shape_head(raw_ref[:, at], cos_ref[...], sin_ref[...], gain_ref[0:1, :])


def keys_kernel(raw_ref, cos_ref, sin_ref, gain_ref, *out_refs):
    for head in range(KEY_VALUE_HEADS):
        out_ref = out_refs[head // HALF]
        out_ref[:, columns(head % HALF)] = shape_head(
            raw_ref[:, columns(head)], cos_ref[...], sin_ref[...], gain_ref[1:2, :]
        )
    for half in range(2):
        first = KEY_COLS + half * HALF * HEAD_SIZE
        out_refs[half][:, HALF * HEAD_SIZE :] = raw_ref[:, first : first + HALF * HEAD_SIZE]


def token_blocks(rows, width):
    return pl.BlockSpec((rows, width), lambda i: (i, 0))


def shape_queries(raw, cosine, sine, gains):
    tokens = raw.shape[0]
    rows = min(256, tokens)
    return pl.pallas_call(
        queries_kernel,
        grid=(tokens // rows,),
        in_specs=[
            token_blocks(rows, QUERY_COLS),
            token_blocks(rows, HEAD_SIZE),
            token_blocks(rows, HEAD_SIZE),
            pl.BlockSpec((2, HEAD_SIZE), lambda i: (0, 0)),
        ],
        out_specs=token_blocks(rows, QUERY_COLS),
        out_shape=jax.ShapeDtypeStruct((tokens, QUERY_COLS), jnp.bfloat16),
        compiler_params=pltpu.CompilerParams(vmem_limit_bytes=VMEM_BYTES),
        cost_estimate=pl.CostEstimate(flops=4 * 10**9, bytes_accessed=8 * 2**20, transcendentals=0),
    )(raw, cosine, sine, gains)


def shape_keys(raw, cosine, sine, gains):
    tokens = raw.shape[0]
    rows = min(256, tokens)
    half = jax.ShapeDtypeStruct((tokens, KEY_COLS), jnp.bfloat16)
    return pl.pallas_call(
        keys_kernel,
        grid=(tokens // rows,),
        in_specs=[
            token_blocks(rows, 2 * KEY_COLS),
            token_blocks(rows, HEAD_SIZE),
            token_blocks(rows, HEAD_SIZE),
            pl.BlockSpec((2, HEAD_SIZE), lambda i: (0, 0)),
        ],
        out_specs=[token_blocks(rows, KEY_COLS)] * 2,
        out_shape=[half, half],
        compiler_params=pltpu.CompilerParams(vmem_limit_bytes=VMEM_BYTES),
        cost_estimate=pl.CostEstimate(flops=2 * 10**9, bytes_accessed=8 * 2**20, transcendentals=0),
    )(raw, cosine, sine, gains)


def add_gain_grad(gain_ref, total):
    @pl.when(pl.program_id(0) == 0)
    def _():
        gain_ref[...] = jnp.zeros_like(gain_ref)

    gain_ref[0:1, :] += total


def queries_back_kernel(raw_ref, cos_ref, sin_ref, gain_ref, dq_ref, *refs):
    out_ref, dgain_ref = refs[-2:]
    total = jnp.zeros((1, HEAD_SIZE), jnp.float32)
    for head in range(QUERY_HEADS):
        at = columns(head)
        grad = dq_ref[:, at].astype(jnp.float32)
        out_ref[:, at], part = shape_head_back(raw_ref[:, at], cos_ref[...], sin_ref[...], gain_ref[0:1, :], grad)
        total = total + part
    add_gain_grad(dgain_ref, total)


def keys_back_kernel(raw_ref, cos_ref, sin_ref, gain_ref, own_a_ref, own_b_ref, more_a_ref, more_b_ref, out_ref, dgain_ref):
    total = jnp.zeros((1, HEAD_SIZE), jnp.float32)
    for head in range(KEY_VALUE_HEADS):
        own_ref, more_ref = ((own_a_ref, more_a_ref), (own_b_ref, more_b_ref))[head // HALF]
        at, part_at = columns(head), columns(head % HALF)
        grad = own_ref[0, :, part_at] + more_ref[0, :, part_at].astype(jnp.float32)
        out_ref[:, at], part = shape_head_back(raw_ref[:, at], cos_ref[...], sin_ref[...], gain_ref[1:2, :], grad)
        total = total + part
    for half, (own_ref, more_ref) in enumerate(((own_a_ref, more_a_ref), (own_b_ref, more_b_ref))):
        first = KEY_COLS + half * HALF * HEAD_SIZE
        out_ref[:, first : first + HALF * HEAD_SIZE] = (
            own_ref[1] + more_ref[1].astype(jnp.float32)
        ).astype(jnp.bfloat16)
    add_gain_grad(dgain_ref, total)


def shape_back(kernel, raw, cosine, sine, gains, grads, after=()):
    tokens = raw.shape[0]
    rows = min(128, tokens)
    wide = [
        pl.BlockSpec((2, rows, g.shape[2]), lambda i: (0, i, 0)) if g.ndim == 3 else token_blocks(rows, g.shape[1])
        for g in grads
    ]
    return pl.pallas_call(
        kernel,
        grid=(tokens // rows,),
        in_specs=[
            token_blocks(rows, raw.shape[1]),
            token_blocks(rows, HEAD_SIZE),
            token_blocks(rows, HEAD_SIZE),
            pl.BlockSpec((2, HEAD_SIZE), lambda i: (0, 0)),
        ]
        + wide
        + [ANY] * len(after),
        out_specs=[token_blocks(rows, raw.shape[1]), pl.BlockSpec((8, HEAD_SIZE), lambda i: (0, 0))],
        out_shape=[
            jax.ShapeDtypeStruct(raw.shape, jnp.bfloat16),
            jax.ShapeDtypeStruct((8, HEAD_SIZE), jnp.float32),
        ],
        compiler_params=pltpu.CompilerParams(vmem_limit_bytes=VMEM_BYTES),
        cost_estimate=pl.CostEstimate(flops=5 * 10**9, bytes_accessed=20 * 2**20, transcendentals=0),
    )(raw, cosine, sine, gains, *grads, *after)


def both_heads(block):
    return jnp.concatenate([block[:, :HEAD_SIZE], block[:, HEAD_SIZE:]], axis=0)


def key_ranges(scalar_ref, step, rows, keys):
    first_own, first_before, low = scalar_ref[0], scalar_ref[1], scalar_ref[2 + 2 * step]
    before = (jnp.minimum(low, first_own) - first_before) // keys, (first_own - first_before) // keys
    own = jnp.maximum(low - first_own, 0) // keys, ((step + 1) * rows - 1) // keys + 1
    return first_own, first_before, before, own


def allowed_keys(begin_ref, offset, rows, keys):
    begin = begin_ref[...] - offset
    at = lax.broadcasted_iota(jnp.int32, (rows, 1), 0)
    key_at = lax.broadcasted_iota(jnp.int32, (rows, keys), 1)
    return begin, at, key_at


def visit_blocks(scalar_ref, begin_ref, rows, keys, refs, work):
    step = pl.program_id(1)
    first_own, first_before, before, own = key_ranges(scalar_ref, step, rows, keys)
    first_row = first_own + step * rows
    last_begin = scalar_ref[3 + 2 * step]

    def run(bounds, base, group):
        def one(j, carry):
            at = pl.ds(pl.multiple_of(j * keys, keys), keys)
            first_key = base + j * keys
            whole = (first_key + keys - 1 <= first_row) & (first_key >= last_begin)

            @pl.when(whole)
            def _():
                work(*group, at, None)

            @pl.when(jnp.logical_not(whole))
            def _():
                begin = begin_ref[...] - first_key
                row = (first_row - first_key) + lax.broadcasted_iota(jnp.int32, (rows, 1), 0)
                key = lax.broadcasted_iota(jnp.int32, (rows, keys), 1)
                work(*group, at, (key <= row) & (key >= begin))

            return carry

        lax.fori_loop(bounds[0], bounds[1], one, 0)

    run(before, first_before, refs[0])
    run(own, first_own, refs[1])


def forward_kernel(keys, scalar_ref, q_ref, kb_ref, vb_ref, k_ref, v_ref, begin_ref, *refs):
    o_ref, lse_ref, acc_ref = refs[-3:]
    rows = q_ref.shape[0]
    query = both_heads(q_ref[...])
    acc_ref[...] = jnp.zeros_like(acc_ref)
    ones = jnp.ones((keys, HEAD_SIZE), jnp.bfloat16)

    def work(key_ref, value_ref, at, mask):
        value = jnp.concatenate([value_ref[at, :], ones], axis=1)
        scores = [
            lax.dot_general(
                query[h * rows : (h + 1) * rows], key_ref[at, :], (((1,), (1,)), ((), ())),
                preferred_element_type=jnp.float32,
            )
            for h in range(2)
        ]
        for h in range(2):
            weight = jnp.exp2(scores[h] * (LOG2E * HEAD_SIZE**-0.5))
            if mask is not None:
                weight = jnp.where(mask, weight, 0.0)
            acc_ref[h * rows : (h + 1) * rows, :] += jnp.dot(
                weight.astype(jnp.bfloat16), value, preferred_element_type=jnp.float32
            )

    visit_blocks(scalar_ref, begin_ref, rows, keys, ((kb_ref, vb_ref), (k_ref, v_ref)), work)
    acc = acc_ref[...]
    total = acc[:, HEAD_SIZE : HEAD_SIZE + 1]
    out = (acc[:, :HEAD_SIZE] / total).astype(jnp.bfloat16)
    o_ref[:, :HEAD_SIZE] = out[:rows]
    o_ref[:, HEAD_SIZE:] = out[rows:]
    lse = jnp.log2(total)
    lse_ref[0, :, 0:1] = lse[:rows]
    lse_ref[0, :, 1:2] = lse[rows:]


def attention_specs(tokens, length, rows, first):
    key = lambda h, i, s: (0, h)
    value = lambda h, i, s: (0, HALF + h)
    return [
        pl.BlockSpec((rows, 2 * HEAD_SIZE), lambda h, i, s: (i, first + h)),
        pl.BlockSpec((length, HEAD_SIZE), key),
        pl.BlockSpec((length, HEAD_SIZE), value),
        pl.BlockSpec((tokens, HEAD_SIZE), key),
        pl.BlockSpec((tokens, HEAD_SIZE), value),
        pl.BlockSpec((rows, 1), lambda h, i, s: (i, 0)),
    ]


def attention_forward(scalars, query, before, own, begin, rows, keys, first, filled):
    tokens = query.shape[0]
    specs = attention_specs(tokens, before.shape[0], rows, first)
    return pl.pallas_call(
        functools.partial(forward_kernel, keys),
        grid_spec=pltpu.PrefetchScalarGridSpec(
            num_scalar_prefetch=1,
            grid=(HALF, tokens // rows),
            in_specs=specs + [ANY] * len(filled),
            out_specs=[specs[0], pl.BlockSpec((1, rows, 2), lambda h, i, s: (first + h, i, 0))],
            scratch_shapes=[pltpu.VMEM((2 * rows, 2 * HEAD_SIZE), jnp.float32)],
        ),
        out_shape=[
            jax.ShapeDtypeStruct((tokens, QUERY_COLS), jnp.bfloat16),
            jax.ShapeDtypeStruct((KEY_VALUE_HEADS, tokens, 2), jnp.float32),
        ],
        input_output_aliases={7 + i: i for i in range(len(filled))},
        compiler_params=pltpu.CompilerParams(vmem_limit_bytes=VMEM_BYTES),
        cost_estimate=pl.CostEstimate(flops=20 * 10**9, bytes_accessed=16 * 2**20, transcendentals=10**7),
    )(scalars, query, before, before, own, own, begin, *filled)


def backward_kernel(keys, scalar_ref, q_ref, kb_ref, vb_ref, k_ref, v_ref, begin_ref, do_ref, o_ref, lse_ref, *refs):
    dq_ref, before_ref, own_ref, acc_ref, dq_acc_ref = refs[-5:]
    step = pl.program_id(1)
    rows = q_ref.shape[0]
    query = both_heads(q_ref[...])
    grad = both_heads(do_ref[...])
    out = both_heads(o_ref[...])
    lse = jnp.concatenate([lse_ref[0, :, 0:1], lse_ref[0, :, 1:2]], axis=0)
    inner = jnp.sum(grad.astype(jnp.float32) * out.astype(jnp.float32), axis=-1, keepdims=True)

    @pl.when(step == 0)
    def _():
        acc_ref[...] = jnp.zeros_like(acc_ref)
        own_ref[...] = jnp.zeros_like(own_ref)

    dq_acc_ref[...] = jnp.zeros_like(dq_acc_ref)

    def work(key_ref, value_ref, sum_ref, at, mask):
        key = key_ref[at, :]
        score = lax.dot_general(query, key, (((1,), (1,)), ((), ())), preferred_element_type=jnp.float32)
        prob_grad = lax.dot_general(
            grad, value_ref[at, :], (((1,), (1,)), ((), ())), preferred_element_type=jnp.float32
        )
        prob = jnp.exp2(score * (LOG2E * HEAD_SIZE**-0.5) - lse)
        if mask is not None:
            prob = jnp.where(jnp.concatenate([mask, mask], axis=0), prob, 0.0)
        sum_ref[1, at, :] += lax.dot_general(
            prob.astype(jnp.bfloat16), grad, (((0,), (0,)), ((), ())), preferred_element_type=jnp.float32
        )
        score_grad = (prob * (prob_grad - inner)).astype(jnp.bfloat16)
        sum_ref[0, at, :] += lax.dot_general(
            score_grad, query, (((0,), (0,)), ((), ())), preferred_element_type=jnp.float32
        )
        dq_acc_ref[...] += jnp.dot(score_grad, key, preferred_element_type=jnp.float32)

    visit_blocks(
        scalar_ref, begin_ref, rows, keys, ((kb_ref, vb_ref, acc_ref), (k_ref, v_ref, own_ref)), work
    )
    dq = dq_acc_ref[...] * HEAD_SIZE**-0.5
    dq_ref[:, :HEAD_SIZE] = dq[:rows]
    dq_ref[:, HEAD_SIZE:] = dq[rows:]

    @pl.when(step == pl.num_programs(1) - 1)
    def _():
        own_ref[0] = own_ref[0] * HEAD_SIZE**-0.5
        before_ref[0] = (acc_ref[0] * HEAD_SIZE**-0.5).astype(before_ref.dtype)
        before_ref[1] = acc_ref[1].astype(before_ref.dtype)


def attention_backward(scalars, query, before, own, begin, grad_out, out, lse, rows, keys, first, filled, after):
    tokens, length = query.shape[0], before.shape[0]
    specs = attention_specs(tokens, length, rows, first)
    both = lambda h, i, s: (0, 0, h)
    before_type = jnp.bfloat16 if length == tokens else jnp.float32
    return pl.pallas_call(
        functools.partial(backward_kernel, keys),
        grid_spec=pltpu.PrefetchScalarGridSpec(
            num_scalar_prefetch=1,
            grid=(HALF, tokens // rows),
            in_specs=specs
            + [specs[0], specs[0], pl.BlockSpec((1, rows, 2), lambda h, i, s: (first + h, i, 0))]
            + [ANY] * (len(filled) + len(after)),
            out_specs=[
                specs[0],
                pl.BlockSpec((2, length, HEAD_SIZE), both),
                pl.BlockSpec((2, tokens, HEAD_SIZE), both),
            ],
            scratch_shapes=[
                pltpu.VMEM((2, length, HEAD_SIZE), jnp.float32),
                pltpu.VMEM((2 * rows, HEAD_SIZE), jnp.float32),
            ],
        ),
        out_shape=[
            jax.ShapeDtypeStruct((tokens, QUERY_COLS), jnp.float32),
            jax.ShapeDtypeStruct((2, length, HALF * HEAD_SIZE), before_type),
            jax.ShapeDtypeStruct((2, tokens, HALF * HEAD_SIZE), jnp.float32),
        ],
        input_output_aliases={10 + i: i for i in range(len(filled))},
        compiler_params=pltpu.CompilerParams(vmem_limit_bytes=VMEM_BYTES),
        cost_estimate=pl.CostEstimate(flops=40 * 10**9, bytes_accessed=40 * 2**20, transcendentals=10**7),
    )(scalars, query, before, before, own, own, begin, grad_out, out, lse, *filled, *after)


def tokens_before(own):
    if lax.axis_size("seq") != 2:
        return lax.all_gather(own, "seq", axis=0, tiled=True)
    return lax.ppermute(own, "seq", [(0, 1), (1, 0)])


def to_tokens_before(parts):
    if lax.axis_size("seq") != 2:
        return lax.psum_scatter(parts, "seq", scatter_dimension=1, tiled=True)
    return lax.ppermute(parts, "seq", [(0, 1), (1, 0)])


def fetch(weight):
    return lax.all_gather(weight.astype(jnp.bfloat16), ("seq", "fsdp"), axis=0, tiled=True)


def trade(values, axis, bit):
    count = lax.axis_size(axis)
    return lax.ppermute(values, axis, [(i, i ^ bit) for i in range(count)])


def halves(values, dim, at):
    return (
        lax.dynamic_index_in_dim(values, at, dim, keepdims=False),
        lax.dynamic_index_in_dim(values, 1 - at, dim, keepdims=False),
    )


def by_stages():
    return (lax.axis_size("seq"), lax.axis_size("fsdp")) == (2, 16)


def where_am_i():
    at = lax.axis_index("fsdp")
    return lax.axis_index("seq"), at >> 2, (at >> 1) & 1, at & 1


def gradient_kernel(height, core_ref, left_ref, right_ref, *refs):
    keep_ref, send_ref, turned_ref = refs[-3:]

    @pl.when(pl.program_id(1) == 0)
    def _():
        turned_ref[...] = left_ref[...].T

    product = jnp.dot(turned_ref[...], right_ref[...], preferred_element_type=jnp.float32)
    even = core_ref[0] == 0
    for p in range(keep_ref.shape[0]):
        first = product[2 * p * height : (2 * p + 1) * height]
        second = product[(2 * p + 1) * height : (2 * p + 2) * height]
        keep_ref[p] = jnp.where(even, first, second).astype(jnp.bfloat16)
        send_ref[p] = jnp.where(even, second, first).astype(jnp.bfloat16)


def gradient_blocks(left, right, rows, place, packed_rows, filled):
    tokens, tall = left.shape
    height = tall // 32
    pairs = rows // (2 * height)
    out = jax.ShapeDtypeStruct((16, packed_rows, D), jnp.bfloat16)
    block = pl.BlockSpec((pairs, height, D), lambda i, j, s: (i, place(j), 0))
    return pl.pallas_call(
        functools.partial(gradient_kernel, height),
        grid_spec=pltpu.PrefetchScalarGridSpec(
            num_scalar_prefetch=1,
            grid=(tall // rows, right.shape[1] // D),
            in_specs=[
                pl.BlockSpec((tokens, rows), lambda i, j, s: (0, i)),
                pl.BlockSpec((tokens, D), lambda i, j, s: (0, j)),
            ]
            + [ANY] * len(filled),
            out_specs=[block, block],
            scratch_shapes=[pltpu.VMEM((rows, tokens), jnp.bfloat16)],
        ),
        out_shape=[out, out],
        input_output_aliases={3 + i: i for i in range(len(filled))},
        compiler_params=pltpu.CompilerParams(vmem_limit_bytes=VMEM_BYTES),
        cost_estimate=pl.CostEstimate(
            flops=2 * tokens * tall * right.shape[1], bytes_accessed=16 * 2**20, transcendentals=0
        ),
    )(where_am_i()[3].reshape(1), left, right, *filled)


def core_kernel(at_ref, keep_ref, got_ref, left_keep_ref, left_send_ref, right_keep_ref, right_send_ref):
    y_other, x_other = pl.program_id(0), pl.program_id(1)
    total = (keep_ref[0].astype(jnp.float32) + got_ref[0].astype(jnp.float32)).astype(jnp.bfloat16)
    left, right = total[:, : D // 2], total[:, D // 2 :]

    @pl.when(y_other == 0)
    def _():
        left_keep_ref[0, 0] = left

    @pl.when(y_other == 1)
    def _():
        left_send_ref[0, 0] = left

    @pl.when(x_other == 0)
    def _():
        right_keep_ref[0, 0] = right

    @pl.when(x_other == 1)
    def _():
        right_send_ref[0, 0] = right


def sum_core(keep, send):
    rows = keep.shape[1]
    got = trade(send, "fsdp", 1)
    y_at, _, x_at, _ = where_am_i()

    def chip(a, b, z, s):
        return (((a ^ s[0]) * 4 + z) * 2 + (b ^ s[1]), 0, 0)

    def left_keep(a, b, z, s):
        return (jnp.where(a == 0, z, 3), jnp.where(a == 0, b, 1) ^ s[1], 0, 0)

    def left_send(a, b, z, s):
        return (jnp.where(a == 1, z, 0), jnp.where(a == 1, b, 0) ^ s[1], 0, 0)

    def right_keep(a, b, z, s):
        return (a ^ s[0], jnp.where(b == 0, z, 3), 0, 0)

    def right_send(a, b, z, s):
        return (jnp.where(b == 1, a, 0) ^ s[0], jnp.where(b == 1, z, jnp.where(a == 0, 0, 3)), 0, 0)

    full = pl.BlockSpec((1, rows, D), chip)
    part = lambda index: pl.BlockSpec((1, 1, rows, D // 2), index)
    left = jax.ShapeDtypeStruct((4, 2, rows, D // 2), jnp.bfloat16)
    right = jax.ShapeDtypeStruct((2, 4, rows, D // 2), jnp.bfloat16)
    lk, ls, rk, rs = pl.pallas_call(
        core_kernel,
        grid_spec=pltpu.PrefetchScalarGridSpec(
            num_scalar_prefetch=1,
            grid=(2, 2, 4),
            in_specs=[full, full],
            out_specs=[part(left_keep), part(left_send), part(right_keep), part(right_send)],
        ),
        out_shape=[left, left, right, right],
        compiler_params=pltpu.CompilerParams(vmem_limit_bytes=VMEM_BYTES),
        cost_estimate=pl.CostEstimate(flops=10**9, bytes_accessed=96 * 2**10 * rows, transcendentals=0),
    )(jnp.stack([y_at, x_at]), keep, got)
    return (lk, rk), (ls, rs)


def sum_first(keep, send, after=0.0):
    y_at, _, x_at, _ = where_am_i()
    low, wide = jnp.bfloat16, jnp.float32
    left = keep[0].astype(wide) + trade(send[0], "seq", 1).astype(wide) + after
    right = keep[1].astype(wide) + trade(send[1], "fsdp", 2).astype(wide) + after
    left_keep, left_send = halves(left, 1, x_at)
    right_keep, right_send = halves(right, 0, y_at)
    return (left_keep, right_keep), (left_send.astype(low), right_send.astype(low))


def sum_second(keep, send, after=0.0):
    z_at = where_am_i()[1]
    left = keep[0] + trade(send[0], "fsdp", 2).astype(jnp.float32) + after
    right = keep[1] + trade(send[1], "seq", 1).astype(jnp.float32) + after
    total = jnp.concatenate([left, right], axis=-1)
    own = lax.dynamic_index_in_dim(total, z_at, 0, keepdims=False)
    sends = tuple(
        lax.dynamic_index_in_dim(total, z_at ^ other, 0, keepdims=False).astype(jnp.bfloat16) for other in (1, 2, 3)
    )
    return own, sends


def sum_last(keep, send):
    total = keep
    for other in (1, 2, 3):
        total = total + trade(send[other - 1], "fsdp", 4 * other).astype(jnp.float32)
    return total


def beside(total, height, starts):
    return jnp.concatenate([total[r : r + height] for r in starts], axis=1)


def plain_sum(left, right):
    grad = lax.dot_general(left, right, (((0,), (0,)), ((), ())), preferred_element_type=jnp.float32)
    return lax.psum_scatter(grad, ("seq", "fsdp"), scatter_dimension=0, tiled=True)


def adam_update(weight, moment_one, moment_two, grad, factor, step_float):
    grad = grad * factor
    moment_one = BETA_ONE * moment_one + (1.0 - BETA_ONE) * grad
    moment_two = BETA_TWO * moment_two + (1.0 - BETA_TWO) * grad * grad
    fix_one = 1.0 - BETA_ONE**step_float
    fix_two = 1.0 - BETA_TWO**step_float
    weight = weight - LEARN_RATE * (
        moment_one / fix_one / (jnp.sqrt(moment_two / fix_two) + ADAM_EPS) + WEIGHT_DECAY * weight
    )
    return (weight, moment_one, moment_two)


def body(
    token_ids,
    seq_lengths,
    pairing,
    step_count,
    embedding,
    embedding_one,
    embedding_two,
    qkv_weight,
    qkv_one,
    qkv_two,
    out_weight,
    out_one,
    out_two,
    gate_up_weight,
    gate_up_one,
    gate_up_two,
    down_weight,
    down_one,
    down_two,
    norm_gains,
    gains_one,
    gains_two,
    score_weight,
    score_one,
    score_two,
):
    seq_at = lax.axis_index("seq")
    group_at = lax.axis_index("fsdp")
    token_rows = token_ids.shape[1]
    per_group = seq_lengths.shape[1] - 1
    lengths = seq_lengths[0]
    bounds = jnp.stack([jnp.sum(lengths[: j + 1]) for j in range(per_group)])
    token_pos = seq_at * token_rows + jnp.arange(token_rows, dtype=jnp.int32)
    segment, begin = layout(bounds, token_pos)
    frequency = ROPE_THETA ** (
        -2.0 * jnp.arange(HEAD_SIZE // 2, dtype=jnp.float32) / HEAD_SIZE
    )
    angles = (token_pos - begin).astype(jnp.float32)[:, None] * frequency[None, :]
    cosine, sine = jnp.cos(angles), jnp.sin(angles)
    cosine = jnp.concatenate([cosine, cosine], axis=1)
    sine = jnp.concatenate([-sine, sine], axis=1)
    query_rows = min(512, token_rows)
    key_rows = min(512, token_rows)
    begin_column = begin[:, None]
    attn_gain = norm_gains[:D]
    mlp_gain = norm_gains[D : 2 * D]
    final_gain = norm_gains[2 * D : 3 * D]
    head_gains = norm_gains[3 * D :].reshape(2, HEAD_SIZE)
    first_own = seq_at * token_rows
    first_before = first_own - token_rows if lax.axis_size("seq") == 2 else 0 * first_own
    scalars = jnp.concatenate(
        [
            jnp.stack([first_own, first_before]),
            jnp.stack([begin[::query_rows], begin[query_rows - 1 :: query_rows]], axis=1).reshape(-1),
        ]
    )
    qkv_full = fetch(qkv_weight)
    out_full, gate_up_full, down_full = fetch(out_weight), fetch(gate_up_weight), fetch(down_weight)
    embedded, kept = embed_forward(token_ids, embedding)
    resid_in = embedded.astype(jnp.float32)
    normed_low = rms_norm(resid_in, attn_gain).astype(jnp.bfloat16)
    key_value_raw = jnp.dot(
        normed_low, qkv_full[:, QUERY_COLS:], preferred_element_type=jnp.float32
    ).astype(jnp.bfloat16)
    own_a, own_b = shape_keys(key_value_raw, cosine, sine, head_gains)
    before_a, before_b = tokens_before(own_a), tokens_before(own_b)
    query_raw = jnp.dot(
        normed_low, qkv_full[:, :QUERY_COLS], preferred_element_type=jnp.float32
    ).astype(jnp.bfloat16)
    query_low = shape_queries(query_raw, cosine, sine, head_gains)
    results = attention_forward(
        scalars, query_low, before_a, own_a, begin_column, query_rows, key_rows, 0, ()
    )
    merged, lse = attention_forward(
        scalars, query_low, before_b, own_b, begin_column, query_rows, key_rows, HALF, tuple(results)
    )
    resid_mid = resid_in + jnp.dot(merged, out_full, preferred_element_type=jnp.float32)
    normed_two = rms_norm(resid_mid, mlp_gain).astype(jnp.bfloat16)
    gate_up = jnp.dot(normed_two, gate_up_full, preferred_element_type=jnp.float32)
    activated = (jax.nn.silu(gate_up[:, :FF]) * gate_up[:, FF:]).astype(jnp.bfloat16)
    resid_out = resid_mid + jnp.dot(activated, down_full, preferred_element_type=jnp.float32)
    final = rms_norm(resid_out, final_gain)
    per_token = jnp.sum(final * score_weight, axis=1)
    slot_list = jnp.arange(per_group, dtype=jnp.int32)
    seq_size = seq_lengths[0, :per_group].astype(jnp.float32)
    picker = (segment[None, :] == slot_list[:, None]).astype(jnp.float32) / seq_size[:, None]
    own_scores = jnp.sum(picker * per_token[None, :], axis=1)
    seq_total = pairing.shape[0]
    score_board = lax.dynamic_update_slice(
        jnp.zeros((seq_total,), jnp.float32), own_scores, (group_at * per_group,)
    )
    all_scores = sum_small(score_board, 3)
    pair_table = pairing.reshape(-1, 2)
    seq_ids = jnp.arange(seq_total, dtype=jnp.int32)
    choose = (pair_table[:, 0:1] == seq_ids[None, :]).astype(jnp.float32)
    reject = (pair_table[:, 1:2] == seq_ids[None, :]).astype(jnp.float32)
    margin = jnp.sum((choose - reject) * all_scores[None, :], axis=1)
    ranking_loss = jnp.sum(jax.nn.softplus(-margin))
    margin_grad = -jax.nn.sigmoid(-margin)
    score_grads = jnp.sum(margin_grad[:, None] * (choose - reject), axis=0)
    own_grads = lax.dynamic_slice_in_dim(score_grads, group_at * per_group, per_group)
    token_grad = jnp.sum(own_grads[:, None] * picker, axis=0)
    score_part = jnp.sum(token_grad[:, None] * final, axis=0)
    final_grad = token_grad[:, None] * score_weight[None, :]
    final_back = jax.vjp(rms_norm, resid_out, final_gain)[1]
    dresid_out, dfinal_gain = final_back(final_grad)
    mlp_low = dresid_out.astype(jnp.bfloat16)
    staged = by_stages()
    if staged:
        early = gradient_blocks(activated, mlp_low, 768, lambda j: 0, 352, ())
    else:
        down_shard = plain_sum(activated, mlp_low)
    act_grad = jnp.dot(mlp_low, down_full.T, preferred_element_type=jnp.float32)
    act_back = jax.vjp(lambda joined: jax.nn.silu(joined[:, :FF]) * joined[:, FF:], gate_up)[1]
    gate_up_low = act_back(act_grad)[0].astype(jnp.bfloat16)
    if staged:
        early = gradient_blocks(
            normed_two, gate_up_low, 512, lambda j: jnp.where(j < 3, 3 + j, 5 + j), 352, tuple(early)
        )
    else:
        gate_up_shard = plain_sum(normed_two, gate_up_low)
    normed_two_grad = jnp.dot(gate_up_low, gate_up_full.T, preferred_element_type=jnp.float32)
    mid_back = jax.vjp(rms_norm, resid_mid, mlp_gain)[1]
    mid_extra, dmlp_gain = mid_back(normed_two_grad)
    dresid_mid = dresid_out + mid_extra
    attn_low = dresid_mid.astype(jnp.bfloat16)
    keep, send = (), ()
    if staged:
        early = gradient_blocks(merged, attn_low, 512, lambda j: 3, 352, tuple(early))
        keep, send = sum_core(*early)
    else:
        out_shard = plain_sum(merged, attn_low)
    merged_grad = jnp.dot(attn_low, out_full.T, preferred_element_type=jnp.float32).astype(
        jnp.bfloat16
    )
    common = (begin_column, merged_grad, merged, lse, query_rows, key_rows)
    query_grad, before_grad_a, own_grad_a = attention_backward(
        scalars, query_low, before_a, own_a, *common, 0, (), send
    )
    more_a = to_tokens_before(before_grad_a)
    if staged:
        keep, send = sum_first(keep, send)
    query_grad, before_grad_b, own_grad_b = attention_backward(
        scalars, query_low, before_b, own_b, *common, HALF, (query_grad,), send
    )
    more_b = to_tokens_before(before_grad_b)
    if staged:
        keep, send = sum_second(keep, send)
    query_raw_grad, query_sums = shape_back(
        queries_back_kernel, query_raw, cosine, sine, head_gains, (query_grad,), send
    )
    key_value_raw_grad, key_sums = shape_back(
        keys_back_kernel, key_value_raw, cosine, sine, head_gains, (own_grad_a, own_grad_b, more_a, more_b)
    )
    if staged:
        total = sum_last(keep, send)
        down_shard, out_shard = total[:96], total[192:256]
        gate_up_shard = beside(total, 32, (96, 128, 160, 256, 288, 320))
        late = gradient_blocks(normed_low, query_raw_grad, 512, lambda j: j, 128, ())
        late = gradient_blocks(normed_low, key_value_raw_grad, 512, lambda j: 2 + j, 128, tuple(late))
        keep, send = sum_core(*late)
    else:
        send = ()
        qkv_shard = jnp.concatenate(
            [plain_sum(normed_low, query_raw_grad), plain_sum(normed_low, key_value_raw_grad)], axis=1
        )
    normed_grad = jnp.dot(
        query_raw_grad, qkv_full[:, :QUERY_COLS].T, preferred_element_type=jnp.float32
    ) + jnp.dot(key_value_raw_grad, qkv_full[:, QUERY_COLS:].T, preferred_element_type=jnp.float32)
    in_back = jax.vjp(rms_norm, resid_in, attn_gain)[1]
    in_extra, dattn_gain = in_back(normed_grad)
    dresid_in = dresid_mid + in_extra
    token_grad_low = dresid_in.astype(jnp.bfloat16)
    arrived = embed_send(token_grad_low, kept, send)
    if staged:
        keep, send = sum_first(keep, send, arrived[0, 0, 0].astype(jnp.float32) * 0.0)
    embed_grad, square = embed_backward(token_grad_low, arrived, kept, embedding.shape[0], send)
    if staged:
        keep, send = sum_second(keep, send, square * 0.0)
        qkv_shard = beside(sum_last(keep, send), 32, (0, 32, 64, 96))
    shards = (qkv_shard, out_shard, gate_up_shard, down_shard)
    for shard in shards:
        square = square + jnp.sum(shard * shard)
    gain_part = jnp.concatenate([dattn_gain, dmlp_gain, dfinal_gain, query_sums[0], key_sums[0]])
    gain_count = gain_part.shape[0]
    sums = sum_small(jnp.concatenate([gain_part, score_part, square.reshape(1)]), 4)
    gain_sum, score_sum, square_sum = sums[:gain_count], sums[gain_count:-1], sums[-1]
    grad_norm = jnp.sqrt(square_sum + jnp.sum(gain_sum * gain_sum) + jnp.sum(score_sum * score_sum))
    factor = CLIP_NORM / jnp.maximum(grad_norm, CLIP_NORM)
    step_float = step_count[0]
    e_new = adam_update(embedding, embedding_one, embedding_two, embed_grad, factor, step_float)
    q_new = adam_update(qkv_weight, qkv_one, qkv_two, shards[0], factor, step_float)
    o_new = adam_update(out_weight, out_one, out_two, shards[1], factor, step_float)
    g_new = adam_update(gate_up_weight, gate_up_one, gate_up_two, shards[2], factor, step_float)
    d_new = adam_update(down_weight, down_one, down_two, shards[3], factor, step_float)
    n_new = adam_update(norm_gains, gains_one, gains_two, gain_sum, factor, step_float)
    s_new = adam_update(score_weight, score_one, score_two, score_sum, factor, step_float)
    clipped_gains = gain_sum * factor
    return (
        ranking_loss,
        grad_norm,
        e_new[0],
        e_new[1],
        e_new[2],
        q_new[0],
        q_new[1],
        q_new[2],
        o_new[0],
        o_new[1],
        o_new[2],
        g_new[0],
        g_new[1],
        g_new[2],
        d_new[0],
        d_new[1],
        d_new[2],
        clipped_gains,
        n_new[1],
        n_new[2],
        s_new[0],
        s_new[1],
        s_new[2],
    )


def solution(mesh):
    return jax.shard_map(
        body,
        mesh=mesh,
        in_specs=(
            P("fsdp", "seq"),
            P("fsdp", None),
            P(),
            P(),
            P("fsdp", "seq"),
            P("fsdp", "seq"),
            P("fsdp", "seq"),
            P(("seq", "fsdp"), None),
            P(("seq", "fsdp"), None),
            P(("seq", "fsdp"), None),
            P(("seq", "fsdp"), None),
            P(("seq", "fsdp"), None),
            P(("seq", "fsdp"), None),
            P(("seq", "fsdp"), None),
            P(("seq", "fsdp"), None),
            P(("seq", "fsdp"), None),
            P(("seq", "fsdp"), None),
            P(("seq", "fsdp"), None),
            P(("seq", "fsdp"), None),
            P(),
            P(),
            P(),
            P(),
            P(),
            P(),
        ),
        out_specs=(
            P(),
            P(),
            P("fsdp", "seq"),
            P("fsdp", "seq"),
            P("fsdp", "seq"),
            P(("seq", "fsdp"), None),
            P(("seq", "fsdp"), None),
            P(("seq", "fsdp"), None),
            P(("seq", "fsdp"), None),
            P(("seq", "fsdp"), None),
            P(("seq", "fsdp"), None),
            P(("seq", "fsdp"), None),
            P(("seq", "fsdp"), None),
            P(("seq", "fsdp"), None),
            P(("seq", "fsdp"), None),
            P(("seq", "fsdp"), None),
            P(("seq", "fsdp"), None),
            P(),
            P(),
            P(),
            P(),
            P(),
            P(),
        ),
        check_vma=False,
    )
```

time: 3070 us -> 1090 us (0.36)
  waiting for transfers between devices: 1090 us -> 215 us
  matrix products: 669 us -> 141 us
  other arithmetic: 654 us -> 164 us
  Pallas kernels: 0 us -> 436 us
  local copies, waits for them, and re-layouts: 382 us -> 52.1 us
  blocking collectives: 174 us -> 0 us
    unnamed x11 -> x4, waiting for transfers between devices: 645 us -> 0.07 us
    dot_general x42 -> x8, matrix products: 570 us -> 44.6 us  [the longest x1 10.1 us: body(): jnp.dot(key_value_raw_grad, qkv_full[:, QUERY_COLS:].T, preferred_element...]
    pallas_call x0 -> x21, Pallas kernels: none -> 436 us  [the longest x5 174 us: exchange(): pl.pallas_call(functools.partial(exchange_kernel, n_seq, n_fsdp, to_all),...]
    reduce_scatter x4 -> x0, waiting for transfers between devices: 231 us -> none  [the longest x1 231 us: reduce_grads(): lax.psum_scatter(pieces[0], ('seq', 'fsdp'), scatter_dimension=0, tiled=T...]
    scatter-add x1 -> x0, other arithmetic: 227 us -> none  [embed_backward(): jax.ops.segment_sum(rows_in, target, num_segments=height + 1)[:height]]
    all_to_all x9 -> x0, waiting for transfers between devices: 217 us -> none  [the longest x1 44.6 us: body(): lax.all_to_all(attended.astype(jnp.bfloat16), 'seq', split_axis=0, concat...]
    ppermute x0 -> x20, waiting for transfers between devices: none -> 185 us  [the longest x16 89.1 us: trade(): return lax.ppermute(values, axis, [(i, i ^ bit) for i in range(count)])]
    gather x2 -> x1, local copies, waits for them, and re-layouts: 180 us -> 14.5 us  [pick_rows(): rows = jnp.take(table, jnp.maximum(wanted, 0).reshape(-1), axis=0)]
  transfers between devices with their start and end apart: 19 -> 24, of which waited for: 10 -> 9; matrix products, arithmetic and copies ran while one was open for 35% -> 17% of each run, Pallas kernels for 0% -> 31%
where the time goes in v1:
time: 1090 us; the launch traced here: 1080 us
  Pallas kernels  436 us (40%)
  waiting for transfers between devices  215 us (20%)
  other arithmetic  164 us (15%)
  matrix products  141 us (13%)
  local copies, waits for them, and re-layouts  52.1 us (5%)
  starting transfers between devices  30.2 us (3%)
  between operations  25.6 us (2%)
  loops' own time  12.2 us (1%)
    pallas_call x5, Pallas kernels, exchange(): pl.pallas_call(functools.partial(exchange_kernel, n_seq, n_fsdp, to_all),...  174 us
    ppermute x16, waiting for transfers between devices, trade(): return lax.ppermute(values, axis, [(i, i ^ bit) for i in range(count)])  89.1 us
    ppermute x2, waiting for transfers between devices, tokens_before(): return lax.ppermute(own, 'seq', [(0, 1), (1, 0)])  88.8 us
    pallas_call x2, Pallas kernels, attention_backward(): pl.pallas_call(functools.partial(backward_kernel, keys), grid_spec=pltpu....  66.2 us
    pallas_call x5, Pallas kernels, gradient_blocks(): pl.pallas_call(functools.partial(gradient_kernel, height), grid_spec=pltp...  62 us
    sub x6, other arithmetic, adam_update(): weight - LEARN_RATE * (moment_one / fix_one / (jnp.sqrt(moment_two / fix_...  56.4 us
    pallas_call x2, Pallas kernels, sum_core(): pl.pallas_call(core_kernel, grid_spec=pltpu.PrefetchScalarGridSpec(num_sc...  32.1 us
    pallas_call x2, Pallas kernels, shape_back(): pl.pallas_call(kernel, grid=(tokens // rows,), in_specs=[token_blocks(row...  30.6 us
  transfers between devices with their start and end apart: 24, of which 9 were waited for; matrix products, arithmetic and copies ran while one was open for 17% of the time, Pallas kernels for 31%

profile of v1, /device:TPU:0, one launch (start us, length us, event | category | flops | bytes accessed | tf_op | source)
XLA Modules:
  0.0 1075.7 jit_solution(3267893996986436248)
XLA Ops:
  10.8 1.9 convert_element_type.249
  15.4 2.3 convert_reduce_fusion.2
  24.7 12.9 %shard_map.416 = s32[32,8,128]{2,1,0:T(8,128)} custom-call(s32[32,8,128]{2,1,0:T(8,128)} %pad_add_fusion.2.x_ref), custom_call_target="tpu_custom_call" | custom-call | tf_op jit(solution)/shard_map/pallas_call | solution.py:98
  40.8 14.5 %gather_fusion.1 = bf16[2560,512]{1,0:T(8,128)(2,1)S(1)} fusion(f32[9496,512]{1,0:T(8,128)} %param.45, s32[3072]{0:T(1024)S(1)} %pad_clamp_fusion.1), kind=kCustom, calls=%fused_computation.1 | custom fusion | bytes 5253120 | tf_op jit(solution)/shard_map/jit(_take)/gather | solution.py:147
  55.4 2.4 broadcast_select_fusion.1
  57.8 76.2 %shard_map.417 = bf16[32,80,512]{2,1,0:T(8,128)(2,1)S(1)} custom-call(bf16[32,80,512]{2,1,0:T(8,128)(2,1)} %bitcast.165), custom_call_target="tpu_custom_call" | custom-call | tf_op jit(solution)/shard_map/pallas_call | solution.py:98
  134.0 12.0 %conditional.2 = (bf16[1024,1024]{0,1:T(8,128)(2,1)}) conditional(s32[]{:T(128)} %convert_element_type.239, (s32[1024]{0:T(1024)S(1)}, bf16[32,80,512]{2,1,0:T(8,128)(2,1)S(1)}, s32[]{:T(128)}, s32[1024]{0:T(1024)S(1)}, s32[1024]{0:T(1024)S(1)}, /*index=5*/s32[1024]{0:T(1024)S(1)}, f32[9496,512]{1,0:T(8,128)}) %tuple.144, (s32[1024]{0:T(1024)S(1)}, ...), branch_computations={%region_10.14_spmd, %region_14.15_spmd} | conditional | flops 5396661248 | bytes 153264544 | solution.py:214
  146.0 2.9 copy.101
  160.0 9.3 convolution_convert_fusion.1.raw_ref
  169.3 7.5 shard_map.419
  181.9 9.3 convolution_convert_fusion.2.raw_ref
  191.2 11.8 %shard_map.418.q_ref = bf16[1024,2048]{1,0:T(8,128)(2,1)} custom-call(bf16[1024,2048]{1,0:T(8,128)(2,1)} %convolution_convert_fusion.2.raw_ref, f32[1024,128]{1,0:T(8,128)} %get-tuple-element.397.cos_ref, f32[1024,128]{1,0:T(8,128)} %get-tuple-element.398.sin_ref, f32[2,128]{1,0:T(2,128)} %slice_bitcast_fusion.gain_ref), custom_call_target="tpu_custom_call" | custom-call | flops 4000000000 | bytes 8388608 | tf_op jit(solution)/shard_map/pallas_call | solution.py:385
  203.0 32.6 %collective-permute-done.1.kb_ref.vb_ref = bf16[1024,1024]{1,0:T(8,128)(2,1)} collective-permute-done((bf16[1024,1024]{1,0:T(8,128)(2,1)}, bf16[1024,1024]{1,0:T(8,128)(2,1)}, u32[]{:S(2)}, u32[]{:S(2)}) %collective-permute-start.1) | collective-permute-done | bytes 2097184 | tf_op jit(solution)/shard_map/ppermute | solution.py:689
  235.6 15.2 %shard_map.420 = (bf16[1024,2048]{1,0:T(8,128)(2,1)}, f32[8,1024,2]{2,1,0:T(8,128)}) custom-call(s32[6]{0:T(128)} %pad_add_fusion.6.scalar_ref, bf16[1024,2048]{1,0:T(8,128)(2,1)} %shard_map.418.q_ref, bf16[1024,1024]{1,0:T(8,128)(2,1)} %collective-permute-done.1.kb_ref.vb_ref, bf16[1024,1024]{1,0:T(8,128)(2,1)} %collective-permute-done.1.kb_ref.vb_ref, ...), custom_call_target="tpu_custom_call" | custom-call | flops 20000000000 | bytes 16777216 | tf_op jit(solution)/shard_map/pallas_call | solution.py:584
  250.8 56.2 %collective-permute-done.kb_ref.vb_ref = bf16[1024,1024]{1,0:T(8,128)(2,1)S(1)} collective-permute-done((bf16[1024,1024]{1,0:T(8,128)(2,1)}, bf16[1024,1024]{1,0:T(8,128)(2,1)S(1)}, u32[]{:S(2)}, u32[]{:S(2)}) %collective-permute-start) | collective-permute-done | bytes 2097184 | tf_op jit(solution)/shard_map/ppermute | solution.py:689
  308.3 15.4 %shard_map.421 = (bf16[1024,2048]{1,0:T(8,128)(2,1)}, f32[8,1024,2]{2,1,0:T(8,128)}) custom-call(s32[6]{0:T(128)} %pad_add_fusion.6.scalar_ref, bf16[1024,2048]{1,0:T(8,128)(2,1)} %shard_map.418.q_ref, bf16[1024,1024]{1,0:T(8,128)(2,1)} %copy-done.59, bf16[1024,1024]{1,0:T(8,128)(2,1)} %copy-done.59, ...), custom_call_target="tpu_custom_call", output_to_operand_aliasing={{0}: (7, {}), {1}: (8, {})} | custom-call | flops 20000000000 | bytes 16777216 | tf_op jit(solution)/shard_map/pallas_call | solution.py:584
  323.7 7.9 multiply_reduce_fusion.6
  331.6 2.0 copy-done.10
  334.0 21.5 %fusion.130 = f32[1024,6144]{1,0:T(8,128)} fusion(bf16[1024,1024]{1,0:T(8,128)(2,1)S(1)} %multiply_convert_fusion.1.left_ref, bf16[1024,6144]{1,0:T(8,128)(2,1)} %all-gather.9.cloned.1.call-done), kind=kOutput, calls=%fused_computation.313 | convolution fusion | flops 12884901888 | bytes 39845888 | tf_op jit(solution)/shard_map/dot_general | solution.py:957
  355.6 12.8 %multiply_convert_fusion.left_ref = bf16[1024,3072]{1,0:T(8,128)(2,1)} fusion(f32[1024,6144]{1,0:T(8,128)} %fusion.130), kind=kLoop, calls=%fused_computation.67 | loop fusion | flops 18874368 | bytes 31457280 | tf_op jit(solution)/shard_map/convert_element_type | solution.py:958
  368.4 30.0 %all-gather.11.cloned.1.call-done = bf16[3072,1024]{1,0:T(8,128)(2,1)} async-done(((bf16[96,1024]{1,0:T(8,128)(2,1)}), bf16[3072,1024]{1,0:T(8,128)(2,1)}) %all-gather.11.cloned.1.call-update) | async-done | bytes 6291472 | tf_op jit(solution)/shard_map/all_gather | solution.py:699
  398.5 11.4 %multiply_reduce_fusion.5 = (f32[1024]{0:T(1024)S(1)}, f32[1024,1024]{1,0:T(8,128)S(1)}) fusion(f32[1024,1024]{1,0:T(8,128)} %copy-done.10, bf16[1024,3072]{1,0:T(8,128)(2,1)} %multiply_convert_fusion.left_ref, bf16[3072,1024]{1,0:T(8,128)(2,1)} %all-gather.11.cloned.1.call-done), kind=kOutput, calls=%fused_computation.112 | convolution fusion | flops 6445595648 | bytes 20975616 | tf_op jit(solution)/shard_map/dot_general | solution.py:959
  409.9 2.0 copy-done.2
  413.7 9.6 shard_map.422
  425.3 4.2 multiply_reduce_fusion.1
  430.6 25.7 %fusion.77 = (f32[1024,3072]{1,0:T(8,128)}, f32[1024,3072]{1,0:T(8,128)}) fusion(f32[1024,6144]{1,0:T(8,128)} %fusion.130, bf16[1024,1024]{1,0:T(8,128)(2,1)S(1)} %fusion.58.right_ref, bf16[3072,1024]{1,0:T(8,128)(2,1)} %all-gather.11.cloned.1.call-done), kind=kOutput, calls=%fused_computation.164 | convolution fusion | flops 6480199680 | bytes 58720256 | tf_op jit(solution)/shard_map/dot_general | solution.py:991
  456.4 13.4 %add_convert_fusion.right_ref = bf16[1024,6144]{1,0:T(8,128)(2,1)} fusion(f32[1024,3072]{1,0:T(8,128)} %get-tuple-element.364, f32[1024,3072]{1,0:T(8,128)} %get-tuple-element.363), kind=kLoop, calls=%fused_computation.60 | loop fusion | flops 12582912 | bytes 37748736 | tf_op jit(solution)/shard_map/convert_element_type | solution.py:993
  469.8 21.4 %multiply_reduce_fusion.2 = (f32[1024]{0:T(1024)}, f32[1024]{0:T(1024)S(1)}, f32[1024,1024]{1,0:T(8,128)}) fusion(f32[1024,1024]{1,0:T(8,128)S(1)} %copy-done.11, f32[1024]{0:T(1024)S(1)} %fusion.112, f32[1024]{0:T(1024)S(1)} %get-tuple-element.379, bf16[1024,6144]{1,0:T(8,128)(2,1)} %add_convert_fusion.right_ref, ...), kind=kOutput, calls=%fused_computation.109 | convolution fusion | flops 12891191296 | bytes 33570816 | tf_op jit(solution)/shard_map/dot_general | solution.py:1000
  491.1 10.7 shard_map.423
  501.9 6.1 fusion.122
  508.0 23.1 %shard_map.424 = (bf16[16,352,1024]{2,1,0:T(8,128)(2,1)}, bf16[16,352,1024]{2,1,0:T(8,128)(2,1)}) custom-call(s32[1]{0:T(128)} %bitcast.31.core_ref, bf16[1024,1024]{1,0:T(8,128)(2,1)} %copy-done.21, bf16[1024,6144]{1,0:T(8,128)(2,1)} %add_convert_fusion.right_ref, ...), custom_call_target="tpu_custom_call", output_to_operand_aliasing={{0}: (3, {}), {1}: (4, {})} | custom-call | flops 12884901888 | bytes 16777216 | tf_op jit(solution)/shard_map/pallas_call | solution.py:745
  531.1 8.6 shard_map.425
  540.4 8.7 convolution_convert_fusion.do_ref
  549.1 8.6 collective-permute-done.2.got_ref
  557.7 19.6 %shard_map.426 = (bf16[4,2,352,512]{3,2,1,0:T(8,128)(2,1)}, bf16[4,2,352,512]{3,2,1,0:T(8,128)(2,1)}, bf16[2,4,352,512]{3,2,1,0:T(8,128)(2,1)}, bf16[2,4,352,512]{3,2,1,0:T(8,128)(2,1)}) custom-call(s32[2]{0:T(128)} %pad_add_fusion.7.at_ref, bf16[16,352,1024]{2,1,0:T(8,128)(2,1)} %get-tuple-element.266.keep_ref, ...), custom_call_target="tpu_custom_call" | custom-call | flops 1000000000 | bytes 34603008 | tf_op jit(solution)/shard_map/pallas_call | solution.py:813
  577.4 2.0 copy.109
  581.5 33.1 %shard_map.427 = (f32[1024,2048]{1,0:T(8,128)}, bf16[2,1024,512]{2,1,0:T(8,128)(2,1)}, f32[2,1024,512]{2,1,0:T(8,128)}) custom-call(s32[6]{0:T(128)} %pad_add_fusion.6.scalar_ref, bf16[1024,2048]{1,0:T(8,128)(2,1)} %shard_map.418.q_ref, bf16[1024,1024]{1,0:T(8,128)(2,1)} %collective-permute-done.1.kb_ref.vb_ref, ...), custom_call_target="tpu_custom_call" | custom-call | flops 40000000000 | bytes 41943040 | tf_op jit(solution)/shard_map/pallas_call | solution.py:657
  614.7 29.9 %collective-permute-done.4 = bf16[2,4,352,512]{3,2,1,0:T(8,128)(2,1)} collective-permute-done((bf16[2,4,352,512]{3,2,1,0:T(8,128)(2,1)}, bf16[2,4,352,512]{3,2,1,0:T(8,128)(2,1)}, u32[]{:S(2)}, u32[]{:S(2)}) %collective-permute-start.4) | collective-permute-done | bytes 2883616 | tf_op jit(solution)/shard_map/ppermute | solution.py:704
  644.6 3.6 convert_add_fusion.1
  657.4 33.0 %shard_map.428 = (f32[1024,2048]{1,0:T(8,128)}, bf16[2,1024,512]{2,1,0:T(8,128)(2,1)}, f32[2,1024,512]{2,1,0:T(8,128)}) custom-call(s32[6]{0:T(128)} %pad_add_fusion.6.scalar_ref, bf16[1024,2048]{1,0:T(8,128)(2,1)} %shard_map.418.q_ref, bf16[1024,1024]{1,0:T(8,128)(2,1)} %copy-done.59, ...), custom_call_target="tpu_custom_call", output_to_operand_aliasing={{0}: (10, {})} | custom-call | flops 40000000000 | bytes 41943040 | tf_op jit(solution)/shard_map/pallas_call | solution.py:657
  691.2 29.4 %collective-permute-done.6 = bf16[4,352,512]{2,1,0:T(8,128)(2,1)S(1)} collective-permute-done((bf16[4,352,512]{2,1,0:T(8,128)(2,1)}, bf16[4,352,512]{2,1,0:T(8,128)(2,1)S(1)}, u32[]{:S(2)}, u32[]{:S(2)}) %collective-permute-start.6) | collective-permute-done | bytes 1441824 | tf_op jit(solution)/shard_map/ppermute | solution.py:704
  720.6 2.3 bitcast_add_fusion
  726.3 2.0 collective-permute-start.19
  728.6 2.0 collective-permute-start.17
  730.7 17.6 %shard_map.429 = (bf16[1024,2048]{1,0:T(8,128)(2,1)}, f32[8,128]{1,0:T(8,128)}) custom-call(bf16[1024,2048]{1,0:T(8,128)(2,1)} %convolution_convert_fusion.2.raw_ref, f32[1024,128]{1,0:T(8,128)} %get-tuple-element.397.cos_ref, f32[1024,128]{1,0:T(8,128)} %get-tuple-element.398.sin_ref, f32[2,128]{1,0:T(2,128)} %slice_bitcast_fusion.gain_ref, ...), custom_call_target="tpu_custom_call" | custom-call | flops 5000000000 | bytes 20971520 | tf_op jit(solution)/shard_map/pallas_call | solution.py:463
  748.3 9.8 shard_map.431
  758.0 6.8 collective-permute-done.8.more_b_ref
  764.9 13.0 %shard_map.430 = (bf16[1024,2048]{1,0:T(8,128)(2,1)}, f32[8,128]{1,0:T(8,128)}) custom-call(bf16[1024,2048]{1,0:T(8,128)(2,1)} %convolution_convert_fusion.1.raw_ref, f32[1024,128]{1,0:T(8,128)} %get-tuple-element.397.cos_ref, f32[1024,128]{1,0:T(8,128)} %get-tuple-element.398.sin_ref, f32[2,128]{1,0:T(2,128)} %slice_bitcast_fusion.gain_ref, ...), custom_call_target="tpu_custom_call" | custom-call | flops 5000000000 | bytes 20971520 | tf_op jit(solution)/shard_map/pallas_call | solution.py:463
  777.9 9.8 shard_map.432
  787.8 10.1 fusion.50
  798.0 8.6 fusion.47
  822.2 12.4 %shard_map.433 = (bf16[4,2,128,512]{3,2,1,0:T(8,128)(2,1)}, bf16[4,2,128,512]{3,2,1,0:T(8,128)(2,1)}, bf16[2,4,128,512]{3,2,1,0:T(8,128)(2,1)}, bf16[2,4,128,512]{3,2,1,0:T(8,128)(2,1)}) custom-call(s32[2]{0:T(128)} %pad_add_fusion.7.at_ref, bf16[16,128,1024]{2,1,0:T(8,128)(2,1)} %get-tuple-element.284.keep_ref, ...), custom_call_target="tpu_custom_call" | custom-call | flops 1000000000 | bytes 12582912 | tf_op jit(solution)/shard_map/pallas_call | solution.py:813
  834.6 2.3 copy.112
  839.1 57.7 %shard_map.434 = bf16[32,80,512]{2,1,0:T(8,128)(2,1)} custom-call(bf16[32,80,512]{2,1,0:T(8,128)(2,1)} %pad_maximum_fusion.3.x_ref, bf16[4,2,128,512]{3,2,1,0:T(8,128)(2,1)} %get-tuple-element.286.refs_0_, bf16[2,4,128,512]{3,2,1,0:T(8,128)(2,1)} %get-tuple-element.287.refs_1_), custom_call_target="tpu_custom_call" | custom-call | tf_op jit(solution)/shard_map/pallas_call | solution.py:98
  901.6 5.0 collective-permute-start.12
  911.0 29.1 %conditional.3 = (f32[9496,512]{1,0:T(8,128)}, f32[]{:T(128)}) conditional(s32[]{:T(128)} %convert_element_type.239, (s32[32,80]{1,0:T(8,128)S(1)}, bf16[32,80,512]{2,1,0:T(8,128)(2,1)}, bf16[4,128,512]{2,1,0:T(8,128)(2,1)}, bf16[4,128,512]{2,1,0:T(8,128)(2,1)}, s32[]{:T(128)}, /*index=5*/s32[1024]{0:T(1024)S(1)}, s32[1024]{0:T(1024)S(1)}, ...), branch_computations={%region_33.40_spmd, %region_40.43_spmd} | conditional | flops 3705905920 | bytes 151820720 | solution.py:328
  917.8 21.1 %branch_1_fun.1 = (f32[9496,512]{1,0:T(8,128)}, f32[8,512]{1,0:T(8,128)}) custom-call(s32[2560]{0:T(1024)} %reshape.548.wanted_ref, s32[32]{0:T(128)} %convert_reduce_fusion.count_ref, bf16[32,80,512]{2,1,0:T(8,128)(2,1)} %get-tuple-element.192.arrived_ref, bf16[4,128,512]{2,1,0:T(8,128)(2,1)} %get-tuple-element.193.refs_0_, ...), custom_call_target="tpu_custom_call" | custom-call | flops 1000000000 | bytes 83886080 | tf_op jit(solution)/shard_map/cond/branch_1_fun/pallas_call | solution.py:280
  944.2 9.5 collective-permute-start.16
  955.8 3.1 collective-permute-done.16
  958.9 18.1 %collective-permute-done.15 = bf16[128,1024]{1,0:T(8,128)(2,1)S(1)} collective-permute-done((bf16[128,1024]{1,0:T(8,128)(2,1)S(1)}, bf16[128,1024]{1,0:T(8,128)(2,1)S(1)}, u32[]{:S(2)}, u32[]{:S(2)}) %collective-permute-start.15) | collective-permute-done | bytes 262176 | tf_op jit(solution)/shard_map/ppermute | solution.py:704
  983.8 17.8 %shard_map.435 = f32[32,40,128]{2,1,0:T(8,128)} custom-call(f32[40,128]{1,0:T(8,128)} %pad_bitcast_fusion.x_ref), custom_call_target="tpu_custom_call" | custom-call | tf_op jit(solution)/shard_map/pallas_call | solution.py:98
  1010.7 2.7 multiply_subtract_fusion.4
  1013.5 2.2 multiply_subtract_fusion.6
  1020.6 47.2 %multiply_subtract_fusion.2 = (f32[9496,512]{1,0:T(8,128)}, f32[9496,512]{1,0:T(8,128)}, f32[9496,512]{1,0:T(8,128)}) fusion(f32[9496,512]{1,0:T(8,128)} %param.45, f32[]{:T(128)} %bitcast.58, f32[]{:T(128)} %bitcast.57, f32[9496,512]{1,0:T(8,128)} %get-tuple-element.291, f32[]{:T(128)S(6)} %div.181, f32[9496,512]{1,0:T(8,128)} %param.47, f32[9496,512]{1,0:T(8,128)} %param.46), kind=kLoop, calls=%fused_computation.62 | loop fusion | flops 77791232 | bytes 136134672 | tf_op jit(solution)/shard_map/sub | solution.py:872
  (279 shorter events, 108.2 us)
Async XLA Ops:
  7.2 152.8 %all-gather.5.cloned.1.call-start = ((), (), s32[]{:S(2)}) async-start(), calls=%async_computation.4 | async-start | bytes 8650752 | tf_op jit(solution)/shard_map/all_gather | solution.py:699
  9.0 314.6 %all-gather.7.cloned.1.call-start = ((), (), s32[]{:S(2)}) async-start(), calls=%async_computation.5 | async-start | bytes 4325376 | tf_op jit(solution)/shard_map/all_gather | solution.py:699
  10.7 323.3 %all-gather.9.cloned.1.call-start = ((), (), s32[]{:S(2)}) async-start(), calls=%async_computation.6 | async-start | bytes 12976128 | tf_op jit(solution)/shard_map/all_gather | solution.py:699
  12.7 385.7 %all-gather.11.cloned.1.call-start = ((), (), s32[]{:S(2)}) async-start(), calls=%async_computation.7 | async-start | bytes 6488064 | tf_op jit(solution)/shard_map/all_gather | solution.py:699
  15.4 118.5 %copy-start.34 = (s32[1024]{0:T(1024)}, s32[1024]{0:T(1024)S(1)}, u32[]{:S(2)}) copy-start(s32[1024]{0:T(1024)S(1)} %get-tuple-element.383) | copy-start | bytes 12292
  17.7 116.3 %copy-start.32 = (s32[1024]{0:T(1024)}, s32[1024]{0:T(1024)S(1)}, u32[]{:S(2)}) copy-start(s32[1024]{0:T(1024)S(1)} %convert_reduce_fusion.2) | copy-start | bytes 12292
  22.6 111.4 %copy-start.52 = (s32[1024]{0:T(1024)}, s32[1024]{0:T(1024)S(1)}, u32[]{:S(2)}) copy-start(s32[1024]{0:T(1024)S(1)} %get-tuple-element.385) | copy-start | bytes 12292
  55.4 78.6 %copy-start.26 = (s32[1,1024]{1,0:T(1,128)S(1)}, s32[1,1024]{1,0:T(1,128)}, u32[]{:S(2)}) copy-start(s32[1,1024]{1,0:T(1,128)} %param.41) | copy-start | bytes 12292
  146.0 10.5 copy-start.51
  148.9 174.8 %copy-start.4 = (bf16[1024,1024]{1,0:T(8,128)(2,1)}, bf16[1024,1024]{1,0:T(8,128)(2,1)S(1)}, u32[]{:S(2)}) copy-start(bf16[1024,1024]{1,0:T(8,128)(2,1)S(1)} %copy.101) | copy-start | bytes 6291460
  158.1 11.2 %copy-start.42 = (f32[1024]{0:T(1024)}, f32[1024]{0:T(1024)S(1)}, u32[]{:S(2)}) copy-start(f32[1024]{0:T(1024)S(1)} %fusion.111) | copy-start | bytes 12292
  158.1 11.2 %copy-start.44 = (f32[1024]{0:T(1024)}, f32[1024]{0:T(1024)S(1)}, u32[]{:S(2)}) copy-start(f32[1024]{0:T(1024)S(1)} %get-tuple-element.378) | copy-start | bytes 12292
  169.3 8.7 copy-start.23
  169.3 10.8 %copy-start.58 = (s32[48]{0:T(128)S(1)}, s32[48]{0:T(128)}, u32[]{:S(2)}) copy-start(s32[48]{0:T(128)} %param.43) | copy-start | bytes 580
  176.8 58.8 %collective-permute-start.1 = (bf16[1024,1024]{1,0:T(8,128)(2,1)}, bf16[1024,1024]{1,0:T(8,128)(2,1)}, u32[]{:S(2)}, u32[]{:S(2)}) collective-permute-start(bf16[1024,1024]{1,0:T(8,128)(2,1)} %get-tuple-element.257.k_ref.v_ref), channel_id=1, source_target_pairs={{0,16},{16,0},{1,17},{17,1},{2,18},{18,2},{3,19},{19,3},{4,20},{20... | collective-permute-start | bytes 6291464 | tf_op jit(solution)/shard_map/ppermute | solution.py:689
  181.0 125.9 %collective-permute-start = (bf16[1024,1024]{1,0:T(8,128)(2,1)}, bf16[1024,1024]{1,0:T(8,128)(2,1)S(1)}, u32[]{:S(2)}, u32[]{:S(2)}) collective-permute-start(bf16[1024,1024]{1,0:T(8,128)(2,1)} %get-tuple-element.256.k_ref.v_ref), channel_id=1, source_target_pairs={{0,16},{16,0},{1,17},{17,1},{2,18},{18,2},{3,19},{19,3},{4,20},{20... | collective-permute-start | bytes 6291464 | tf_op jit(solution)/shard_map/ppermute | solution.py:689
  334.0 21.6 %copy-start.21 = (bf16[1024,1024]{1,0:T(8,128)(2,1)}, bf16[1024,1024]{1,0:T(8,128)(2,1)S(1)}, u32[]{:S(2)}) copy-start(bf16[1024,1024]{1,0:T(8,128)(2,1)S(1)} %multiply_convert_fusion.1.left_ref) | copy-start | bytes 6291460
  368.4 43.4 %copy-start.39 = (f32[1024]{0:T(1024)S(1)}, f32[1024]{0:T(1024)}, u32[]{:S(2)}) copy-start(f32[1024]{0:T(1024)} %param.63) | copy-start | bytes 12292
  424.2 5.3 copy-start.3
  430.6 25.7 %copy-start.22 = (bf16[1024,1024]{1,0:T(8,128)(2,1)}, bf16[1024,1024]{1,0:T(8,128)(2,1)S(1)}, u32[]{:S(2)}) copy-start(bf16[1024,1024]{1,0:T(8,128)(2,1)S(1)} %fusion.58.right_ref) | copy-start | bytes 6291460
  456.4 13.4 %copy-start.11 = (f32[1024,1024]{1,0:T(8,128)S(1)}, f32[1024,1024]{1,0:T(8,128)}, u32[]{:S(2)}) copy-start(f32[1024,1024]{1,0:T(8,128)} %copy-done.10) | copy-start | bytes 12582916
  531.1 9.3 copy-start.14
  539.7 18.0 %collective-permute-start.2 = (bf16[16,352,1024]{2,1,0:T(8,128)(2,1)}, bf16[16,352,1024]{2,1,0:T(8,128)(2,1)}, u32[]{:S(2)}, u32[]{:S(2)}) collective-permute-start(bf16[16,352,1024]{2,1,0:T(8,128)(2,1)} %get-tuple-element.267), channel_id=1, source_target_pairs={{0,1},{1,0},{2,3},{3,2},{4,5},{5,4},{6,7},{7,6},{8,9},{9,8},{10,11... | collective-permute-start | bytes 34603016 | tf_op jit(solution)/shard_map/ppermute | solution.py:704
  579.4 71.6 %collective-permute-start.3 = (bf16[4,2,352,512]{3,2,0,1:T(8,128)(2,1)S(1)}, bf16[4,2,352,512]{3,2,0,1:T(8,128)(2,1)S(1)}, u32[]{:S(2)}, u32[]{:S(2)}) collective-permute-start(bf16[4,2,352,512]{3,2,0,1:T(8,128)(2,1)S(1)} %copy.109), channel_id=1, source_target_pairs={{0,16},{16,0},{1,17},{17,1},{2,18},{18,2},{3,19},{19,3},{4,20},{20... | collective-permute-start | bytes 8650760 | tf_op jit(solution)/shard_map/ppermute | solution.py:704
  580.0 64.6 %collective-permute-start.4 = (bf16[2,4,352,512]{3,2,1,0:T(8,128)(2,1)}, bf16[2,4,352,512]{3,2,1,0:T(8,128)(2,1)}, u32[]{:S(2)}, u32[]{:S(2)}) collective-permute-start(bf16[2,4,352,512]{3,2,1,0:T(8,128)(2,1)} %get-tuple-element.269.refs_1_), channel_id=1, source_target_pairs={{0,2},{1,3},{2,0},{3,1},{4,6},{5,7},{6,4},{7,5},{8,10},{9,11},{10,... | collective-permute-start | bytes 8650760 | tf_op jit(solution)/shard_map/ppermute | solution.py:704
  614.6 143.4 %collective-permute-start.7 = (bf16[2,1024,512]{2,1,0:T(8,128)(2,1)}, bf16[2,1024,512]{2,1,0:T(8,128)(2,1)}, u32[]{:S(2)}, u32[]{:S(2)}) collective-permute-start(bf16[2,1024,512]{2,1,0:T(8,128)(2,1)} %get-tuple-element.277), channel_id=1, source_target_pairs={{0,16},{16,0},{1,17},{17,1},{2,18},{18,2},{3,19},{19,3},{4,20},{20... | collective-permute-start | bytes 6291464 | tf_op jit(solution)/shard_map/ppermute | solution.py:695
  648.2 4.8 copy-start.6
  649.5 71.1 %collective-permute-start.6 = (bf16[4,352,512]{2,1,0:T(8,128)(2,1)}, bf16[4,352,512]{2,1,0:T(8,128)(2,1)S(1)}, u32[]{:S(2)}, u32[]{:S(2)}) collective-permute-start(bf16[4,352,512]{2,1,0:T(8,128)(2,1)} %fusion.65.refs_2_), channel_id=1, source_target_pairs={{0,16},{16,0},{1,17},{17,1},{2,18},{18,2},{3,19},{19,3},{4,20},{20... | collective-permute-start | bytes 4325384 | tf_op jit(solution)/shard_map/ppermute | solution.py:704
  656.0 67.0 %collective-permute-start.5 = (bf16[4,352,512]{2,1,0:T(8,128)(2,1)}, bf16[4,352,512]{2,1,0:T(8,128)(2,1)}, u32[]{:S(2)}, u32[]{:S(2)}) collective-permute-start(bf16[4,352,512]{2,1,0:T(8,128)(2,1)} %fusion.64.refs_1_), channel_id=1, source_target_pairs={{0,2},{1,3},{2,0},{3,1},{4,6},{5,7},{6,4},{7,5},{8,10},{9,11},{10,... | collective-permute-start | bytes 4325384 | tf_op jit(solution)/shard_map/ppermute | solution.py:704
  690.4 74.4 %collective-permute-start.8 = (bf16[2,1024,512]{2,1,0:T(8,128)(2,1)}, bf16[2,1024,512]{2,1,0:T(8,128)(2,1)}, u32[]{:S(2)}, u32[]{:S(2)}) collective-permute-start(bf16[2,1024,512]{2,1,0:T(8,128)(2,1)} %get-tuple-element.278), channel_id=1, source_target_pairs={{0,16},{16,0},{1,17},{17,1},{2,18},{18,2},{3,19},{19,3},{4,20},{20... | collective-permute-start | bytes 6291464 | tf_op jit(solution)/shard_map/ppermute | solution.py:695
  691.2 31.8 %copy-start.8 = (f32[4,2,352,512]{3,2,0,1:T(8,128)S(1)}, f32[4,2,352,512]{3,2,0,1:T(8,128)}, u32[]{:S(2)}) copy-start(f32[4,2,352,512]{3,2,0,1:T(8,128)} %copy-done.7) | copy-start | bytes 17301508
  726.3 4.4 copy-start.30
  726.3 93.3 %collective-permute-start.19 = (bf16[352,1024]{1,0:T(8,128)(2,1)}, bf16[352,1024]{1,0:T(8,128)(2,1)S(1)}, u32[]{:S(2)}, u32[]{:S(2)}) collective-permute-start(bf16[352,1024]{1,0:T(8,128)(2,1)} %get-tuple-element.365.refs_2_), channel_id=1, source_target_pairs={{0,12},{1,13},{2,14},{3,15},{4,8},{5,9},{6,10},{7,11},{8,4},{9,5},... | collective-permute-start | bytes 2162696 | tf_op jit(solution)/shard_map/ppermute | solution.py:704
  728.3 91.3 %collective-permute-start.18 = (bf16[352,1024]{1,0:T(8,128)(2,1)}, bf16[352,1024]{1,0:T(8,128)(2,1)S(1)}, u32[]{:S(2)}, u32[]{:S(2)}) collective-permute-start(bf16[352,1024]{1,0:T(8,128)(2,1)} %get-tuple-element.367.refs_1_), channel_id=1, source_target_pairs={{0,8},{1,9},{2,10},{3,11},{4,12},{5,13},{6,14},{7,15},{8,0},{9,1},... | collective-permute-start | bytes 2162696 | tf_op jit(solution)/shard_map/ppermute | solution.py:704
  728.6 91.8 %collective-permute-start.17 = (bf16[352,1024]{1,0:T(8,128)(2,1)S(1)}, bf16[352,1024]{1,0:T(8,128)(2,1)}, u32[]{:S(2)}, u32[]{:S(2)}) collective-permute-start(bf16[352,1024]{1,0:T(8,128)(2,1)S(1)} %get-tuple-element.366.refs_0_), channel_id=1, source_target_pairs={{0,4},{1,5},{2,6},{3,7},{4,0},{5,1},{6,2},{7,3},{8,12},{9,13},{10,... | collective-permute-start | bytes 2162696 | tf_op jit(solution)/shard_map/ppermute | solution.py:704
  787.7 10.2 copy-start.5
  787.7 10.2 copy-start.43
  787.7 10.2 copy-start.45
  787.7 10.2 copy-start.60
  787.7 34.5 %collective-permute-start.9 = (bf16[16,128,1024]{2,1,0:T(8,128)(2,1)}, bf16[16,128,1024]{2,1,0:T(8,128)(2,1)}, u32[]{:S(2)}, u32[]{:S(2)}) collective-permute-start(bf16[16,128,1024]{2,1,0:T(8,128)(2,1)} %get-tuple-element.285), channel_id=1, source_target_pairs={{0,1},{1,0},{2,3},{3,2},{4,5},{5,4},{6,7},{7,6},{8,9},{9,8},{10,11... | collective-permute-start | bytes 12582920 | tf_op jit(solution)/shard_map/ppermute | solution.py:704
  798.0 9.2 copy-start.54
  798.0 9.8 copy-start.49
  798.0 11.7 %copy-start.47 = (f32[1024]{0:T(1024)S(1)}, f32[1024]{0:T(1024)}, u32[]{:S(2)}) copy-start(f32[1024]{0:T(1024)} %copy-done.46) | copy-start | bytes 12292
  798.0 11.7 %copy-start.9 = (f32[1024,1024]{1,0:T(8,128)S(1)}, f32[1024,1024]{1,0:T(8,128)}, u32[]{:S(2)}) copy-start(f32[1024,1024]{1,0:T(8,128)} %get-tuple-element.350) | copy-start | bytes 12582916
  811.4 4.5 copy-start.19
  822.2 88.7 %copy-start.12 = (f32[352,1024]{1,0:T(8,128)}, f32[352,1024]{1,0:T(8,128)S(1)}, u32[]{:S(2)}) copy-start(f32[352,1024]{1,0:T(8,128)S(1)} %fusion.70) | copy-start | bytes 4325380
  836.9 61.9 %collective-permute-start.10 = (bf16[4,2,128,512]{3,2,0,1:T(8,128)(2,1)}, bf16[4,2,128,512]{3,2,0,1:T(8,128)(2,1)}, u32[]{:S(2)}, u32[]{:S(2)}) collective-permute-start(bf16[4,2,128,512]{3,2,0,1:T(8,128)(2,1)} %copy.112), channel_id=1, source_target_pairs={{0,16},{16,0},{1,17},{17,1},{2,18},{18,2},{3,19},{19,3},{4,20},{20... | collective-permute-start | bytes 3145736 | tf_op jit(solution)/shard_map/ppermute | solution.py:704
  837.5 69.1 %collective-permute-start.11 = (bf16[2,4,128,512]{3,2,1,0:T(8,128)(2,1)}, bf16[2,4,128,512]{3,2,1,0:T(8,128)(2,1)}, u32[]{:S(2)}, u32[]{:S(2)}) collective-permute-start(bf16[2,4,128,512]{3,2,1,0:T(8,128)(2,1)} %get-tuple-element.287.refs_1_), channel_id=1, source_target_pairs={{0,2},{1,3},{2,0},{3,1},{4,6},{5,7},{6,4},{7,5},{8,10},{9,11},{10,... | collective-permute-start | bytes 3145736 | tf_op jit(solution)/shard_map/ppermute | solution.py:704
  896.8 9.8 copy-start.25
  900.7 10.3 copy-start.15
  900.7 10.3 copy-start.27
  900.7 10.3 copy-start.33
  900.7 10.3 copy-start.35
  900.7 10.3 copy-start.36
  901.6 39.3 %collective-permute-start.12 = (bf16[4,128,512]{2,1,0:T(8,128)(2,1)}, bf16[4,128,512]{2,1,0:T(8,128)(2,1)}, u32[]{:S(2)}, u32[]{:S(2)}) collective-permute-start(bf16[4,128,512]{2,1,0:T(8,128)(2,1)} %fusion.87), channel_id=1, source_target_pairs={{0,2},{1,3},{2,0},{3,1},{4,6},{5,7},{6,4},{7,5},{8,10},{9,11},{10,... | collective-permute-start | bytes 1572872 | tf_op jit(solution)/shard_map/ppermute | solution.py:704
  909.1 33.4 %collective-permute-start.13 = (bf16[4,128,512]{2,1,0:T(8,128)(2,1)}, bf16[4,128,512]{2,1,0:T(8,128)(2,1)}, u32[]{:S(2)}, u32[]{:S(2)}) collective-permute-start(bf16[4,128,512]{2,1,0:T(8,128)(2,1)} %fusion.88), channel_id=1, source_target_pairs={{0,16},{16,0},{1,17},{17,1},{2,18},{18,2},{3,19},{19,3},{4,20},{20... | collective-permute-start | bytes 1572872 | tf_op jit(solution)/shard_map/ppermute | solution.py:704
  940.2 14.2 %copy-start.13 = (f32[352,1024]{1,0:T(8,128)S(1)}, f32[352,1024]{1,0:T(8,128)}, u32[]{:S(2)}) copy-start(f32[352,1024]{1,0:T(8,128)} %copy-done.12) | copy-start | bytes 4325380
  944.2 14.7 %collective-permute-start.16 = (bf16[128,1024]{1,0:T(8,128)(2,1)S(1)}, bf16[128,1024]{1,0:T(8,128)(2,1)S(1)}, u32[]{:S(2)}, u32[]{:S(2)}) collective-permute-start(bf16[128,1024]{1,0:T(8,128)(2,1)S(1)} %get-tuple-element.370), channel_id=1, source_target_pairs={{0,12},{1,13},{2,14},{3,15},{4,8},{5,9},{6,10},{7,11},{8,4},{9,5},... | collective-permute-start | bytes 786440 | tf_op jit(solution)/shard_map/ppermute | solution.py:704
  953.7 23.3 %collective-permute-start.15 = (bf16[128,1024]{1,0:T(8,128)(2,1)S(1)}, bf16[128,1024]{1,0:T(8,128)(2,1)S(1)}, u32[]{:S(2)}, u32[]{:S(2)}) collective-permute-start(bf16[128,1024]{1,0:T(8,128)(2,1)S(1)} %get-tuple-element.369), channel_id=1, source_target_pairs={{0,8},{1,9},{2,10},{3,11},{4,12},{5,13},{6,14},{7,15},{8,0},{9,1},... | collective-permute-start | bytes 786440 | tf_op jit(solution)/shard_map/ppermute | solution.py:704
  953.9 23.1 %collective-permute-start.14 = (bf16[128,1024]{1,0:T(8,128)(2,1)S(1)}, bf16[128,1024]{1,0:T(8,128)(2,1)S(1)}, u32[]{:S(2)}, u32[]{:S(2)}) collective-permute-start(bf16[128,1024]{1,0:T(8,128)(2,1)S(1)} %get-tuple-element.368), channel_id=1, source_target_pairs={{0,4},{1,5},{2,6},{3,7},{4,0},{5,1},{6,2},{7,3},{8,12},{9,13},{10,... | collective-permute-start | bytes 786440 | tf_op jit(solution)/shard_map/ppermute | solution.py:704
  977.1 38.5 %copy-start.17 = (f32[32,6144]{1,0:T(8,128)S(1)}, f32[32,6144]{1,0:T(8,128)}, u32[]{:S(2)}) copy-start(f32[32,6144]{1,0:T(8,128)} %param.54) | copy-start | bytes 2359300
  1009.2 6.4 copy-start.28
  1009.2 6.4 copy-start.29
  1010.7 8.0 copy-start.41
  (18 other events, 50.5 us)
Sparse Core Ops, SparseCore 0:
  11.4 118.8 all-gather.4
  133.8 67.2 all-gather.6
  204.5 122.2 all-gather.8
  330.1 68.2 all-gather.10

commit v2 on v1

--- a/solution.py
+++ b/solution.py
@@ -295,10 +295,10 @@
     )(wanted.reshape(-1), counts, arrived, *after)
 
 
-def embed_send(token_grad, kept, after):
+def embed_send(token_grad, kept):
     n_seq, n_fsdp = lax.axis_size("seq"), lax.axis_size("fsdp")
     slot, size = kept[3], kept[6]
-    return exchange(collect_rows(token_grad, slot, n_seq, n_fsdp, size), False, 5, after)
+    return lax.all_to_all(collect_rows(token_grad, slot, n_seq, n_fsdp, size), ("seq", "fsdp"), 0, 0, tiled=True)
 
 
 def embed_backward(token_grad, arrived, kept, height, after):
@@ -437,7 +437,8 @@
     add_gain_grad(dgain_ref, total)
 
 
-def keys_back_kernel(raw_ref, cos_ref, sin_ref, gain_ref, own_a_ref, own_b_ref, more_a_ref, more_b_ref, out_ref, dgain_ref):
+def keys_back_kernel(raw_ref, cos_ref, sin_ref, gain_ref, own_a_ref, own_b_ref, more_a_ref, more_b_ref, *refs):
+    out_ref, dgain_ref = refs[-2:]
     total = jnp.zeros((1, HEAD_SIZE), jnp.float32)
     for head in range(KEY_VALUE_HEADS):
         own_ref, more_ref = ((own_a_ref, more_a_ref), (own_b_ref, more_b_ref))[head // HALF]
@@ -764,9 +765,10 @@
     )(where_am_i()[3].reshape(1), left, right, *filled)
 
 
-def core_kernel(at_ref, keep_ref, got_ref, left_keep_ref, left_send_ref, right_keep_ref, right_send_ref):
+def core_kernel(at_ref, keep_ref, got_ref, *refs):
+    left_keep_ref, left_send_ref, right_keep_ref, right_send_ref = refs[-4:]
     y_other, x_other = pl.program_id(0), pl.program_id(1)
-    total = (keep_ref[0].astype(jnp.float32) + got_ref[0].astype(jnp.float32)).astype(jnp.bfloat16)
+    total = keep_ref[0] + got_ref[0]
     left, right = total[:, : D // 2], total[:, D // 2 :]
 
     @pl.when(y_other == 0)
@@ -786,7 +788,7 @@
         right_send_ref[0, 0] = right
 
 
-def sum_core(keep, send):
+def sum_core(keep, send, after=()):
     rows = keep.shape[1]
     got = trade(send, "fsdp", 1)
     y_at, _, x_at, _ = where_am_i()
@@ -815,30 +817,30 @@
         grid_spec=pltpu.PrefetchScalarGridSpec(
             num_scalar_prefetch=1,
             grid=(2, 2, 4),
-            in_specs=[full, full],
+            in_specs=[full, full] + [ANY] * len(after),
             out_specs=[part(left_keep), part(left_send), part(right_keep), part(right_send)],
         ),
         out_shape=[left, left, right, right],
         compiler_params=pltpu.CompilerParams(vmem_limit_bytes=VMEM_BYTES),
         cost_estimate=pl.CostEstimate(flops=10**9, bytes_accessed=96 * 2**10 * rows, transcendentals=0),
-    )(jnp.stack([y_at, x_at]), keep, got)
+    )(jnp.stack([y_at, x_at]), keep, got, *after)
     return (lk, rk), (ls, rs)
 
 
-def sum_first(keep, send, after=0.0):
+def sum_first(keep, send):
     y_at, _, x_at, _ = where_am_i()
     low, wide = jnp.bfloat16, jnp.float32
-    left = keep[0].astype(wide) + trade(send[0], "seq", 1).astype(wide) + after
-    right = keep[1].astype(wide) + trade(send[1], "fsdp", 2).astype(wide) + after
+    left = keep[0].astype(wide) + trade(send[0], "seq", 1).astype(wide)
+    right = keep[1].astype(wide) + trade(send[1], "fsdp", 2).astype(wide)
     left_keep, left_send = halves(left, 1, x_at)
     right_keep, right_send = halves(right, 0, y_at)
     return (left_keep, right_keep), (left_send.astype(low), right_send.astype(low))
 
 
-def sum_second(keep, send, after=0.0):
+def sum_second(keep, send):
     z_at = where_am_i()[1]
-    left = keep[0] + trade(send[0], "fsdp", 2).astype(jnp.float32) + after
-    right = keep[1] + trade(send[1], "seq", 1).astype(jnp.float32) + after
+    left = keep[0] + trade(send[0], "fsdp", 2).astype(jnp.float32)
+    right = keep[1] + trade(send[1], "seq", 1).astype(jnp.float32)
     total = jnp.concatenate([left, right], axis=-1)
     own = lax.dynamic_index_in_dim(total, z_at, 0, keepdims=False)
     sends = tuple(
@@ -984,17 +986,16 @@
     dresid_out, dfinal_gain = final_back(final_grad)
     mlp_low = dresid_out.astype(jnp.bfloat16)
     staged = by_stages()
+    keep, send = (), ()
     if staged:
-        early = gradient_blocks(activated, mlp_low, 768, lambda j: 0, 352, ())
+        early = gradient_blocks(activated, mlp_low, 768, lambda j: 0, 288, ())
     else:
         down_shard = plain_sum(activated, mlp_low)
     act_grad = jnp.dot(mlp_low, down_full.T, preferred_element_type=jnp.float32)
     act_back = jax.vjp(lambda joined: jax.nn.silu(joined[:, :FF]) * joined[:, FF:], gate_up)[1]
     gate_up_low = act_back(act_grad)[0].astype(jnp.bfloat16)
     if staged:
-        early = gradient_blocks(
-            normed_two, gate_up_low, 512, lambda j: jnp.where(j < 3, 3 + j, 5 + j), 352, tuple(early)
-        )
+        early = gradient_blocks(normed_two, gate_up_low, 512, lambda j: 3 + j, 288, tuple(early))
     else:
         gate_up_shard = plain_sum(normed_two, gate_up_low)
     normed_two_grad = jnp.dot(gate_up_low, gate_up_full.T, preferred_element_type=jnp.float32)
@@ -1002,10 +1003,9 @@
     mid_extra, dmlp_gain = mid_back(normed_two_grad)
     dresid_mid = dresid_out + mid_extra
     attn_low = dresid_mid.astype(jnp.bfloat16)
-    keep, send = (), ()
     if staged:
-        early = gradient_blocks(merged, attn_low, 512, lambda j: 3, 352, tuple(early))
-        keep, send = sum_core(*early)
+        late = gradient_blocks(merged, attn_low, 512, lambda j: 0, 192, ())
+        keep, send = sum_core(*early, (attn_low,))
     else:
         out_shard = plain_sum(merged, attn_low)
     merged_grad = jnp.dot(attn_low, out_full.T, preferred_element_type=jnp.float32).astype(
@@ -1027,15 +1027,15 @@
     query_raw_grad, query_sums = shape_back(
         queries_back_kernel, query_raw, cosine, sine, head_gains, (query_grad,), send
     )
+    total = sum_last(keep, send) if staged else begin_column
     key_value_raw_grad, key_sums = shape_back(
-        keys_back_kernel, key_value_raw, cosine, sine, head_gains, (own_grad_a, own_grad_b, more_a, more_b)
+        keys_back_kernel, key_value_raw, cosine, sine, head_gains, (own_grad_a, own_grad_b, more_a, more_b), (total,)
     )
     if staged:
-        total = sum_last(keep, send)
-        down_shard, out_shard = total[:96], total[192:256]
-        gate_up_shard = beside(total, 32, (96, 128, 160, 256, 288, 320))
-        late = gradient_blocks(normed_low, query_raw_grad, 512, lambda j: j, 128, ())
-        late = gradient_blocks(normed_low, key_value_raw_grad, 512, lambda j: 2 + j, 128, tuple(late))
+        down_shard = total[:96]
+        gate_up_shard = beside(total, 32, range(96, 288, 32))
+        late = gradient_blocks(normed_low, query_raw_grad, 512, lambda j: 2 + j, 192, tuple(late))
+        late = gradient_blocks(normed_low, key_value_raw_grad, 512, lambda j: 4 + j, 192, tuple(late))
         keep, send = sum_core(*late)
     else:
         send = ()
@@ -1049,13 +1049,14 @@
     in_extra, dattn_gain = in_back(normed_grad)
     dresid_in = dresid_mid + in_extra
     token_grad_low = dresid_in.astype(jnp.bfloat16)
-    arrived = embed_send(token_grad_low, kept, send)
+    arrived = embed_send(token_grad_low, kept)
     if staged:
-        keep, send = sum_first(keep, send, arrived[0, 0, 0].astype(jnp.float32) * 0.0)
+        keep, send = sum_first(keep, send)
+        keep, send = sum_second(keep, send)
     embed_grad, square = embed_backward(token_grad_low, arrived, kept, embedding.shape[0], send)
     if staged:
-        keep, send = sum_second(keep, send, square * 0.0)
-        qkv_shard = beside(sum_last(keep, send), 32, (0, 32, 64, 96))
+        total = sum_last(keep, send)
+        out_shard, qkv_shard = total[:64], beside(total, 32, range(64, 192, 32))
     shards = (qkv_shard, out_shard, gate_up_shard, down_shard)
     for shard in shards:
         square = square + jnp.sum(shard * shard)

time: 1090 us -> 1020 us (0.936)
  Pallas kernels: 436 us -> 374 us
  starting transfers between devices: 30.2 us -> 60.2 us
  local copies, waits for them, and re-layouts: 52.1 us -> 39.7 us
    pallas_call x5 -> x4, Pallas kernels: 174 us -> 116 us  [exchange(): pl.pallas_call(functools.partial(exchange_kernel, n_seq, n_fsdp, to_all),...]
    ppermute x2, starting transfers between devices: 0.07 us -> 34.3 us  [to_tokens_before(): return lax.ppermute(parts, 'seq', [(0, 1), (1, 0)])]
  transfers between devices with their start and end apart: 24 -> 25, of which waited for: 9 -> 10; matrix products, arithmetic and copies ran while one was open for 17% -> 19% of each run, Pallas kernels for 31% -> 27%
where the time goes in v2:
time: 1020 us; the launch traced here: 1010 us
  Pallas kernels  374 us (37%)
  waiting for transfers between devices  207 us (20%)
  other arithmetic  156 us (15%)
  matrix products  135 us (13%)
  starting transfers between devices  60.2 us (6%)
  local copies, waits for them, and re-layouts  39.7 us (4%)
  between operations  24.3 us (2%)
  loops' own time  11.7 us (1%)
    pallas_call x4, Pallas kernels, exchange(): pl.pallas_call(functools.partial(exchange_kernel, n_seq, n_fsdp, to_all),...  116 us
    ppermute x2, waiting for transfers between devices, tokens_before(): return lax.ppermute(own, 'seq', [(0, 1), (1, 0)])  89.3 us
    ppermute x16, waiting for transfers between devices, trade(): return lax.ppermute(values, axis, [(i, i ^ bit) for i in range(count)])  87.9 us
    pallas_call x2, Pallas kernels, attention_backward(): pl.pallas_call(functools.partial(backward_kernel, keys), grid_spec=pltpu....  66.2 us
    pallas_call x5, Pallas kernels, gradient_blocks(): pl.pallas_call(functools.partial(gradient_kernel, height), grid_spec=pltp...  62.6 us
    sub x6, other arithmetic, adam_update(): weight - LEARN_RATE * (moment_one / fix_one / (jnp.sqrt(moment_two / fix_...  56.6 us
    ppermute x2, starting transfers between devices, to_tokens_before(): return lax.ppermute(parts, 'seq', [(0, 1), (1, 0)])  34.3 us
    pallas_call x2, Pallas kernels, attention_forward(): pl.pallas_call(functools.partial(forward_kernel, keys), grid_spec=pltpu.P...  30.7 us
  transfers between devices with their start and end apart: 25, of which 10 were waited for; matrix products, arithmetic and copies ran while one was open for 19% of the time, Pallas kernels for 27%

profile of v2, /device:TPU:0, one launch (start us, length us, event | category | flops | bytes accessed | tf_op | source)
XLA Modules:
  0.0 1007.3 jit_solution(7974012049492636935)
XLA Ops:
  10.8 1.9 convert_element_type.245
  15.4 2.3 convert_reduce_fusion.2
  24.7 12.9 %shard_map.416 = s32[32,8,128]{2,1,0:T(8,128)} custom-call(s32[32,8,128]{2,1,0:T(8,128)} %pad_add_fusion.2.x_ref), custom_call_target="tpu_custom_call" | custom-call | tf_op jit(solution)/shard_map/pallas_call | solution.py:98
  40.9 14.5 %gather_fusion.1 = bf16[2560,512]{1,0:T(8,128)(2,1)S(1)} fusion(f32[9496,512]{1,0:T(8,128)} %param.45, s32[3072]{0:T(1024)S(1)} %pad_clamp_fusion.1), kind=kCustom, calls=%fused_computation.1 | custom fusion | bytes 5253120 | tf_op jit(solution)/shard_map/jit(_take)/gather | solution.py:147
  55.5 2.4 broadcast_select_fusion.1
  57.9 76.1 %shard_map.417 = bf16[32,80,512]{2,1,0:T(8,128)(2,1)S(1)} custom-call(bf16[32,80,512]{2,1,0:T(8,128)(2,1)} %bitcast.160), custom_call_target="tpu_custom_call" | custom-call | tf_op jit(solution)/shard_map/pallas_call | solution.py:98
  134.0 12.0 %conditional.2 = (bf16[1024,1024]{0,1:T(8,128)(2,1)}) conditional(s32[]{:T(128)} %convert_element_type.235, (s32[1024]{0:T(1024)S(1)}, bf16[32,80,512]{2,1,0:T(8,128)(2,1)S(1)}, s32[]{:T(128)}, s32[1024]{0:T(1024)S(1)}, s32[1024]{0:T(1024)S(1)}, /*index=5*/s32[1024]{0:T(1024)S(1)}, f32[9496,512]{1,0:T(8,128)}) %tuple.144, (s32[1024]{0:T(1024)S(1)}, ...), branch_computations={%region_10.14_spmd, %region_14.15_spmd} | conditional | flops 5396661248 | bytes 153264544 | solution.py:214
  146.0 2.9 copy.101
  160.1 9.3 convolution_convert_fusion.1.raw_ref
  169.4 7.5 shard_map.419
  181.9 9.3 convolution_convert_fusion.2.raw_ref
  191.3 11.8 %shard_map.418.q_ref = bf16[1024,2048]{1,0:T(8,128)(2,1)} custom-call(bf16[1024,2048]{1,0:T(8,128)(2,1)} %convolution_convert_fusion.2.raw_ref, f32[1024,128]{1,0:T(8,128)} %get-tuple-element.403.cos_ref, f32[1024,128]{1,0:T(8,128)} %get-tuple-element.404.sin_ref, f32[2,128]{1,0:T(2,128)} %slice_bitcast_fusion.gain_ref), custom_call_target="tpu_custom_call" | custom-call | flops 4000000000 | bytes 8388608 | tf_op jit(solution)/shard_map/pallas_call | solution.py:385
  203.0 32.8 %collective-permute-done.1.kb_ref.vb_ref = bf16[1024,1024]{1,0:T(8,128)(2,1)} collective-permute-done((bf16[1024,1024]{1,0:T(8,128)(2,1)}, bf16[1024,1024]{1,0:T(8,128)(2,1)}, u32[]{:S(2)}, u32[]{:S(2)}) %collective-permute-start.1) | collective-permute-done | bytes 2097184 | tf_op jit(solution)/shard_map/ppermute | solution.py:690
  235.8 15.3 %shard_map.420 = (bf16[1024,2048]{1,0:T(8,128)(2,1)}, f32[8,1024,2]{2,1,0:T(8,128)}) custom-call(s32[6]{0:T(128)} %pad_add_fusion.6.scalar_ref, bf16[1024,2048]{1,0:T(8,128)(2,1)} %shard_map.418.q_ref, bf16[1024,1024]{1,0:T(8,128)(2,1)} %collective-permute-done.1.kb_ref.vb_ref, bf16[1024,1024]{1,0:T(8,128)(2,1)} %collective-permute-done.1.kb_ref.vb_ref, ...), custom_call_target="tpu_custom_call" | custom-call | flops 20000000000 | bytes 16777216 | tf_op jit(solution)/shard_map/pallas_call | solution.py:585
  251.1 56.6 %collective-permute-done.kb_ref.vb_ref = bf16[1024,1024]{1,0:T(8,128)(2,1)S(1)} collective-permute-done((bf16[1024,1024]{1,0:T(8,128)(2,1)}, bf16[1024,1024]{1,0:T(8,128)(2,1)S(1)}, u32[]{:S(2)}, u32[]{:S(2)}) %collective-permute-start) | collective-permute-done | bytes 2097184 | tf_op jit(solution)/shard_map/ppermute | solution.py:690
  308.9 15.4 %shard_map.421 = (bf16[1024,2048]{1,0:T(8,128)(2,1)}, f32[8,1024,2]{2,1,0:T(8,128)}) custom-call(s32[6]{0:T(128)} %pad_add_fusion.6.scalar_ref, bf16[1024,2048]{1,0:T(8,128)(2,1)} %shard_map.418.q_ref, bf16[1024,1024]{1,0:T(8,128)(2,1)} %copy-done.70, bf16[1024,1024]{1,0:T(8,128)(2,1)} %copy-done.70, ...), custom_call_target="tpu_custom_call", output_to_operand_aliasing={{0}: (7, {}), {1}: (8, {})} | custom-call | flops 20000000000 | bytes 16777216 | tf_op jit(solution)/shard_map/pallas_call | solution.py:585
  324.4 7.9 multiply_reduce_fusion.6
  332.3 2.0 copy-done.8
  334.7 21.6 %fusion.128 = f32[1024,6144]{1,0:T(8,128)} fusion(bf16[1024,1024]{1,0:T(8,128)(2,1)S(1)} %multiply_convert_fusion.1.left_ref, bf16[1024,6144]{1,0:T(8,128)(2,1)} %all-gather.9.cloned.1.call-done), kind=kOutput, calls=%fused_computation.311 | convolution fusion | flops 12884901888 | bytes 39845888 | tf_op jit(solution)/shard_map/dot_general | solution.py:959
  356.3 12.8 %multiply_convert_fusion.left_ref = bf16[1024,3072]{1,0:T(8,128)(2,1)} fusion(f32[1024,6144]{1,0:T(8,128)} %fusion.128), kind=kLoop, calls=%fused_computation.67 | loop fusion | flops 18874368 | bytes 31457280 | tf_op jit(solution)/shard_map/convert_element_type | solution.py:960
  369.1 29.2 %all-gather.11.cloned.1.call-done = bf16[3072,1024]{1,0:T(8,128)(2,1)} async-done(((bf16[96,1024]{1,0:T(8,128)(2,1)}), bf16[3072,1024]{1,0:T(8,128)(2,1)}) %all-gather.11.cloned.1.call-update) | async-done | bytes 6291472 | tf_op jit(solution)/shard_map/all_gather | solution.py:700
  398.3 11.4 %multiply_reduce_fusion.5 = (f32[1024]{0:T(1024)S(1)}, f32[1024,1024]{1,0:T(8,128)S(1)}) fusion(f32[1024,1024]{1,0:T(8,128)} %copy-done.8, bf16[1024,3072]{1,0:T(8,128)(2,1)} %multiply_convert_fusion.left_ref, bf16[3072,1024]{1,0:T(8,128)(2,1)} %all-gather.11.cloned.1.call-done), kind=kOutput, calls=%fused_computation.120 | convolution fusion | flops 6445595648 | bytes 20975616 | tf_op jit(solution)/shard_map/dot_general | solution.py:961
  409.7 2.0 copy-done.2
  413.5 9.6 shard_map.422
  425.1 4.2 multiply_reduce_fusion.1
  429.3 2.1 fusion.58.right_ref
  431.4 11.2 %shard_map.423 = (bf16[16,288,1024]{2,1,0:T(8,128)(2,1)}, bf16[16,288,1024]{2,1,0:T(8,128)(2,1)}) custom-call(s32[1]{0:T(128)} %bitcast.31.core_ref, bf16[1024,3072]{1,0:T(8,128)(2,1)} %multiply_convert_fusion.left_ref, bf16[1024,1024]{1,0:T(8,128)(2,1)} %fusion.58.right_ref), custom_call_target="tpu_custom_call" | custom-call | flops 6442450944 | bytes 16777216 | tf_op jit(solution)/shard_map/pallas_call | solution.py:746
  442.6 25.0 %fusion.64 = (f32[1024,3072]{1,0:T(8,128)}, f32[1024,3072]{1,0:T(8,128)}) fusion(f32[1024,6144]{1,0:T(8,128)} %fusion.128, bf16[1024,1024]{1,0:T(8,128)(2,1)S(1)} %copy-done.25, bf16[3072,1024]{1,0:T(8,128)(2,1)} %all-gather.11.cloned.1.call-done), kind=kOutput, calls=%fused_computation.155 | convolution fusion | flops 6480199680 | bytes 58720256 | tf_op jit(solution)/shard_map/dot_general | solution.py:994
  467.6 13.2 %add_convert_fusion.right_ref = bf16[1024,6144]{1,0:T(8,128)(2,1)} fusion(f32[1024,3072]{1,0:T(8,128)} %get-tuple-element.370, f32[1024,3072]{1,0:T(8,128)} %get-tuple-element.369), kind=kLoop, calls=%fused_computation.60 | loop fusion | flops 12582912 | bytes 37748736 | tf_op jit(solution)/shard_map/convert_element_type | solution.py:996
  480.9 23.1 %shard_map.424 = (bf16[16,288,1024]{2,1,0:T(8,128)(2,1)}, bf16[16,288,1024]{2,1,0:T(8,128)(2,1)}) custom-call(s32[1]{0:T(128)} %bitcast.31.core_ref, bf16[1024,1024]{1,0:T(8,128)(2,1)} %copy-done.23, bf16[1024,6144]{1,0:T(8,128)(2,1)} %add_convert_fusion.right_ref, ...), custom_call_target="tpu_custom_call", output_to_operand_aliasing={{0}: (3, {}), {1}: (4, {})} | custom-call | flops 12884901888 | bytes 16777216 | tf_op jit(solution)/shard_map/pallas_call | solution.py:746
  504.7 22.5 %multiply_reduce_fusion.2 = (f32[1024]{0:T(1024)}, f32[1024]{0:T(1024)S(1)}, f32[1024,1024]{1,0:T(8,128)S(1)}) fusion(f32[1024,1024]{1,0:T(8,128)} %copy-done.8, f32[1024]{0:T(1024)S(1)} %fusion.110, f32[1024]{0:T(1024)S(1)} %get-tuple-element.385, bf16[1024,6144]{1,0:T(8,128)(2,1)} %add_convert_fusion.right_ref, ...), kind=kOutput, calls=%fused_computation.117 | convolution fusion | flops 12891191296 | bytes 33570816 | tf_op jit(solution)/shard_map/dot_general | solution.py:1001
  527.3 3.7 fusion.120
  531.0 6.5 convolution_convert_fusion.do_ref
  537.5 16.1 %shard_map.425 = (bf16[4,2,288,512]{3,2,1,0:T(8,128)(2,1)}, bf16[4,2,288,512]{3,2,1,0:T(8,128)(2,1)}, bf16[2,4,288,512]{3,2,1,0:T(8,128)(2,1)}, bf16[2,4,288,512]{3,2,1,0:T(8,128)(2,1)}) custom-call(s32[2]{0:T(128)} %pad_add_fusion.7.at_ref, bf16[16,288,1024]{2,1,0:T(8,128)(2,1)} %get-tuple-element.270.keep_ref, ...), custom_call_target="tpu_custom_call" | custom-call | flops 1000000000 | bytes 28311552 | tf_op jit(solution)/shard_map/pallas_call | solution.py:815
  557.5 33.2 %shard_map.426 = (f32[1024,2048]{1,0:T(8,128)}, bf16[2,1024,512]{2,1,0:T(8,128)(2,1)}, f32[2,1024,512]{2,1,0:T(8,128)}) custom-call(s32[6]{0:T(128)} %pad_add_fusion.6.scalar_ref, bf16[1024,2048]{1,0:T(8,128)(2,1)} %shard_map.418.q_ref, bf16[1024,1024]{1,0:T(8,128)(2,1)} %collective-permute-done.1.kb_ref.vb_ref, ...), custom_call_target="tpu_custom_call" | custom-call | flops 40000000000 | bytes 41943040 | tf_op jit(solution)/shard_map/pallas_call | solution.py:658
  590.7 17.1 %collective-permute-start.7 = (bf16[2,1024,512]{2,1,0:T(8,128)(2,1)}, bf16[2,1024,512]{2,1,0:T(8,128)(2,1)}, u32[]{:S(2)}, u32[]{:S(2)}) collective-permute-start(bf16[2,1024,512]{2,1,0:T(8,128)(2,1)} %get-tuple-element.281), channel_id=1, source_target_pairs={{0,16},{16,0},{1,17},{17,1},{2,18},{18,2},{3,19},{19,3},{4,20},{20... | collective-permute-start | bytes 6291464 | tf_op jit(solution)/shard_map/ppermute | solution.py:696
  610.7 3.3 convert_add_fusion.2
  614.7 2.4 convert_add_fusion.1
  617.1 2.1 copy-done.10
  620.9 33.0 %shard_map.427 = (f32[1024,2048]{1,0:T(8,128)}, bf16[2,1024,512]{2,1,0:T(8,128)(2,1)}, f32[2,1024,512]{2,1,0:T(8,128)}) custom-call(s32[6]{0:T(128)} %pad_add_fusion.6.scalar_ref, bf16[1024,2048]{1,0:T(8,128)(2,1)} %shard_map.418.q_ref, bf16[1024,1024]{1,0:T(8,128)(2,1)} %copy-done.70, ...), custom_call_target="tpu_custom_call", output_to_operand_aliasing={{0}: (10, {})} | custom-call | flops 40000000000 | bytes 41943040 | tf_op jit(solution)/shard_map/pallas_call | solution.py:658
  653.9 17.3 %collective-permute-start.8 = (bf16[2,1024,512]{2,1,0:T(8,128)(2,1)}, bf16[2,1024,512]{2,1,0:T(8,128)(2,1)}, u32[]{:S(2)}, u32[]{:S(2)}) collective-permute-start(bf16[2,1024,512]{2,1,0:T(8,128)(2,1)} %get-tuple-element.282), channel_id=1, source_target_pairs={{0,16},{16,0},{1,17},{17,1},{2,18},{18,2},{3,19},{19,3},{4,20},{20... | collective-permute-start | bytes 6291464 | tf_op jit(solution)/shard_map/ppermute | solution.py:696
  671.1 8.7 shard_map.430
  684.4 2.8 collective-permute-start.11
  688.9 17.4 %shard_map.428 = (bf16[1024,2048]{1,0:T(8,128)(2,1)}, f32[8,128]{1,0:T(8,128)}) custom-call(bf16[1024,2048]{1,0:T(8,128)(2,1)} %convolution_convert_fusion.2.raw_ref, f32[1024,128]{1,0:T(8,128)} %get-tuple-element.403.cos_ref, f32[1024,128]{1,0:T(8,128)} %get-tuple-element.404.sin_ref, f32[2,128]{1,0:T(2,128)} %slice_bitcast_fusion.gain_ref, ...), custom_call_target="tpu_custom_call" | custom-call | flops 5000000000 | bytes 20971520 | tf_op jit(solution)/shard_map/pallas_call | solution.py:464
  706.3 9.8 shard_map.431
  716.0 18.2 %collective-permute-done.10 = bf16[288,1024]{1,0:T(8,128)(2,1)S(1)} collective-permute-done((bf16[288,1024]{1,0:T(8,128)(2,1)S(1)}, bf16[288,1024]{1,0:T(8,128)(2,1)S(1)}, u32[]{:S(2)}, u32[]{:S(2)}) %collective-permute-start.10) | collective-permute-done | bytes 589856 | tf_op jit(solution)/shard_map/ppermute | solution.py:705
  735.7 13.0 %shard_map.429 = (bf16[1024,2048]{1,0:T(8,128)(2,1)}, f32[8,128]{1,0:T(8,128)}) custom-call(bf16[1024,2048]{1,0:T(8,128)(2,1)} %convolution_convert_fusion.1.raw_ref, f32[1024,128]{1,0:T(8,128)} %get-tuple-element.403.cos_ref, f32[1024,128]{1,0:T(8,128)} %get-tuple-element.404.sin_ref, f32[2,128]{1,0:T(2,128)} %slice_bitcast_fusion.gain_ref, ...), custom_call_target="tpu_custom_call" | custom-call | flops 5000000000 | bytes 20971520 | tf_op jit(solution)/shard_map/pallas_call | solution.py:464
  748.7 9.9 shard_map.432
  758.7 6.5 fusion.50
  765.3 7.4 fusion.47
  780.0 5.5 all-to-all-start.4
  785.6 13.6 %shard_map.433 = (bf16[4,2,192,512]{3,2,1,0:T(8,128)(2,1)}, bf16[4,2,192,512]{3,2,1,0:T(8,128)(2,1)}, bf16[2,4,192,512]{3,2,1,0:T(8,128)(2,1)}, bf16[2,4,192,512]{3,2,1,0:T(8,128)(2,1)}) custom-call(s32[2]{0:T(128)} %pad_add_fusion.7.at_ref, bf16[16,192,1024]{2,1,0:T(8,128)(2,1)} %get-tuple-element.290.keep_ref, ...), custom_call_target="tpu_custom_call" | custom-call | flops 1000000000 | bytes 18874368 | tf_op jit(solution)/shard_map/pallas_call | solution.py:815
  804.9 46.3 %collective-permute-done.15 = bf16[2,4,192,512]{3,2,1,0:T(8,128)(2,1)S(1)} collective-permute-done((bf16[2,4,192,512]{3,2,1,0:T(8,128)(2,1)}, bf16[2,4,192,512]{3,2,1,0:T(8,128)(2,1)S(1)}, u32[]{:S(2)}, u32[]{:S(2)}) %collective-permute-start.15) | collective-permute-done | bytes 1572896 | tf_op jit(solution)/shard_map/ppermute | solution.py:705
  856.0 15.1 %collective-permute-done.16 = bf16[4,192,512]{2,1,0:T(8,128)(2,1)S(1)} collective-permute-done((bf16[4,192,512]{2,1,0:T(8,128)(2,1)S(1)}, bf16[4,192,512]{2,1,0:T(8,128)(2,1)S(1)}, u32[]{:S(2)}, u32[]{:S(2)}) %collective-permute-start.16) | collective-permute-done | bytes 786464 | tf_op jit(solution)/shard_map/ppermute | solution.py:705
  871.4 2.4 collective-permute-done.14
  875.3 2.5 collective-permute-start.19
  881.1 26.9 %conditional.3 = (f32[9496,512]{1,0:T(8,128)}, f32[]{:T(128)}) conditional(s32[]{:T(128)} %convert_element_type.235, (s32[32,80]{1,0:T(8,128)S(1)}, bf16[32,80,512]{2,1,0:T(8,128)(2,1)S(1)}, bf16[192,1024]{1,0:T(8,128)(2,1)}, bf16[192,1024]{1,0:T(8,128)(2,1)}, bf16[192,1024]{1,0:T(8,128)(2,1)}, /*index=5*/s32[]{:T(128)}, s32[1024]{0:T(1024)S(1)}, ...), branch_computations={%region_33.40_spmd, %region_40.43_spmd} | conditional | flops 3705905920 | bytes 151820720 | solution.py:328
  887.4 19.3 %branch_1_fun.1 = (f32[9496,512]{1,0:T(8,128)}, f32[8,512]{1,0:T(8,128)}) custom-call(s32[2560]{0:T(1024)} %reshape.545.wanted_ref, s32[32]{0:T(128)} %convert_reduce_fusion.count_ref, bf16[32,80,512]{2,1,0:T(8,128)(2,1)S(1)} %get-tuple-element.197.arrived_ref, bf16[192,1024]{1,0:T(8,128)(2,1)} %get-tuple-element.198.refs_0_, ...), custom_call_target="tpu_custom_call" | custom-call | flops 1000000000 | bytes 83886080 | tf_op jit(solution)/shard_map/cond/branch_1_fun/pallas_call | solution.py:280
  908.0 3.9 collective-permute-done.18
  918.9 17.7 %shard_map.434 = f32[32,40,128]{2,1,0:T(8,128)} custom-call(f32[40,128]{1,0:T(8,128)} %pad_bitcast_fusion.x_ref), custom_call_target="tpu_custom_call" | custom-call | tf_op jit(solution)/shard_map/pallas_call | solution.py:98
  942.2 2.6 multiply_subtract_fusion.4
  944.7 2.2 multiply_subtract_fusion.6
  948.8 2.2 multiply_subtract_fusion.5
  952.2 47.2 %multiply_subtract_fusion.2 = (f32[9496,512]{1,0:T(8,128)}, f32[9496,512]{1,0:T(8,128)}, f32[9496,512]{1,0:T(8,128)}) fusion(f32[9496,512]{1,0:T(8,128)} %param.45, f32[]{:T(128)} %bitcast.57, f32[]{:T(128)} %bitcast.56, f32[9496,512]{1,0:T(8,128)} %get-tuple-element.297, f32[]{:T(128)S(6)} %div.181, f32[9496,512]{1,0:T(8,128)} %param.47, f32[9496,512]{1,0:T(8,128)} %param.46), kind=kLoop, calls=%fused_computation.62 | loop fusion | flops 77791232 | bytes 136134672 | tf_op jit(solution)/shard_map/sub | solution.py:874
  (299 shorter events, 93.9 us)
Async XLA Ops:
  7.2 152.9 %all-gather.5.cloned.1.call-start = ((), (), s32[]{:S(2)}) async-start(), calls=%async_computation.5 | async-start | bytes 8650752 | tf_op jit(solution)/shard_map/all_gather | solution.py:700
  9.0 315.3 %all-gather.7.cloned.1.call-start = ((), (), s32[]{:S(2)}) async-start(), calls=%async_computation.6 | async-start | bytes 4325376 | tf_op jit(solution)/shard_map/all_gather | solution.py:700
  10.7 324.0 %all-gather.9.cloned.1.call-start = ((), (), s32[]{:S(2)}) async-start(), calls=%async_computation.7 | async-start | bytes 12976128 | tf_op jit(solution)/shard_map/all_gather | solution.py:700
  12.7 385.6 %all-gather.11.cloned.1.call-start = ((), (), s32[]{:S(2)}) async-start(), calls=%async_computation.8 | async-start | bytes 6488064 | tf_op jit(solution)/shard_map/all_gather | solution.py:700
  15.4 118.6 %copy-start.41 = (s32[1024]{0:T(1024)}, s32[1024]{0:T(1024)S(1)}, u32[]{:S(2)}) copy-start(s32[1024]{0:T(1024)S(1)} %get-tuple-element.389) | copy-start | bytes 12292
  17.7 116.3 %copy-start.39 = (s32[1024]{0:T(1024)}, s32[1024]{0:T(1024)S(1)}, u32[]{:S(2)}) copy-start(s32[1024]{0:T(1024)S(1)} %convert_reduce_fusion.2) | copy-start | bytes 12292
  22.6 111.4 %copy-start.62 = (s32[1024]{0:T(1024)}, s32[1024]{0:T(1024)S(1)}, u32[]{:S(2)}) copy-start(s32[1024]{0:T(1024)S(1)} %get-tuple-element.391) | copy-start | bytes 12292
  55.4 78.6 %copy-start.32 = (s32[1,1024]{1,0:T(1,128)S(1)}, s32[1,1024]{1,0:T(1,128)}, u32[]{:S(2)}) copy-start(s32[1,1024]{1,0:T(1,128)} %param.41) | copy-start | bytes 12292
  146.0 10.4 %copy-start.61 = (f32[3328]{0:T(1024)S(1)}, f32[3328]{0:T(1024)}, u32[]{:S(2)}) copy-start(f32[3328]{0:T(1024)} %param.60) | copy-start | bytes 39940
  148.9 175.4 %copy-start.5 = (bf16[1024,1024]{1,0:T(8,128)(2,1)}, bf16[1024,1024]{1,0:T(8,128)(2,1)S(1)}, u32[]{:S(2)}) copy-start(bf16[1024,1024]{1,0:T(8,128)(2,1)S(1)} %copy.101) | copy-start | bytes 6291460
  158.1 11.2 %copy-start.49 = (f32[1024]{0:T(1024)}, f32[1024]{0:T(1024)S(1)}, u32[]{:S(2)}) copy-start(f32[1024]{0:T(1024)S(1)} %fusion.109) | copy-start | bytes 12292
  158.1 11.2 %copy-start.51 = (f32[1024]{0:T(1024)}, f32[1024]{0:T(1024)S(1)}, u32[]{:S(2)}) copy-start(f32[1024]{0:T(1024)S(1)} %get-tuple-element.384) | copy-start | bytes 12292
  169.4 8.8 copy-start.28
  169.4 10.9 %copy-start.68 = (s32[48]{0:T(128)S(1)}, s32[48]{0:T(128)}, u32[]{:S(2)}) copy-start(s32[48]{0:T(128)} %param.43) | copy-start | bytes 580
  176.9 59.0 %collective-permute-start.1 = (bf16[1024,1024]{1,0:T(8,128)(2,1)}, bf16[1024,1024]{1,0:T(8,128)(2,1)}, u32[]{:S(2)}, u32[]{:S(2)}) collective-permute-start(bf16[1024,1024]{1,0:T(8,128)(2,1)} %get-tuple-element.263.k_ref.v_ref), channel_id=1, source_target_pairs={{0,16},{16,0},{1,17},{17,1},{2,18},{18,2},{3,19},{19,3},{4,20},{20... | collective-permute-start | bytes 6291464 | tf_op jit(solution)/shard_map/ppermute | solution.py:690
  181.2 126.5 %collective-permute-start = (bf16[1024,1024]{1,0:T(8,128)(2,1)}, bf16[1024,1024]{1,0:T(8,128)(2,1)S(1)}, u32[]{:S(2)}, u32[]{:S(2)}) collective-permute-start(bf16[1024,1024]{1,0:T(8,128)(2,1)} %get-tuple-element.262.k_ref.v_ref), channel_id=1, source_target_pairs={{0,16},{16,0},{1,17},{17,1},{2,18},{18,2},{3,19},{19,3},{4,20},{20... | collective-permute-start | bytes 6291464 | tf_op jit(solution)/shard_map/ppermute | solution.py:690
  332.3 24.1 %copy-start.58 = (f32[1024]{0:T(1024)}, f32[1024]{0:T(1024)S(1)}, u32[]{:S(2)}) copy-start(f32[1024]{0:T(1024)S(1)} %get-tuple-element.397) | copy-start | bytes 12292
  334.7 21.7 %copy-start.23 = (bf16[1024,1024]{1,0:T(8,128)(2,1)}, bf16[1024,1024]{1,0:T(8,128)(2,1)S(1)}, u32[]{:S(2)}) copy-start(bf16[1024,1024]{1,0:T(8,128)(2,1)S(1)} %multiply_convert_fusion.1.left_ref) | copy-start | bytes 6291460
  369.1 42.6 %copy-start.46 = (f32[1024]{0:T(1024)S(1)}, f32[1024]{0:T(1024)}, u32[]{:S(2)}) copy-start(f32[1024]{0:T(1024)} %param.63) | copy-start | bytes 12292
  431.4 11.2 %copy-start.25 = (bf16[1024,1024]{1,0:T(8,128)(2,1)S(1)}, bf16[1024,1024]{1,0:T(8,128)(2,1)}, u32[]{:S(2)}) copy-start(bf16[1024,1024]{1,0:T(8,128)(2,1)} %fusion.58.right_ref) | copy-start | bytes 6291460
  504.0 33.5 %collective-permute-start.2 = (bf16[16,288,1024]{2,1,0:T(8,128)(2,1)}, bf16[16,288,1024]{2,1,0:T(8,128)(2,1)}, u32[]{:S(2)}, u32[]{:S(2)}) collective-permute-start(bf16[16,288,1024]{2,1,0:T(8,128)(2,1)} %get-tuple-element.271), channel_id=1, source_target_pairs={{0,1},{1,0},{2,3},{3,2},{4,5},{5,4},{6,7},{7,6},{8,9},{9,8},{10,11... | collective-permute-start | bytes 28311560 | tf_op jit(solution)/shard_map/ppermute | solution.py:705
  504.7 22.5 %copy-start.59 = (f32[1024]{0:T(1024)S(1)}, f32[1024]{0:T(1024)}, u32[]{:S(2)}) copy-start(f32[1024]{0:T(1024)} %copy-done.58) | copy-start | bytes 12292
  504.7 22.6 %copy-start.4 = (f32[1024,1024]{1,0:T(8,128)S(1)}, f32[1024,1024]{1,0:T(8,128)}, u32[]{:S(2)}) copy-start(f32[1024,1024]{1,0:T(8,128)} %copy-done.2) | copy-start | bytes 12582916
  504.7 22.6 %copy-start.9 = (f32[1024,1024]{1,0:T(8,128)S(1)}, f32[1024,1024]{1,0:T(8,128)}, u32[]{:S(2)}) copy-start(f32[1024,1024]{1,0:T(8,128)} %copy-done.8) | copy-start | bytes 12582916
  531.0 6.5 copy-start.15
  555.4 53.9 %collective-permute-start.3 = (bf16[4,2,288,512]{3,2,0,1:T(8,128)(2,1)S(1)}, bf16[4,2,288,512]{3,2,0,1:T(8,128)(2,1)S(1)}, u32[]{:S(2)}, u32[]{:S(2)}) collective-permute-start(bf16[4,2,288,512]{3,2,0,1:T(8,128)(2,1)S(1)} %copy.109), channel_id=1, source_target_pairs={{0,16},{16,0},{1,17},{17,1},{2,18},{18,2},{3,19},{19,3},{4,20},{20... | collective-permute-start | bytes 7077896 | tf_op jit(solution)/shard_map/ppermute | solution.py:705
  556.1 58.6 %collective-permute-start.4 = (bf16[2,4,288,512]{3,2,1,0:T(8,128)(2,1)}, bf16[2,4,288,512]{3,2,1,0:T(8,128)(2,1)}, u32[]{:S(2)}, u32[]{:S(2)}) collective-permute-start(bf16[2,4,288,512]{3,2,1,0:T(8,128)(2,1)} %get-tuple-element.273.refs_1_), channel_id=1, source_target_pairs={{0,2},{1,3},{2,0},{3,1},{4,6},{5,7},{6,4},{7,5},{8,10},{9,11},{10,... | collective-permute-start | bytes 7077896 | tf_op jit(solution)/shard_map/ppermute | solution.py:705
  590.7 144.9 %collective-permute-start.7 = (bf16[2,1024,512]{2,1,0:T(8,128)(2,1)}, bf16[2,1024,512]{2,1,0:T(8,128)(2,1)}, u32[]{:S(2)}, u32[]{:S(2)}) collective-permute-start(bf16[2,1024,512]{2,1,0:T(8,128)(2,1)} %get-tuple-element.281), channel_id=1, source_target_pairs={{0,16},{16,0},{1,17},{17,1},{2,18},{18,2},{3,19},{19,3},{4,20},{20... | collective-permute-start | bytes 6291464 | tf_op jit(solution)/shard_map/ppermute | solution.py:696
  614.2 65.6 %collective-permute-start.5 = (bf16[4,288,512]{2,1,0:T(8,128)(2,1)S(1)}, bf16[4,288,512]{2,1,0:T(8,128)(2,1)}, u32[]{:S(2)}, u32[]{:S(2)}) collective-permute-start(bf16[4,288,512]{2,1,0:T(8,128)(2,1)S(1)} %fusion.65.refs_1_), channel_id=1, source_target_pairs={{0,2},{1,3},{2,0},{3,1},{4,6},{5,7},{6,4},{7,5},{8,10},{9,11},{10,... | collective-permute-start | bytes 3538952 | tf_op jit(solution)/shard_map/ppermute | solution.py:705
  619.5 62.2 %collective-permute-start.6 = (bf16[4,288,512]{2,1,0:T(8,128)(2,1)S(1)}, bf16[4,288,512]{2,1,0:T(8,128)(2,1)}, u32[]{:S(2)}, u32[]{:S(2)}) collective-permute-start(bf16[4,288,512]{2,1,0:T(8,128)(2,1)S(1)} %fusion.66.refs_2_), channel_id=1, source_target_pairs={{0,16},{16,0},{1,17},{17,1},{2,18},{18,2},{3,19},{19,3},{4,20},{20... | collective-permute-start | bytes 3538952 | tf_op jit(solution)/shard_map/ppermute | solution.py:705
  653.9 81.8 %collective-permute-start.8 = (bf16[2,1024,512]{2,1,0:T(8,128)(2,1)}, bf16[2,1024,512]{2,1,0:T(8,128)(2,1)}, u32[]{:S(2)}, u32[]{:S(2)}) collective-permute-start(bf16[2,1024,512]{2,1,0:T(8,128)(2,1)} %get-tuple-element.282), channel_id=1, source_target_pairs={{0,16},{16,0},{1,17},{17,1},{2,18},{18,2},{3,19},{19,3},{4,20},{20... | collective-permute-start | bytes 6291464 | tf_op jit(solution)/shard_map/ppermute | solution.py:696
  684.4 31.6 %collective-permute-start.11 = (bf16[288,1024]{1,0:T(8,128)(2,1)S(1)}, bf16[288,1024]{1,0:T(8,128)(2,1)S(1)}, u32[]{:S(2)}, u32[]{:S(2)}) collective-permute-start(bf16[288,1024]{1,0:T(8,128)(2,1)S(1)} %get-tuple-element.373.refs_2_), channel_id=1, source_target_pairs={{0,12},{1,13},{2,14},{3,15},{4,8},{5,9},{6,10},{7,11},{8,4},{9,5},... | collective-permute-start | bytes 1769480 | tf_op jit(solution)/shard_map/ppermute | solution.py:705
  687.2 47.1 %collective-permute-start.10 = (bf16[288,1024]{1,0:T(8,128)(2,1)S(1)}, bf16[288,1024]{1,0:T(8,128)(2,1)S(1)}, u32[]{:S(2)}, u32[]{:S(2)}) collective-permute-start(bf16[288,1024]{1,0:T(8,128)(2,1)S(1)} %get-tuple-element.372.refs_1_), channel_id=1, source_target_pairs={{0,8},{1,9},{2,10},{3,11},{4,12},{5,13},{6,14},{7,15},{8,0},{9,1},... | collective-permute-start | bytes 1769480 | tf_op jit(solution)/shard_map/ppermute | solution.py:705
  687.2 47.1 %collective-permute-start.9 = (bf16[288,1024]{1,0:T(8,128)(2,1)S(1)}, bf16[288,1024]{1,0:T(8,128)(2,1)S(1)}, u32[]{:S(2)}, u32[]{:S(2)}) collective-permute-start(bf16[288,1024]{1,0:T(8,128)(2,1)S(1)} %get-tuple-element.371.refs_0_), channel_id=1, source_target_pairs={{0,4},{1,5},{2,6},{3,7},{4,0},{5,1},{6,2},{7,3},{8,12},{9,13},{10,... | collective-permute-start | bytes 1769480 | tf_op jit(solution)/shard_map/ppermute | solution.py:705
  748.7 10.0 copy-start.17
  758.6 6.6 copy-start.6
  758.6 6.6 copy-start.16
  758.6 6.6 copy-start.50
  758.6 6.7 copy-start.52
  758.6 26.9 %collective-permute-start.12 = (bf16[16,192,1024]{2,1,0:T(8,128)(2,1)}, bf16[16,192,1024]{2,1,0:T(8,128)(2,1)}, u32[]{:S(2)}, u32[]{:S(2)}) collective-permute-start(bf16[16,192,1024]{2,1,0:T(8,128)(2,1)} %get-tuple-element.291), channel_id=1, source_target_pairs={{0,1},{1,0},{2,3},{3,2},{4,5},{5,4},{6,7},{7,6},{8,9},{9,8},{10,11... | collective-permute-start | bytes 18874376 | tf_op jit(solution)/shard_map/ppermute | solution.py:705
  765.3 7.5 copy-start.54
  765.3 7.5 copy-start.7
  780.0 101.0 %all-to-all-start.4 = ((bf16[32,80,512]{2,1,0:T(8,128)(2,1)}), bf16[32,80,512]{2,1,0:T(8,128)(2,1)S(1)}, u32[]{:S(2)}, u32[]{:S(2)}) async-start(bf16[32,80,512]{2,1,0:T(8,128)(2,1)} %pad_maximum_fusion.3), calls=%async_computation.4 | async-start | bytes 5242880 | tf_op jit(solution)/shard_map/all_to_all | solution.py:301
  785.6 16.1 %copy-start.14 = (f32[288,1024]{1,0:T(8,128)S(1)}, f32[288,1024]{1,0:T(8,128)}, u32[]{:S(2)}) copy-start(f32[288,1024]{1,0:T(8,128)} %fusion.71.refs_0_) | copy-start | bytes 3538948
  799.1 52.0 %copy-start.27 = (bf16[2,4,192,512]{3,2,1,0:T(8,128)(2,1)S(1)}, bf16[2,4,192,512]{3,2,1,0:T(8,128)(2,1)}, u32[]{:S(2)}) copy-start(bf16[2,4,192,512]{3,2,1,0:T(8,128)(2,1)} %get-tuple-element.294) | copy-start | bytes 4718596
  799.1 52.0 %collective-permute-start.15 = (bf16[2,4,192,512]{3,2,1,0:T(8,128)(2,1)}, bf16[2,4,192,512]{3,2,1,0:T(8,128)(2,1)S(1)}, u32[]{:S(2)}, u32[]{:S(2)}) collective-permute-start(bf16[2,4,192,512]{3,2,1,0:T(8,128)(2,1)} %get-tuple-element.295), channel_id=1, source_target_pairs={{0,2},{1,3},{2,0},{3,1},{4,6},{5,7},{6,4},{7,5},{8,10},{9,11},{10,... | collective-permute-start | bytes 4718600 | tf_op jit(solution)/shard_map/ppermute | solution.py:705
  803.3 50.5 %collective-permute-start.13 = (bf16[4,2,192,512]{3,2,0,1:T(8,128)(2,1)S(1)}, bf16[4,2,192,512]{3,2,0,1:T(8,128)(2,1)S(1)}, u32[]{:S(2)}, u32[]{:S(2)}) collective-permute-start(bf16[4,2,192,512]{3,2,0,1:T(8,128)(2,1)S(1)} %copy.112), channel_id=1, source_target_pairs={{0,16},{16,0},{1,17},{17,1},{2,18},{18,2},{3,19},{19,3},{4,20},{20... | collective-permute-start | bytes 4718600 | tf_op jit(solution)/shard_map/ppermute | solution.py:705
  804.8 48.9 %copy-start.26 = (bf16[4,2,192,512]{3,2,1,0:T(8,128)(2,1)S(1)}, bf16[4,2,192,512]{3,2,1,0:T(8,128)(2,1)}, u32[]{:S(2)}) copy-start(bf16[4,2,192,512]{3,2,1,0:T(8,128)(2,1)} %get-tuple-element.292) | copy-start | bytes 4718596
  851.7 19.4 %collective-permute-start.16 = (bf16[4,192,512]{2,1,0:T(8,128)(2,1)S(1)}, bf16[4,192,512]{2,1,0:T(8,128)(2,1)S(1)}, u32[]{:S(2)}, u32[]{:S(2)}) collective-permute-start(bf16[4,192,512]{2,1,0:T(8,128)(2,1)S(1)} %fusion.82), channel_id=1, source_target_pairs={{0,16},{16,0},{1,17},{17,1},{2,18},{18,2},{3,19},{19,3},{4,20},{20... | collective-permute-start | bytes 2359304 | tf_op jit(solution)/shard_map/ppermute | solution.py:705
  854.4 19.4 %collective-permute-start.14 = (bf16[4,192,512]{2,1,0:T(8,128)(2,1)S(1)}, bf16[4,192,512]{2,1,0:T(8,128)(2,1)S(1)}, u32[]{:S(2)}, u32[]{:S(2)}) collective-permute-start(bf16[4,192,512]{2,1,0:T(8,128)(2,1)S(1)} %fusion.81), channel_id=1, source_target_pairs={{0,2},{1,3},{2,0},{3,1},{4,6},{5,7},{6,4},{7,5},{8,10},{9,11},{10,... | collective-permute-start | bytes 2359304 | tf_op jit(solution)/shard_map/ppermute | solution.py:705
  871.3 9.7 copy-start.12
  871.3 9.7 copy-start.55
  871.3 9.7 copy-start.33
  871.3 9.7 copy-start.40
  871.3 9.7 copy-start.42
  871.4 9.7 copy-start.43
  874.1 7.0 copy-start.13
  875.3 32.7 %collective-permute-start.19 = (bf16[192,1024]{1,0:T(8,128)(2,1)}, bf16[192,1024]{1,0:T(8,128)(2,1)}, u32[]{:S(2)}, u32[]{:S(2)}) collective-permute-start(bf16[192,1024]{1,0:T(8,128)(2,1)} %get-tuple-element.374), channel_id=1, source_target_pairs={{0,12},{1,13},{2,14},{3,15},{4,8},{5,9},{6,10},{7,11},{8,4},{9,5},... | collective-permute-start | bytes 1179656 | tf_op jit(solution)/shard_map/ppermute | solution.py:705
  877.8 34.1 %collective-permute-start.18 = (bf16[192,1024]{1,0:T(8,128)(2,1)}, bf16[192,1024]{1,0:T(8,128)(2,1)}, u32[]{:S(2)}, u32[]{:S(2)}) collective-permute-start(bf16[192,1024]{1,0:T(8,128)(2,1)} %get-tuple-element.376), channel_id=1, source_target_pairs={{0,8},{1,9},{2,10},{3,11},{4,12},{5,13},{6,14},{7,15},{8,0},{9,1},... | collective-permute-start | bytes 1179656 | tf_op jit(solution)/shard_map/ppermute | solution.py:705
  878.8 33.1 %collective-permute-start.17 = (bf16[192,1024]{1,0:T(8,128)(2,1)}, bf16[192,1024]{1,0:T(8,128)(2,1)}, u32[]{:S(2)}, u32[]{:S(2)}) collective-permute-start(bf16[192,1024]{1,0:T(8,128)(2,1)} %get-tuple-element.375), channel_id=1, source_target_pairs={{0,4},{1,5},{2,6},{3,7},{4,0},{5,1},{6,2},{7,3},{8,12},{9,13},{10,... | collective-permute-start | bytes 1179656 | tf_op jit(solution)/shard_map/ppermute | solution.py:705
  908.0 33.5 %copy-start.60 = (f32[3328]{0:T(1024)S(1)}, f32[3328]{0:T(1024)}, u32[]{:S(2)}) copy-start(f32[3328]{0:T(1024)} %param.62) | copy-start | bytes 39940
  908.0 34.2 %copy-start.24 = (f32[32,4096]{1,0:T(8,128)S(1)}, f32[32,4096]{1,0:T(8,128)}, u32[]{:S(2)}) copy-start(f32[32,4096]{1,0:T(8,128)} %param.48) | copy-start | bytes 1572868
  913.6 33.3 %copy-start.18 = (f32[32,6144]{1,0:T(8,128)S(1)}, f32[32,6144]{1,0:T(8,128)}, u32[]{:S(2)}) copy-start(f32[32,6144]{1,0:T(8,128)} %param.54) | copy-start | bytes 2359300
  942.1 8.8 copy-start.48
  (29 other events, 95.0 us)
Sparse Core Ops, SparseCore 0:
  11.4 118.9 all-gather.4
  133.8 67.0 all-gather.6
  204.4 122.3 all-gather.8
  330.1 68.1 all-gather.10

commit v3 on v2

--- a/solution.py
+++ b/solution.py
@@ -863,6 +863,41 @@
 def plain_sum(left, right):
     grad = lax.dot_general(left, right, (((0,), (0,)), ((), ())), preferred_element_type=jnp.float32)
     return lax.psum_scatter(grad, ("seq", "fsdp"), scatter_dimension=0, tiled=True)
+
+
+def activation_back_kernel(grad_ref, down_ref, gate_ref, up_ref, gate_grad_ref, up_grad_ref):
+    grad = lax.dot_general(
+        grad_ref[...], down_ref[...], (((1,), (1,)), ((), ())), preferred_element_type=jnp.float32
+    )
+    gate = gate_ref[...]
+    share = 0.5 + 0.5 * jnp.tanh(0.5 * gate)
+    silu = gate * share
+    up_grad_ref[...] = (grad * silu).astype(jnp.bfloat16)
+    gate_grad_ref[...] = (grad * up_ref[...] * (share + silu - silu * share)).astype(jnp.bfloat16)
+
+
+def activation_back(grad, down, gate_up):
+    tokens, width = gate_up.shape
+    rows, wide = min(512, tokens), 512
+    tiles = width // (2 * wide)
+    out = jax.ShapeDtypeStruct((tokens, width // 2), jnp.bfloat16)
+    block = pl.BlockSpec((rows, wide), lambda i, j: (i, j))
+    return pl.pallas_call(
+        activation_back_kernel,
+        grid=(tokens // rows, tiles),
+        in_specs=[
+            pl.BlockSpec((rows, D), lambda i, j: (i, 0)),
+            pl.BlockSpec((wide, D), lambda i, j: (j, 0)),
+            block,
+            pl.BlockSpec((rows, wide), lambda i, j: (i, tiles + j)),
+        ],
+        out_specs=[block, block],
+        out_shape=[out, out],
+        compiler_params=pltpu.CompilerParams(vmem_limit_bytes=VMEM_BYTES),
+        cost_estimate=pl.CostEstimate(
+            flops=tokens * width * D, bytes_accessed=6 * tokens * width, transcendentals=tokens * width // 2
+        ),
+    )(grad, down, gate_up, gate_up)
 
 
 def adam_update(weight, moment_one, moment_two, grad, factor, step_float):
@@ -991,14 +1026,15 @@
         early = gradient_blocks(activated, mlp_low, 768, lambda j: 0, 288, ())
     else:
         down_shard = plain_sum(activated, mlp_low)
-    act_grad = jnp.dot(mlp_low, down_full.T, preferred_element_type=jnp.float32)
-    act_back = jax.vjp(lambda joined: jax.nn.silu(joined[:, :FF]) * joined[:, FF:], gate_up)[1]
-    gate_up_low = act_back(act_grad)[0].astype(jnp.bfloat16)
+    gate_low, up_low = activation_back(mlp_low, down_full, gate_up)
     if staged:
-        early = gradient_blocks(normed_two, gate_up_low, 512, lambda j: 3 + j, 288, tuple(early))
+        early = gradient_blocks(normed_two, gate_low, 512, lambda j: 3 + j, 288, tuple(early))
+        early = gradient_blocks(normed_two, up_low, 512, lambda j: 6 + j, 288, tuple(early))
     else:
-        gate_up_shard = plain_sum(normed_two, gate_up_low)
-    normed_two_grad = jnp.dot(gate_up_low, gate_up_full.T, preferred_element_type=jnp.float32)
+        gate_up_shard = jnp.concatenate([plain_sum(normed_two, gate_low), plain_sum(normed_two, up_low)], axis=1)
+    normed_two_grad = jnp.dot(
+        gate_low, gate_up_full[:, :FF].T, preferred_element_type=jnp.float32
+    ) + jnp.dot(up_low, gate_up_full[:, FF:].T, preferred_element_type=jnp.float32)
     mid_back = jax.vjp(rms_norm, resid_mid, mlp_gain)[1]
     mid_extra, dmlp_gain = mid_back(normed_two_grad)
     dresid_mid = dresid_out + mid_extra

time: 1020 us -> 1000 us (0.980)
  Pallas kernels: 374 us -> 401 us
  matrix products: 135 us -> 111 us
  other arithmetic: 156 us -> 142 us
    dot_general x2, matrix products: 47.6 us -> 23.3 us  [the longest x1 12.1 us: body(): jnp.dot(up_low, gate_up_full[:, FF:].T, preferred_element_type=jnp.float32)]
    pallas_call x0 -> x1, Pallas kernels: none -> 23.6 us  [activation_back(): pl.pallas_call(activation_back_kernel, grid=(tokens // rows, tiles), in_s...]
    convert_element_type x1 -> x0, other arithmetic: 13.2 us -> none  [body(): gate_up_low = act_back(act_grad)[0].astype(jnp.bfloat16)]
    pallas_call x5 -> x6, Pallas kernels: 62.6 us -> 65.6 us  [gradient_blocks(): pl.pallas_call(functools.partial(gradient_kernel, height), grid_spec=pltp...]
  transfers between devices with their start and end apart: 25 -> 25, of which waited for: 10 -> 10; matrix products, arithmetic and copies ran while one was open for 19% -> 19% of each run, Pallas kernels for 27% -> 28%
where the time goes in v3:
time: 1000 us; the launch traced here: 994 us
  Pallas kernels  401 us (40%)
  waiting for transfers between devices  207 us (21%)
  other arithmetic  142 us (14%)
  matrix products  111 us (11%)
  starting transfers between devices  57.2 us (6%)
  local copies, waits for them, and re-layouts  39.8 us (4%)
  between operations  24.2 us (2%)
  loops' own time  11.7 us (1%)
    pallas_call x4, Pallas kernels, exchange(): pl.pallas_call(functools.partial(exchange_kernel, n_seq, n_fsdp, to_all),...  116 us
    ppermute x2, waiting for transfers between devices, tokens_before(): return lax.ppermute(own, 'seq', [(0, 1), (1, 0)])  88.7 us
    ppermute x16, waiting for transfers between devices, trade(): return lax.ppermute(values, axis, [(i, i ^ bit) for i in range(count)])  88 us
    pallas_call x2, Pallas kernels, attention_backward(): pl.pallas_call(functools.partial(backward_kernel, keys), grid_spec=pltpu....  66.1 us
    pallas_call x6, Pallas kernels, gradient_blocks(): pl.pallas_call(functools.partial(gradient_kernel, height), grid_spec=pltp...  65.6 us
    sub x6, other arithmetic, adam_update(): weight - LEARN_RATE * (moment_one / fix_one / (jnp.sqrt(moment_two / fix_...  56.6 us
    ppermute x2, starting transfers between devices, to_tokens_before(): return lax.ppermute(parts, 'seq', [(0, 1), (1, 0)])  34.9 us
    pallas_call x2, Pallas kernels, attention_forward(): pl.pallas_call(functools.partial(forward_kernel, keys), grid_spec=pltpu.P...  30.5 us
  transfers between devices with their start and end apart: 25, of which 10 were waited for; matrix products, arithmetic and copies ran while one was open for 19% of the time, Pallas kernels for 28%

profile of v3, /device:TPU:0, one launch (start us, length us, event | category | flops | bytes accessed | tf_op | source)
XLA Modules:
  0.0 994.3 jit_solution(7522144176077640580)
XLA Ops:
  15.4 2.3 convert_reduce_fusion.2
  24.7 12.9 %shard_map.416 = s32[32,8,128]{2,1,0:T(8,128)} custom-call(s32[32,8,128]{2,1,0:T(8,128)} %pad_add_fusion.2.x_ref), custom_call_target="tpu_custom_call" | custom-call | tf_op jit(solution)/shard_map/pallas_call | solution.py:98
  40.7 14.5 %gather_fusion.1 = bf16[2560,512]{1,0:T(8,128)(2,1)S(1)} fusion(f32[9496,512]{1,0:T(8,128)} %param.45, s32[3072]{0:T(1024)S(1)} %pad_clamp_fusion.1), kind=kCustom, calls=%fused_computation.1 | custom fusion | bytes 5253120 | tf_op jit(solution)/shard_map/jit(_take)/gather | solution.py:147
  55.2 2.4 broadcast_select_fusion.1
  57.6 76.1 %shard_map.417 = bf16[32,80,512]{2,1,0:T(8,128)(2,1)S(1)} custom-call(bf16[32,80,512]{2,1,0:T(8,128)(2,1)} %bitcast.158), custom_call_target="tpu_custom_call" | custom-call | tf_op jit(solution)/shard_map/pallas_call | solution.py:98
  133.8 12.0 %conditional.2 = (bf16[1024,1024]{0,1:T(8,128)(2,1)}) conditional(s32[]{:T(128)} %convert_element_type.232, (s32[1024]{0:T(1024)S(1)}, bf16[32,80,512]{2,1,0:T(8,128)(2,1)S(1)}, s32[]{:T(128)}, s32[1024]{0:T(1024)S(1)}, s32[1024]{0:T(1024)S(1)}, /*index=5*/s32[1024]{0:T(1024)S(1)}, f32[9496,512]{1,0:T(8,128)}) %tuple.141, (s32[1024]{0:T(1024)S(1)}, ...), branch_computations={%region_10.14_spmd, %region_14.15_spmd} | conditional | flops 5396661248 | bytes 153264544 | solution.py:214
  145.8 2.9 copy.103
  159.8 9.4 convolution_convert_fusion.1.raw_ref
  169.2 7.5 shard_map.419
  181.8 9.3 convolution_convert_fusion.2.raw_ref
  191.1 11.8 %shard_map.418.q_ref = bf16[1024,2048]{1,0:T(8,128)(2,1)} custom-call(bf16[1024,2048]{1,0:T(8,128)(2,1)} %convolution_convert_fusion.2.raw_ref, f32[1024,128]{1,0:T(8,128)} %get-tuple-element.409.cos_ref, f32[1024,128]{1,0:T(8,128)} %get-tuple-element.410.sin_ref, f32[2,128]{1,0:T(2,128)} %slice_bitcast_fusion.gain_ref), custom_call_target="tpu_custom_call" | custom-call | flops 4000000000 | bytes 8388608 | tf_op jit(solution)/shard_map/pallas_call | solution.py:385
  202.9 32.6 %collective-permute-done.1.kb_ref.vb_ref = bf16[1024,1024]{1,0:T(8,128)(2,1)} collective-permute-done((bf16[1024,1024]{1,0:T(8,128)(2,1)}, bf16[1024,1024]{1,0:T(8,128)(2,1)}, u32[]{:S(2)}, u32[]{:S(2)}) %collective-permute-start.1) | collective-permute-done | bytes 2097184 | tf_op jit(solution)/shard_map/ppermute | solution.py:690
  235.5 15.2 %shard_map.420 = (bf16[1024,2048]{1,0:T(8,128)(2,1)}, f32[8,1024,2]{2,1,0:T(8,128)}) custom-call(s32[6]{0:T(128)} %pad_add_fusion.6.scalar_ref, bf16[1024,2048]{1,0:T(8,128)(2,1)} %shard_map.418.q_ref, bf16[1024,1024]{1,0:T(8,128)(2,1)} %collective-permute-done.1.kb_ref.vb_ref, bf16[1024,1024]{1,0:T(8,128)(2,1)} %collective-permute-done.1.kb_ref.vb_ref, ...), custom_call_target="tpu_custom_call" | custom-call | flops 20000000000 | bytes 16777216 | tf_op jit(solution)/shard_map/pallas_call | solution.py:585
  250.7 56.1 %collective-permute-done.kb_ref.vb_ref = bf16[1024,1024]{1,0:T(8,128)(2,1)S(1)} collective-permute-done((bf16[1024,1024]{1,0:T(8,128)(2,1)}, bf16[1024,1024]{1,0:T(8,128)(2,1)S(1)}, u32[]{:S(2)}, u32[]{:S(2)}) %collective-permute-start) | collective-permute-done | bytes 2097184 | tf_op jit(solution)/shard_map/ppermute | solution.py:690
  308.1 15.3 %shard_map.421 = (bf16[1024,2048]{1,0:T(8,128)(2,1)}, f32[8,1024,2]{2,1,0:T(8,128)}) custom-call(s32[6]{0:T(128)} %pad_add_fusion.6.scalar_ref, bf16[1024,2048]{1,0:T(8,128)(2,1)} %shard_map.418.q_ref, bf16[1024,1024]{1,0:T(8,128)(2,1)} %copy-done.67, bf16[1024,1024]{1,0:T(8,128)(2,1)} %copy-done.67, ...), custom_call_target="tpu_custom_call", output_to_operand_aliasing={{0}: (7, {}), {1}: (8, {})} | custom-call | flops 20000000000 | bytes 16777216 | tf_op jit(solution)/shard_map/pallas_call | solution.py:585
  323.4 7.9 multiply_reduce_fusion.6
  331.4 2.0 copy-done.9
  333.8 21.5 %fusion.132.gate_ref.up_ref = f32[1024,6144]{1,0:T(8,128)} fusion(bf16[1024,1024]{1,0:T(8,128)(2,1)S(1)} %multiply_convert_fusion.left_ref, bf16[1024,6144]{1,0:T(8,128)(2,1)} %all-gather.9.cloned.1.call-done), kind=kOutput, calls=%fused_computation.310 | convolution fusion | flops 12884901888 | bytes 39845888 | tf_op jit(solution)/shard_map/dot_general | solution.py:994
  355.3 12.8 %fusion.30.left_ref = bf16[1024,3072]{1,0:T(8,128)(2,1)} fusion(f32[1024,6144]{1,0:T(8,128)} %fusion.132.gate_ref.up_ref), kind=kLoop, calls=%fused_computation.64 | loop fusion | flops 18874368 | bytes 31457280 | tf_op jit(solution)/shard_map/convert_element_type | solution.py:995
  368.1 30.3 %all-gather.11.cloned.1.call-done.down_ref = bf16[3072,1024]{1,0:T(8,128)(2,1)} async-done(((bf16[96,1024]{1,0:T(8,128)(2,1)}), bf16[3072,1024]{1,0:T(8,128)(2,1)}) %all-gather.11.cloned.1.call-update) | async-done | bytes 6291472 | tf_op jit(solution)/shard_map/all_gather | solution.py:700
  398.4 11.5 %multiply_reduce_fusion.5 = (f32[1024]{0:T(1024)S(1)}, f32[1024,1024]{1,0:T(8,128)S(1)}) fusion(f32[1024,1024]{1,0:T(8,128)} %copy-done.9, bf16[1024,3072]{1,0:T(8,128)(2,1)} %fusion.30.left_ref, bf16[3072,1024]{1,0:T(8,128)(2,1)} %all-gather.11.cloned.1.call-done.down_ref), kind=kOutput, calls=%fused_computation.119 | convolution fusion | flops 6445595648 | bytes 20975616 | tf_op jit(solution)/shard_map/dot_general | solution.py:996
  409.9 2.0 copy-done.2
  413.7 9.6 shard_map.422
  425.3 4.3 multiply_reduce_fusion.1
  429.7 2.2 fusion.60.grad_ref.right_ref
  431.8 10.9 %shard_map.424 = (bf16[16,288,1024]{2,1,0:T(8,128)(2,1)}, bf16[16,288,1024]{2,1,0:T(8,128)(2,1)}) custom-call(s32[1]{0:T(128)} %bitcast.31.core_ref, bf16[1024,3072]{1,0:T(8,128)(2,1)} %fusion.30.left_ref, bf16[1024,1024]{1,0:T(8,128)(2,1)} %fusion.60.grad_ref.right_ref), custom_call_target="tpu_custom_call" | custom-call | flops 6442450944 | bytes 16777216 | tf_op jit(solution)/shard_map/pallas_call | solution.py:746
  442.8 23.6 %shard_map.423 = (bf16[1024,3072]{1,0:T(8,128)(2,1)}, bf16[1024,3072]{1,0:T(8,128)(2,1)}) custom-call(bf16[1024,1024]{1,0:T(8,128)(2,1)} %fusion.60.grad_ref.right_ref, bf16[3072,1024]{1,0:T(8,128)(2,1)} %all-gather.11.cloned.1.call-done.down_ref, f32[1024,6144]{1,0:T(8,128)} %fusion.132.gate_ref.up_ref, f32[1024,6144]{1,0:T(8,128)} %fusion.132.gate_ref.up_ref), custom_call_target="tpu_custom_call" | custom-call | flops 6442450944 | bytes 37748736 | tf_op jit(solution)/shard_map/pallas_call | solution.py:885
  466.4 13.1 %shard_map.425 = (bf16[16,288,1024]{2,1,0:T(8,128)(2,1)}, bf16[16,288,1024]{2,1,0:T(8,128)(2,1)}) custom-call(s32[1]{0:T(128)} %bitcast.31.core_ref, bf16[1024,1024]{1,0:T(8,128)(2,1)} %copy-done.7, bf16[1024,3072]{1,0:T(8,128)(2,1)} %get-tuple-element.271.right_ref, ...), custom_call_target="tpu_custom_call", output_to_operand_aliasing={{0}: (3, {}), {1}: (4, {})} | custom-call | flops 6442450944 | bytes 16777216 | tf_op jit(solution)/shard_map/pallas_call | solution.py:746
  479.5 13.3 %shard_map.426 = (bf16[16,288,1024]{2,1,0:T(8,128)(2,1)}, bf16[16,288,1024]{2,1,0:T(8,128)(2,1)}) custom-call(s32[1]{0:T(128)} %bitcast.31.core_ref, bf16[1024,1024]{1,0:T(8,128)(2,1)} %copy-done.7, bf16[1024,3072]{1,0:T(8,128)(2,1)} %get-tuple-element.272.right_ref, ...), custom_call_target="tpu_custom_call", output_to_operand_aliasing={{0}: (3, {}), {1}: (4, {})} | custom-call | flops 6442450944 | bytes 16777216 | tf_op jit(solution)/shard_map/pallas_call | solution.py:746
  493.5 12.1 %fusion.31 = f32[1024,1024]{1,0:T(8,128)} fusion(bf16[1024,3072]{1,0:T(8,128)(2,1)} %get-tuple-element.272.right_ref, bf16[1024,6144]{1,0:T(8,128)(2,1)} %all-gather.9.cloned.1.call-done), kind=kOutput, calls=%fused_computation.78 | convolution fusion | flops 6442450944 | bytes 16777216 | tf_op jit(solution)/shard_map/dot_general | solution.py:1037
  505.6 11.2 %multiply_reduce_fusion.2 = (f32[1024]{0:T(1024)}, f32[1024]{0:T(1024)S(1)}, f32[1024,1024]{1,0:T(8,128)S(1)}) fusion(f32[1024,1024]{1,0:T(8,128)S(1)} %copy-done.10, f32[1024]{0:T(1024)S(1)} %fusion.114, f32[1024]{0:T(1024)S(1)} %get-tuple-element.391, f32[1024,1024]{1,0:T(8,128)} %fusion.31, bf16[1024,3072]{1,0:T(8,128)(2,1)S(1)} %bitcast.160, ...), kind=kOutput, calls=%fused_computation.116 | convolution fusion | flops 6449788928 | bytes 25182208 | tf_op jit(solution)/shard_map/dot_general | solution.py:1035
  516.9 3.7 fusion.124
  520.6 6.5 convolution_convert_fusion.do_ref
  527.1 16.1 %shard_map.427 = (bf16[4,2,288,512]{3,2,1,0:T(8,128)(2,1)}, bf16[4,2,288,512]{3,2,1,0:T(8,128)(2,1)}, bf16[2,4,288,512]{3,2,1,0:T(8,128)(2,1)}, bf16[2,4,288,512]{3,2,1,0:T(8,128)(2,1)}) custom-call(s32[2]{0:T(128)} %pad_add_fusion.7.at_ref, bf16[16,288,1024]{2,1,0:T(8,128)(2,1)} %get-tuple-element.278.keep_ref, ...), custom_call_target="tpu_custom_call" | custom-call | flops 1000000000 | bytes 28311552 | tf_op jit(solution)/shard_map/pallas_call | solution.py:815
  546.6 33.1 %shard_map.428 = (f32[1024,2048]{1,0:T(8,128)}, bf16[2,1024,512]{2,1,0:T(8,128)(2,1)}, f32[2,1024,512]{2,1,0:T(8,128)}) custom-call(s32[6]{0:T(128)} %pad_add_fusion.6.scalar_ref, bf16[1024,2048]{1,0:T(8,128)(2,1)} %shard_map.418.q_ref, bf16[1024,1024]{1,0:T(8,128)(2,1)} %collective-permute-done.1.kb_ref.vb_ref, ...), custom_call_target="tpu_custom_call" | custom-call | flops 40000000000 | bytes 41943040 | tf_op jit(solution)/shard_map/pallas_call | solution.py:658
  579.7 17.5 %collective-permute-start.7 = (bf16[2,1024,512]{2,1,0:T(8,128)(2,1)}, bf16[2,1024,512]{2,1,0:T(8,128)(2,1)}, u32[]{:S(2)}, u32[]{:S(2)}) collective-permute-start(bf16[2,1024,512]{2,1,0:T(8,128)(2,1)} %get-tuple-element.289), channel_id=1, source_target_pairs={{0,16},{16,0},{1,17},{17,1},{2,18},{18,2},{3,19},{19,3},{4,20},{20... | collective-permute-start | bytes 6291464 | tf_op jit(solution)/shard_map/ppermute | solution.py:696
  600.5 3.3 convert_add_fusion.2
  604.7 2.4 convert_add_fusion.1
  607.1 2.1 copy-done.11
  610.5 33.0 %shard_map.429 = (f32[1024,2048]{1,0:T(8,128)}, bf16[2,1024,512]{2,1,0:T(8,128)(2,1)}, f32[2,1024,512]{2,1,0:T(8,128)}) custom-call(s32[6]{0:T(128)} %pad_add_fusion.6.scalar_ref, bf16[1024,2048]{1,0:T(8,128)(2,1)} %shard_map.418.q_ref, bf16[1024,1024]{1,0:T(8,128)(2,1)} %copy-done.67, ...), custom_call_target="tpu_custom_call", output_to_operand_aliasing={{0}: (10, {})} | custom-call | flops 40000000000 | bytes 41943040 | tf_op jit(solution)/shard_map/pallas_call | solution.py:658
  643.4 17.3 %collective-permute-start.8 = (bf16[2,1024,512]{2,1,0:T(8,128)(2,1)}, bf16[2,1024,512]{2,1,0:T(8,128)(2,1)}, u32[]{:S(2)}, u32[]{:S(2)}) collective-permute-start(bf16[2,1024,512]{2,1,0:T(8,128)(2,1)} %get-tuple-element.290), channel_id=1, source_target_pairs={{0,16},{16,0},{1,17},{17,1},{2,18},{18,2},{3,19},{19,3},{4,20},{20... | collective-permute-start | bytes 6291464 | tf_op jit(solution)/shard_map/ppermute | solution.py:696
  660.8 8.7 shard_map.432
  674.1 2.8 collective-permute-start.11
  678.5 17.4 %shard_map.430 = (bf16[1024,2048]{1,0:T(8,128)(2,1)}, f32[8,128]{1,0:T(8,128)}) custom-call(bf16[1024,2048]{1,0:T(8,128)(2,1)} %convolution_convert_fusion.2.raw_ref, f32[1024,128]{1,0:T(8,128)} %get-tuple-element.409.cos_ref, f32[1024,128]{1,0:T(8,128)} %get-tuple-element.410.sin_ref, f32[2,128]{1,0:T(2,128)} %slice_bitcast_fusion.gain_ref, ...), custom_call_target="tpu_custom_call" | custom-call | flops 5000000000 | bytes 20971520 | tf_op jit(solution)/shard_map/pallas_call | solution.py:464
  696.0 9.8 shard_map.433
  705.7 18.2 %collective-permute-done.10 = bf16[288,1024]{1,0:T(8,128)(2,1)S(1)} collective-permute-done((bf16[288,1024]{1,0:T(8,128)(2,1)S(1)}, bf16[288,1024]{1,0:T(8,128)(2,1)S(1)}, u32[]{:S(2)}, u32[]{:S(2)}) %collective-permute-start.10) | collective-permute-done | bytes 589856 | tf_op jit(solution)/shard_map/ppermute | solution.py:705
  725.3 13.0 %shard_map.431 = (bf16[1024,2048]{1,0:T(8,128)(2,1)}, f32[8,128]{1,0:T(8,128)}) custom-call(bf16[1024,2048]{1,0:T(8,128)(2,1)} %convolution_convert_fusion.1.raw_ref, f32[1024,128]{1,0:T(8,128)} %get-tuple-element.409.cos_ref, f32[1024,128]{1,0:T(8,128)} %get-tuple-element.410.sin_ref, f32[2,128]{1,0:T(2,128)} %slice_bitcast_fusion.gain_ref, ...), custom_call_target="tpu_custom_call" | custom-call | flops 5000000000 | bytes 20971520 | tf_op jit(solution)/shard_map/pallas_call | solution.py:464
  738.4 9.9 shard_map.434
  748.4 6.5 fusion.52
  755.0 7.4 fusion.49
  769.7 2.8 all-to-all-start.4
  772.5 13.5 %shard_map.435 = (bf16[4,2,192,512]{3,2,1,0:T(8,128)(2,1)}, bf16[4,2,192,512]{3,2,1,0:T(8,128)(2,1)}, bf16[2,4,192,512]{3,2,1,0:T(8,128)(2,1)}, bf16[2,4,192,512]{3,2,1,0:T(8,128)(2,1)}) custom-call(s32[2]{0:T(128)} %pad_add_fusion.7.at_ref, bf16[16,192,1024]{2,1,0:T(8,128)(2,1)} %get-tuple-element.298.keep_ref, ...), custom_call_target="tpu_custom_call" | custom-call | flops 1000000000 | bytes 18874368 | tf_op jit(solution)/shard_map/pallas_call | solution.py:815
  791.7 46.3 %collective-permute-done.15 = bf16[2,4,192,512]{3,2,1,0:T(8,128)(2,1)S(1)} collective-permute-done((bf16[2,4,192,512]{3,2,1,0:T(8,128)(2,1)}, bf16[2,4,192,512]{3,2,1,0:T(8,128)(2,1)S(1)}, u32[]{:S(2)}, u32[]{:S(2)}) %collective-permute-start.15) | collective-permute-done | bytes 1572896 | tf_op jit(solution)/shard_map/ppermute | solution.py:705
  842.8 15.0 %collective-permute-done.16 = bf16[4,192,512]{2,1,0:T(8,128)(2,1)S(1)} collective-permute-done((bf16[4,192,512]{2,1,0:T(8,128)(2,1)S(1)}, bf16[4,192,512]{2,1,0:T(8,128)(2,1)S(1)}, u32[]{:S(2)}, u32[]{:S(2)}) %collective-permute-start.16) | collective-permute-done | bytes 786464 | tf_op jit(solution)/shard_map/ppermute | solution.py:705
  858.1 2.4 collective-permute-done.14
  862.0 2.6 collective-permute-start.19
  867.9 27.1 %conditional.3 = (f32[9496,512]{1,0:T(8,128)}, f32[]{:T(128)}) conditional(s32[]{:T(128)} %convert_element_type.232, (s32[32,80]{1,0:T(8,128)S(1)}, bf16[32,80,512]{2,1,0:T(8,128)(2,1)S(1)}, bf16[192,1024]{1,0:T(8,128)(2,1)}, bf16[192,1024]{1,0:T(8,128)(2,1)}, bf16[192,1024]{1,0:T(8,128)(2,1)}, /*index=5*/s32[]{:T(128)}, s32[1024]{0:T(1024)S(1)}, ...), branch_computations={%region_33.40_spmd, %region_40.43_spmd} | conditional | flops 3705905920 | bytes 151820720 | solution.py:328
  874.2 19.5 %branch_1_fun.1 = (f32[9496,512]{1,0:T(8,128)}, f32[8,512]{1,0:T(8,128)}) custom-call(s32[2560]{0:T(1024)} %reshape.546.wanted_ref, s32[32]{0:T(128)} %convert_reduce_fusion.count_ref, bf16[32,80,512]{2,1,0:T(8,128)(2,1)S(1)} %get-tuple-element.197.arrived_ref, bf16[192,1024]{1,0:T(8,128)(2,1)} %get-tuple-element.198.refs_0_, ...), custom_call_target="tpu_custom_call" | custom-call | flops 1000000000 | bytes 83886080 | tf_op jit(solution)/shard_map/cond/branch_1_fun/pallas_call | solution.py:280
  895.0 3.8 collective-permute-done.18
  905.8 17.8 %shard_map.436 = f32[32,40,128]{2,1,0:T(8,128)} custom-call(f32[40,128]{1,0:T(8,128)} %pad_bitcast_fusion.x_ref), custom_call_target="tpu_custom_call" | custom-call | tf_op jit(solution)/shard_map/pallas_call | solution.py:98
  929.1 2.6 multiply_subtract_fusion.4
  931.7 2.2 multiply_subtract_fusion.6
  935.8 2.2 multiply_subtract_fusion.5
  939.2 47.2 %multiply_subtract_fusion.2 = (f32[9496,512]{1,0:T(8,128)}, f32[9496,512]{1,0:T(8,128)}, f32[9496,512]{1,0:T(8,128)}) fusion(f32[9496,512]{1,0:T(8,128)} %param.45, f32[]{:T(128)} %bitcast.57, f32[]{:T(128)} %bitcast.56, f32[9496,512]{1,0:T(8,128)} %get-tuple-element.305, f32[]{:T(128)S(6)} %div.179, f32[9496,512]{1,0:T(8,128)} %param.47, f32[9496,512]{1,0:T(8,128)} %param.46), kind=kLoop, calls=%fused_computation.61 | loop fusion | flops 77791232 | bytes 136134672 | tf_op jit(solution)/shard_map/sub | solution.py:909
  (299 shorter events, 95.3 us)
Async XLA Ops:
  7.2 152.6 %all-gather.5.cloned.1.call-start = ((), (), s32[]{:S(2)}) async-start(), calls=%async_computation.5 | async-start | bytes 8650752 | tf_op jit(solution)/shard_map/all_gather | solution.py:700
  9.0 314.4 %all-gather.7.cloned.1.call-start = ((), (), s32[]{:S(2)}) async-start(), calls=%async_computation.6 | async-start | bytes 4325376 | tf_op jit(solution)/shard_map/all_gather | solution.py:700
  10.7 323.1 %all-gather.9.cloned.1.call-start = ((), (), s32[]{:S(2)}) async-start(), calls=%async_computation.7 | async-start | bytes 12976128 | tf_op jit(solution)/shard_map/all_gather | solution.py:700
  12.7 385.7 %all-gather.11.cloned.1.call-start = ((), (), s32[]{:S(2)}) async-start(), calls=%async_computation.8 | async-start | bytes 6488064 | tf_op jit(solution)/shard_map/all_gather | solution.py:700
  15.4 118.4 %copy-start.40 = (s32[1024]{0:T(1024)}, s32[1024]{0:T(1024)S(1)}, u32[]{:S(2)}) copy-start(s32[1024]{0:T(1024)S(1)} %get-tuple-element.395) | copy-start | bytes 12292
  17.7 116.1 %copy-start.38 = (s32[1024]{0:T(1024)}, s32[1024]{0:T(1024)S(1)}, u32[]{:S(2)}) copy-start(s32[1024]{0:T(1024)S(1)} %convert_reduce_fusion.2) | copy-start | bytes 12292
  22.6 111.2 %copy-start.59 = (s32[1024]{0:T(1024)}, s32[1024]{0:T(1024)S(1)}, u32[]{:S(2)}) copy-start(s32[1024]{0:T(1024)S(1)} %get-tuple-element.397) | copy-start | bytes 12292
  55.2 78.6 %copy-start.31 = (s32[1,1024]{1,0:T(1,128)S(1)}, s32[1,1024]{1,0:T(1,128)}, u32[]{:S(2)}) copy-start(s32[1,1024]{1,0:T(1,128)} %param.41) | copy-start | bytes 12292
  145.8 10.5 %copy-start.58 = (f32[3328]{0:T(1024)S(1)}, f32[3328]{0:T(1024)}, u32[]{:S(2)}) copy-start(f32[3328]{0:T(1024)} %param.60) | copy-start | bytes 39940
  148.7 174.8 %copy-start.5 = (bf16[1024,1024]{1,0:T(8,128)(2,1)}, bf16[1024,1024]{1,0:T(8,128)(2,1)S(1)}, u32[]{:S(2)}) copy-start(bf16[1024,1024]{1,0:T(8,128)(2,1)S(1)} %copy.103) | copy-start | bytes 6291460
  157.9 11.3 %copy-start.48 = (f32[1024]{0:T(1024)}, f32[1024]{0:T(1024)S(1)}, u32[]{:S(2)}) copy-start(f32[1024]{0:T(1024)S(1)} %fusion.113) | copy-start | bytes 12292
  157.9 11.3 %copy-start.50 = (f32[1024]{0:T(1024)}, f32[1024]{0:T(1024)S(1)}, u32[]{:S(2)}) copy-start(f32[1024]{0:T(1024)S(1)} %get-tuple-element.390) | copy-start | bytes 12292
  169.2 8.8 copy-start.27
  169.2 10.9 %copy-start.65 = (s32[48]{0:T(128)S(1)}, s32[48]{0:T(128)}, u32[]{:S(2)}) copy-start(s32[48]{0:T(128)} %param.43) | copy-start | bytes 580
  176.7 58.8 %collective-permute-start.1 = (bf16[1024,1024]{1,0:T(8,128)(2,1)}, bf16[1024,1024]{1,0:T(8,128)(2,1)}, u32[]{:S(2)}, u32[]{:S(2)}) collective-permute-start(bf16[1024,1024]{1,0:T(8,128)(2,1)} %get-tuple-element.267.k_ref.v_ref), channel_id=1, source_target_pairs={{0,16},{16,0},{1,17},{17,1},{2,18},{18,2},{3,19},{19,3},{4,20},{20... | collective-permute-start | bytes 6291464 | tf_op jit(solution)/shard_map/ppermute | solution.py:690
  180.9 125.9 %collective-permute-start = (bf16[1024,1024]{1,0:T(8,128)(2,1)}, bf16[1024,1024]{1,0:T(8,128)(2,1)S(1)}, u32[]{:S(2)}, u32[]{:S(2)}) collective-permute-start(bf16[1024,1024]{1,0:T(8,128)(2,1)} %get-tuple-element.266.k_ref.v_ref), channel_id=1, source_target_pairs={{0,16},{16,0},{1,17},{17,1},{2,18},{18,2},{3,19},{19,3},{4,20},{20... | collective-permute-start | bytes 6291464 | tf_op jit(solution)/shard_map/ppermute | solution.py:690
  333.8 21.5 %copy-start.7 = (bf16[1024,1024]{1,0:T(8,128)(2,1)}, bf16[1024,1024]{1,0:T(8,128)(2,1)S(1)}, u32[]{:S(2)}) copy-start(bf16[1024,1024]{1,0:T(8,128)(2,1)S(1)} %multiply_convert_fusion.left_ref) | copy-start | bytes 6291460
  368.1 43.8 %copy-start.45 = (f32[1024]{0:T(1024)S(1)}, f32[1024]{0:T(1024)}, u32[]{:S(2)}) copy-start(f32[1024]{0:T(1024)} %param.63) | copy-start | bytes 12292
  479.5 26.1 %slice-start.5 = ((s8[6291456]{0:T(1024)(128)(4,1)}), s8[2097152]{0:T(1024)(128)(4,1)S(1)}, s32[]{:S(2)}) async-start(s8[6291456]{0:T(1024)(128)(4,1)} %bitcast.159), calls=%async_computation.14 | async-start | bytes 4194304
  492.8 34.3 %collective-permute-start.2 = (bf16[16,288,1024]{2,1,0:T(8,128)(2,1)}, bf16[16,288,1024]{2,1,0:T(8,128)(2,1)}, u32[]{:S(2)}, u32[]{:S(2)}) collective-permute-start(bf16[16,288,1024]{2,1,0:T(8,128)(2,1)} %get-tuple-element.279), channel_id=1, source_target_pairs={{0,1},{1,0},{2,3},{3,2},{4,5},{5,4},{6,7},{7,6},{8,9},{9,8},{10,11... | collective-permute-start | bytes 28311560 | tf_op jit(solution)/shard_map/ppermute | solution.py:705
  493.5 12.2 %copy-start.10 = (f32[1024,1024]{1,0:T(8,128)S(1)}, f32[1024,1024]{1,0:T(8,128)}, u32[]{:S(2)}) copy-start(f32[1024,1024]{1,0:T(8,128)} %copy-done.9) | copy-start | bytes 12582916
  493.5 12.2 %slice-start.6 = ((s8[6291456]{0:T(1024)(128)(4,1)}), s8[4194304]{0:T(1024)(128)(4,1)S(1)}, s32[]{:S(2)}) async-start(s8[6291456]{0:T(1024)(128)(4,1)} %bitcast.159), calls=%async_computation.15 | async-start | bytes 8388608
  505.6 11.2 %copy-start.4 = (f32[1024,1024]{1,0:T(8,128)S(1)}, f32[1024,1024]{1,0:T(8,128)}, u32[]{:S(2)}) copy-start(f32[1024,1024]{1,0:T(8,128)} %copy-done.2) | copy-start | bytes 12582916
  520.6 6.5 copy-start.16
  544.9 54.2 %collective-permute-start.3 = (bf16[4,2,288,512]{3,2,0,1:T(8,128)(2,1)S(1)}, bf16[4,2,288,512]{3,2,0,1:T(8,128)(2,1)S(1)}, u32[]{:S(2)}, u32[]{:S(2)}) collective-permute-start(bf16[4,2,288,512]{3,2,0,1:T(8,128)(2,1)S(1)} %copy.111), channel_id=1, source_target_pairs={{0,16},{16,0},{1,17},{17,1},{2,18},{18,2},{3,19},{19,3},{4,20},{20... | collective-permute-start | bytes 7077896 | tf_op jit(solution)/shard_map/ppermute | solution.py:705
  545.2 59.5 %collective-permute-start.4 = (bf16[2,4,288,512]{3,2,1,0:T(8,128)(2,1)}, bf16[2,4,288,512]{3,2,1,0:T(8,128)(2,1)}, u32[]{:S(2)}, u32[]{:S(2)}) collective-permute-start(bf16[2,4,288,512]{3,2,1,0:T(8,128)(2,1)} %get-tuple-element.281.refs_1_), channel_id=1, source_target_pairs={{0,2},{1,3},{2,0},{3,1},{4,6},{5,7},{6,4},{7,5},{8,10},{9,11},{10,... | collective-permute-start | bytes 7077896 | tf_op jit(solution)/shard_map/ppermute | solution.py:705
  579.7 145.6 %collective-permute-start.7 = (bf16[2,1024,512]{2,1,0:T(8,128)(2,1)}, bf16[2,1024,512]{2,1,0:T(8,128)(2,1)}, u32[]{:S(2)}, u32[]{:S(2)}) collective-permute-start(bf16[2,1024,512]{2,1,0:T(8,128)(2,1)} %get-tuple-element.289), channel_id=1, source_target_pairs={{0,16},{16,0},{1,17},{17,1},{2,18},{18,2},{3,19},{19,3},{4,20},{20... | collective-permute-start | bytes 6291464 | tf_op jit(solution)/shard_map/ppermute | solution.py:696
  603.9 65.5 %collective-permute-start.5 = (bf16[4,288,512]{2,1,0:T(8,128)(2,1)S(1)}, bf16[4,288,512]{2,1,0:T(8,128)(2,1)}, u32[]{:S(2)}, u32[]{:S(2)}) collective-permute-start(bf16[4,288,512]{2,1,0:T(8,128)(2,1)S(1)} %fusion.69.refs_1_), channel_id=1, source_target_pairs={{0,2},{1,3},{2,0},{3,1},{4,6},{5,7},{6,4},{7,5},{8,10},{9,11},{10,... | collective-permute-start | bytes 3538952 | tf_op jit(solution)/shard_map/ppermute | solution.py:705
  609.4 61.9 %collective-permute-start.6 = (bf16[4,288,512]{2,1,0:T(8,128)(2,1)S(1)}, bf16[4,288,512]{2,1,0:T(8,128)(2,1)}, u32[]{:S(2)}, u32[]{:S(2)}) collective-permute-start(bf16[4,288,512]{2,1,0:T(8,128)(2,1)S(1)} %fusion.70.refs_2_), channel_id=1, source_target_pairs={{0,16},{16,0},{1,17},{17,1},{2,18},{18,2},{3,19},{19,3},{4,20},{20... | collective-permute-start | bytes 3538952 | tf_op jit(solution)/shard_map/ppermute | solution.py:705
  643.4 81.9 %collective-permute-start.8 = (bf16[2,1024,512]{2,1,0:T(8,128)(2,1)}, bf16[2,1024,512]{2,1,0:T(8,128)(2,1)}, u32[]{:S(2)}, u32[]{:S(2)}) collective-permute-start(bf16[2,1024,512]{2,1,0:T(8,128)(2,1)} %get-tuple-element.290), channel_id=1, source_target_pairs={{0,16},{16,0},{1,17},{17,1},{2,18},{18,2},{3,19},{19,3},{4,20},{20... | collective-permute-start | bytes 6291464 | tf_op jit(solution)/shard_map/ppermute | solution.py:696
  674.1 31.6 %collective-permute-start.11 = (bf16[288,1024]{1,0:T(8,128)(2,1)S(1)}, bf16[288,1024]{1,0:T(8,128)(2,1)S(1)}, u32[]{:S(2)}, u32[]{:S(2)}) collective-permute-start(bf16[288,1024]{1,0:T(8,128)(2,1)S(1)} %get-tuple-element.379.refs_2_), channel_id=1, source_target_pairs={{0,12},{1,13},{2,14},{3,15},{4,8},{5,9},{6,10},{7,11},{8,4},{9,5},... | collective-permute-start | bytes 1769480 | tf_op jit(solution)/shard_map/ppermute | solution.py:705
  676.9 47.1 %collective-permute-start.10 = (bf16[288,1024]{1,0:T(8,128)(2,1)S(1)}, bf16[288,1024]{1,0:T(8,128)(2,1)S(1)}, u32[]{:S(2)}, u32[]{:S(2)}) collective-permute-start(bf16[288,1024]{1,0:T(8,128)(2,1)S(1)} %get-tuple-element.378.refs_1_), channel_id=1, source_target_pairs={{0,8},{1,9},{2,10},{3,11},{4,12},{5,13},{6,14},{7,15},{8,0},{9,1},... | collective-permute-start | bytes 1769480 | tf_op jit(solution)/shard_map/ppermute | solution.py:705
  676.9 47.1 %collective-permute-start.9 = (bf16[288,1024]{1,0:T(8,128)(2,1)S(1)}, bf16[288,1024]{1,0:T(8,128)(2,1)S(1)}, u32[]{:S(2)}, u32[]{:S(2)}) collective-permute-start(bf16[288,1024]{1,0:T(8,128)(2,1)S(1)} %get-tuple-element.377.refs_0_), channel_id=1, source_target_pairs={{0,4},{1,5},{2,6},{3,7},{4,0},{5,1},{6,2},{7,3},{8,12},{9,13},{10,... | collective-permute-start | bytes 1769480 | tf_op jit(solution)/shard_map/ppermute | solution.py:705
  738.4 10.0 %copy-start.18 = (bf16[1024,2048]{1,0:T(8,128)(2,1)S(1)}, bf16[1024,2048]{1,0:T(8,128)(2,1)}, u32[]{:S(2)}) copy-start(bf16[1024,2048]{1,0:T(8,128)(2,1)} %get-tuple-element.291.right_ref) | copy-start | bytes 12582916
  748.3 6.6 copy-start.6
  748.3 6.6 copy-start.17
  748.3 6.6 copy-start.49
  748.3 6.6 copy-start.51
  748.3 24.2 %collective-permute-start.12 = (bf16[16,192,1024]{2,1,0:T(8,128)(2,1)}, bf16[16,192,1024]{2,1,0:T(8,128)(2,1)}, u32[]{:S(2)}, u32[]{:S(2)}) collective-permute-start(bf16[16,192,1024]{2,1,0:T(8,128)(2,1)} %get-tuple-element.299), channel_id=1, source_target_pairs={{0,1},{1,0},{2,3},{3,2},{4,5},{5,4},{6,7},{7,6},{8,9},{9,8},{10,11... | collective-permute-start | bytes 18874376 | tf_op jit(solution)/shard_map/ppermute | solution.py:705
  754.9 7.5 copy-start.53
  755.0 7.5 copy-start.8
  769.7 98.1 %all-to-all-start.4 = ((bf16[32,80,512]{2,1,0:T(8,128)(2,1)}), bf16[32,80,512]{2,1,0:T(8,128)(2,1)S(1)}, u32[]{:S(2)}, u32[]{:S(2)}) async-start(bf16[32,80,512]{2,1,0:T(8,128)(2,1)} %pad_maximum_fusion.3), calls=%async_computation.4 | async-start | bytes 5242880 | tf_op jit(solution)/shard_map/all_to_all | solution.py:301
  772.5 15.9 %copy-start.15 = (f32[288,1024]{1,0:T(8,128)S(1)}, f32[288,1024]{1,0:T(8,128)}, u32[]{:S(2)}) copy-start(f32[288,1024]{1,0:T(8,128)} %fusion.75.refs_0_) | copy-start | bytes 3538948
  786.0 52.0 %copy-start.26 = (bf16[2,4,192,512]{3,2,1,0:T(8,128)(2,1)S(1)}, bf16[2,4,192,512]{3,2,1,0:T(8,128)(2,1)}, u32[]{:S(2)}) copy-start(bf16[2,4,192,512]{3,2,1,0:T(8,128)(2,1)} %get-tuple-element.302) | copy-start | bytes 4718596
  786.0 51.9 %collective-permute-start.15 = (bf16[2,4,192,512]{3,2,1,0:T(8,128)(2,1)}, bf16[2,4,192,512]{3,2,1,0:T(8,128)(2,1)S(1)}, u32[]{:S(2)}, u32[]{:S(2)}) collective-permute-start(bf16[2,4,192,512]{3,2,1,0:T(8,128)(2,1)} %get-tuple-element.303), channel_id=1, source_target_pairs={{0,2},{1,3},{2,0},{3,1},{4,6},{5,7},{6,4},{7,5},{8,10},{9,11},{10,... | collective-permute-start | bytes 4718600 | tf_op jit(solution)/shard_map/ppermute | solution.py:705
  790.0 50.5 %collective-permute-start.13 = (bf16[4,2,192,512]{3,2,0,1:T(8,128)(2,1)S(1)}, bf16[4,2,192,512]{3,2,0,1:T(8,128)(2,1)S(1)}, u32[]{:S(2)}, u32[]{:S(2)}) collective-permute-start(bf16[4,2,192,512]{3,2,0,1:T(8,128)(2,1)S(1)} %copy.114), channel_id=1, source_target_pairs={{0,16},{16,0},{1,17},{17,1},{2,18},{18,2},{3,19},{19,3},{4,20},{20... | collective-permute-start | bytes 4718600 | tf_op jit(solution)/shard_map/ppermute | solution.py:705
  791.7 48.9 %copy-start.25 = (bf16[4,2,192,512]{3,2,1,0:T(8,128)(2,1)S(1)}, bf16[4,2,192,512]{3,2,1,0:T(8,128)(2,1)}, u32[]{:S(2)}) copy-start(bf16[4,2,192,512]{3,2,1,0:T(8,128)(2,1)} %get-tuple-element.300) | copy-start | bytes 4718596
  838.5 19.3 %collective-permute-start.16 = (bf16[4,192,512]{2,1,0:T(8,128)(2,1)S(1)}, bf16[4,192,512]{2,1,0:T(8,128)(2,1)S(1)}, u32[]{:S(2)}, u32[]{:S(2)}) collective-permute-start(bf16[4,192,512]{2,1,0:T(8,128)(2,1)S(1)} %fusion.86), channel_id=1, source_target_pairs={{0,16},{16,0},{1,17},{17,1},{2,18},{18,2},{3,19},{19,3},{4,20},{20... | collective-permute-start | bytes 2359304 | tf_op jit(solution)/shard_map/ppermute | solution.py:705
  841.2 19.4 %collective-permute-start.14 = (bf16[4,192,512]{2,1,0:T(8,128)(2,1)S(1)}, bf16[4,192,512]{2,1,0:T(8,128)(2,1)S(1)}, u32[]{:S(2)}, u32[]{:S(2)}) collective-permute-start(bf16[4,192,512]{2,1,0:T(8,128)(2,1)S(1)} %fusion.85), channel_id=1, source_target_pairs={{0,2},{1,3},{2,0},{3,1},{4,6},{5,7},{6,4},{7,5},{8,10},{9,11},{10,... | collective-permute-start | bytes 2359304 | tf_op jit(solution)/shard_map/ppermute | solution.py:705
  858.1 9.7 copy-start.13
  858.1 9.7 copy-start.54
  858.1 9.7 copy-start.32
  858.1 9.7 copy-start.39
  858.1 9.7 copy-start.41
  858.1 9.7 copy-start.42
  860.8 7.0 copy-start.14
  862.0 33.0 %collective-permute-start.19 = (bf16[192,1024]{1,0:T(8,128)(2,1)}, bf16[192,1024]{1,0:T(8,128)(2,1)}, u32[]{:S(2)}, u32[]{:S(2)}) collective-permute-start(bf16[192,1024]{1,0:T(8,128)(2,1)} %get-tuple-element.380), channel_id=1, source_target_pairs={{0,12},{1,13},{2,14},{3,15},{4,8},{5,9},{6,10},{7,11},{8,4},{9,5},... | collective-permute-start | bytes 1179656 | tf_op jit(solution)/shard_map/ppermute | solution.py:705
  864.6 34.2 %collective-permute-start.18 = (bf16[192,1024]{1,0:T(8,128)(2,1)}, bf16[192,1024]{1,0:T(8,128)(2,1)}, u32[]{:S(2)}, u32[]{:S(2)}) collective-permute-start(bf16[192,1024]{1,0:T(8,128)(2,1)} %get-tuple-element.382), channel_id=1, source_target_pairs={{0,8},{1,9},{2,10},{3,11},{4,12},{5,13},{6,14},{7,15},{8,0},{9,1},... | collective-permute-start | bytes 1179656 | tf_op jit(solution)/shard_map/ppermute | solution.py:705
  865.7 33.1 %collective-permute-start.17 = (bf16[192,1024]{1,0:T(8,128)(2,1)}, bf16[192,1024]{1,0:T(8,128)(2,1)}, u32[]{:S(2)}, u32[]{:S(2)}) collective-permute-start(bf16[192,1024]{1,0:T(8,128)(2,1)} %get-tuple-element.381), channel_id=1, source_target_pairs={{0,4},{1,5},{2,6},{3,7},{4,0},{5,1},{6,2},{7,3},{8,12},{9,13},{10,... | collective-permute-start | bytes 1179656 | tf_op jit(solution)/shard_map/ppermute | solution.py:705
  895.0 33.5 %copy-start.57 = (f32[3328]{0:T(1024)S(1)}, f32[3328]{0:T(1024)}, u32[]{:S(2)}) copy-start(f32[3328]{0:T(1024)} %param.62) | copy-start | bytes 39940
  895.0 34.2 %copy-start.24 = (f32[32,4096]{1,0:T(8,128)S(1)}, f32[32,4096]{1,0:T(8,128)}, u32[]{:S(2)}) copy-start(f32[32,4096]{1,0:T(8,128)} %param.48) | copy-start | bytes 1572868
  900.5 33.4 %copy-start.19 = (f32[32,6144]{1,0:T(8,128)S(1)}, f32[32,6144]{1,0:T(8,128)}, u32[]{:S(2)}) copy-start(f32[32,6144]{1,0:T(8,128)} %param.54) | copy-start | bytes 2359300
  928.5 5.4 copy-start.33
  929.1 8.8 copy-start.47
  (28 other events, 89.7 us)
Sparse Core Ops, SparseCore 0:
  11.4 118.7 all-gather.4
  133.6 67.3 all-gather.6
  204.4 122.3 all-gather.8
  330.1 68.2 all-gather.10
